TPU v7x, 512 devices: a whole 4x8x8 slice. The times are simulated.
512 devices in a mesh: lon: 128 (over z, y, core), lat: 4 (over x).
Axes of the slice: x: 4, y: 8, z: 8, core: 2. Of those that a mesh axis runs over, the one named last changes fastest.
Arguments:
- initial: float32 [2, 8, 4096, 1024], P(None, None, 'lon', 'lat'), may hold values from -6 to 6
- depth_levels: int32 [4096, 1024], P('lon', 'lat'), may hold values from 0 to 8, as said below
- mixing: float32 [4096, 1024], P('lon', 'lat'), may hold values from 0.02 to 0.2
- controls: float32 [4, 2, 256, 64], replicated, may hold values from -6 to 6
- drift_move: int32 [2, 2097152], P(None, ('lon', 'lat')), may hold values from 0 to 8, as said below
- drift_cell: int32 [2, 2097152], P(None, ('lon', 'lat')), may hold values from 0 to 8191
- drift_weight: float32 [4, 2, 2097152], P(None, None, ('lon', 'lat')), may hold values from 0 to 1, as said below
- drift_obs: float32 [2, 2, 2097152], P(None, None, ('lon', 'lat')), may hold values from -6 to 6
- drift_precision: float32 [2, 2097152], P(None, ('lon', 'lat')), may hold values from 0.1 to 8, as said below
Outputs:
- grad_initial: float32 [2, 8, 4096, 1024], P(None, None, 'lon', 'lat')
- grad_controls: float32 [4, 2, 256, 64], replicated
Inputs may be any that keep to these rules, and one draw needn't show every extreme that they name: `depth_levels`: the first and last latitude rows of the grid are land (0). `drift_move`: code d means that at that step the drifter lies in the block of the device at lon offset d // 3 - 1 (periodic) and lat offset d % 3 - 1 from its home block, column n having home block n // 4096 in lon-major order; no code leaves the latitude range. For each step and home block at most 128 drifters carry any one code other than 4; in every draw some block receives exactly 128 from each of its neighbours. `drift_cell`: index cx * 256 + cy of the cell within the owning block. `drift_weight`: bilinear weights of the corners (cell, next in longitude, next in latitude, both); non-negative, summing to one. `drift_precision`: Positive.
All inputs are finite; a program needn't handle non-finite values.
Results may differ from a plain program's by a relative error of at most 0.0003.
Values sent between devices are 32-bit elements; how exact they have to be, the bound alone decides.
No kernel may reach another device: no remote copies, remote signals or barrier semaphores. Data moves between devices by JAX's collectives and lax.ppermute only.
A program may use at most 128 MiB of HBM per device.

v0:
```python
import math

import jax
import jax.numpy as jnp
from jax import lax
from jax.sharding import PartitionSpec as P

CAPACITY = 128


VISCOUS = 0.1
FRICTION = 0.02
ROTATION = 0.3
HIGHEST_PRECISION = lax.Precision.HIGHEST


def padded_2(cells, sides, width):
    for axis, dim in sides:
        count = lax.axis_size(axis)
        head = lax.slice_in_dim(cells, 0, width, axis=dim)
        tail = lax.slice_in_dim(cells, cells.shape[dim] - width, cells.shape[dim], axis=dim)
        cells = jnp.concatenate(
            [
                lax.ppermute(tail, axis, [(i, (i + 1) % count) for i in range(count)]),
                cells,
                lax.ppermute(head, axis, [((i + 1) % count, i) for i in range(count)]),
            ],
            axis=dim,
        )
    return cells


def from_behind(value, axis, steps):
    count = lax.axis_size(axis)
    initial, last = (max(0, -steps), min(count, count - steps))
    return lax.ppermute(value, axis, [(source, source + steps) for source in range(initial, last)])


def from_behind_2(block, axis, distance):
    devices = range(lax.axis_size(axis))
    route = [((i - distance) % len(devices), i) for i in devices]
    return lax.ppermute(block, axis, route)


def coarse_weights(points, span_count, refine, offset, periodic):
    shifted = points - refine // 2
    low_point = shifted // refine
    fraction = ((shifted - low_point * refine).astype(jnp.float32) + 0.5) / refine
    high_point = low_point + 1 - offset
    low_point = low_point - offset
    if periodic:
        low_point = low_point % span_count
        high_point = high_point % span_count
    return (1.0 - fraction)[:, None] * jax.nn.one_hot(
        low_point, span_count, dtype=jnp.float32
    ) + fraction[:, None] * jax.nn.one_hot(high_point, span_count, dtype=jnp.float32)


def period_weights(steps_total, periods):
    time_table = []
    for step_index in range(steps_total):
        position = (step_index + 0.5) * (periods - 1) / steps_total
        time_table.append([max(0.0, 1.0 - abs(position - period)) for period in range(periods)])
    return time_table


def stencil(padded):
    center = padded[..., 1:-1, 1:-1]
    return (
        padded[..., 2:, 1:-1]
        + padded[..., :-2, 1:-1]
        + padded[..., 1:-1, 2:]
        + padded[..., 1:-1, :-2]
        - 4.0 * center
    )


def vertical(values):
    above_level = jnp.concatenate([values[:, :1], values[:, :-1]], axis=1)
    below_level = jnp.concatenate([values[:, 1:], values[:, -1:]], axis=1)
    return above_level + below_level - 2.0 * values


def shards(
    initial,
    depth_levels,
    mixing,
    controls,
    drift_move,
    drift_cell,
    drift_weight,
    drift_obs,
    drift_precision,
):
    levels = initial.shape[1]
    cells_lon = initial.shape[2]
    cells_lat = initial.shape[3]
    periods = controls.shape[0]
    ctrl_lon = controls.shape[2]
    ctrl_lat = controls.shape[3]
    steps_total = drift_move.shape[0]
    drift_local = drift_move.shape[1]
    capacity = CAPACITY
    lon_count = lax.axis_size("lon")
    lat_count = lax.axis_size("lat")
    lon_index = lax.axis_index("lon")
    lat_index = lax.axis_index("lat")
    refine = cells_lon * lon_count // ctrl_lon
    grid_lat = cells_lat * lat_count
    wet_mask = (jnp.arange(levels, dtype=jnp.int32)[:, None, None] < depth_levels[None]).astype(
        jnp.float32
    )
    col_ids = lon_index * cells_lon + jnp.arange(cells_lon, dtype=jnp.int32)
    row_ids = lat_index * cells_lat + jnp.arange(cells_lat, dtype=jnp.int32)
    rotation = ROTATION * jnp.sin(
        (row_ids.astype(jnp.float32) + 0.5) * (math.pi / grid_lat) - 0.5 * math.pi
    )
    lon_interp = coarse_weights(col_ids, ctrl_lon, refine, 0, True)
    lat_interp = coarse_weights(row_ids, ctrl_lat, refine, 0, False)
    time_table = period_weights(steps_total, periods)
    weight_local = jnp.sum(drift_precision)
    normalizer = float(steps_total * drift_local * lon_count * lat_count)
    source_scale = normalizer / lax.psum(weight_local, ("lon", "lat"))
    ocean_state = wet_mask * initial
    surfaces = []
    for step_index in range(steps_total):
        padded = padded_2(ocean_state, (("lon", 2), ("lat", 3)), 1)
        if step_index > 0:
            surfaces.append(padded[:, 0, 1:, 1:])
        turning = jnp.stack([rotation * ocean_state[1], -rotation * ocean_state[0]])
        tendency = (
            ocean_state
            + mixing * stencil(padded)
            + VISCOUS * vertical(ocean_state)
            - FRICTION * ocean_state
            + turning
        )
        blended = time_table[step_index][0] * controls[0]
        for forcing_period in range(1, periods):
            blended = blended + time_table[step_index][forcing_period] * controls[forcing_period]
        forcing_across = jnp.einsum("xa,cab->cxb", lon_interp, blended, precision=HIGHEST_PRECISION)
        tendency = tendency.at[:, 0].add(
            jnp.einsum("cxb,yb->cxy", forcing_across, lat_interp, precision=HIGHEST_PRECISION)
        )
        ocean_state = wet_mask * tendency
    last_surface = ocean_state[:, 0]
    upper_row = from_behind(last_surface[:, :, 0], "lat", -1)
    extended = jnp.concatenate([last_surface, upper_row[:, :, None]], axis=2)
    upper_col = from_behind_2(extended[:, 0], "lon", -1)
    surfaces.append(jnp.concatenate([extended, upper_col[:, None]], axis=1))
    fields = jnp.concatenate(
        [drift_weight, drift_obs, drift_precision[None], drift_cell[None].astype(jnp.float32)],
        axis=0,
    )
    fields = jnp.transpose(fields, (1, 0, 2))
    code_list = jnp.array([0, 1, 2, 3, 5, 6, 7, 8], jnp.int32)
    matches = (drift_move[:, :, None] == code_list[None, None, :]).astype(jnp.int32)
    positions = jnp.cumsum(matches, axis=1) - 1
    targets = jnp.sum(
        matches * (positions + capacity * jnp.arange(8, dtype=jnp.int32)[None, None, :]), axis=2
    )
    staying_mask = drift_move == 4
    targets = jnp.where(staying_mask, 8 * capacity, targets)
    outgoing = []
    for step_index in range(steps_total):
        buffer = (
            jnp.zeros((8, 8 * capacity + 1), jnp.float32)
            .at[:, targets[step_index]]
            .set(fields[step_index])
        )
        outgoing.append(buffer[:, : 8 * capacity].reshape(8, 8, capacity))
    outgoing = jnp.stack(outgoing)
    arrived = []
    for bucket, direction in enumerate((0, 1, 2, 3, 5, 6, 7, 8)):
        packet = outgoing[:, :, bucket]
        if direction // 3 != 1:
            packet = from_behind_2(packet, "lon", direction // 3 - 1)
        if direction % 3 != 1:
            packet = from_behind(packet, "lat", direction % 3 - 1)
        arrived.append(packet)
    received = jnp.concatenate(arrived, axis=2)
    own_records = fields.at[:, 6].multiply(staying_mask.astype(jnp.float32))
    all_records = jnp.concatenate([own_records, received], axis=2)
    row_width = cells_lat + 1
    local_sources = []
    for step_index in range(steps_total):
        records = all_records[step_index]
        cell_ids = records[7].astype(jnp.int32)
        anchor = cell_ids // cells_lat * row_width + cell_ids % cells_lat
        corners = (anchor, anchor + row_width, anchor + 1, anchor + row_width + 1)
        flattened = surfaces[step_index].reshape(2, -1)
        modeled = records[0] * jnp.take(flattened, corners[0], axis=1)
        for corner in range(1, 4):
            modeled = modeled + records[corner] * jnp.take(flattened, corners[corner], axis=1)
        mismatch = modeled - records[4:6]
        scaled_miss = records[6] * mismatch * source_scale
        source = jnp.zeros_like(flattened)
        for corner in range(4):
            source = source.at[:, corners[corner]].add(records[corner] * scaled_miss)
        source = source.reshape(2, cells_lon + 1, row_width)
        edge_column = from_behind_2(source[:, cells_lon], "lon", 1)
        source = source.at[:, 0].add(edge_column)
        top_row = from_behind(source[:, :cells_lon, cells_lat], "lat", 1)
        source = source.at[:, :cells_lon, 0].add(top_row)
        local_sources.append(source[:, :cells_lon, :cells_lat])
    adjoint = jnp.zeros_like(initial)
    forcing_grads = [None] * steps_total
    for step_index in reversed(range(steps_total)):
        adjoint = adjoint.at[:, 0].add(local_sources[step_index])
        nudged = wet_mask * adjoint
        forcing_grads[step_index] = nudged[:, 0]
        spread = padded_2(mixing * nudged, (("lon", 2), ("lat", 3)), 1)
        turning = jnp.stack([-rotation * nudged[1], rotation * nudged[0]])
        adjoint = (
            nudged + stencil(spread) + VISCOUS * vertical(nudged) - FRICTION * nudged + turning
        )
    grad_initial = wet_mask * adjoint
    projected = []
    for step_index in range(steps_total):
        across = jnp.einsum(
            "xa,cxy->cay", lon_interp, forcing_grads[step_index], precision=HIGHEST_PRECISION
        )
        projected.append(jnp.einsum("cay,yb->cab", across, lat_interp, precision=HIGHEST_PRECISION))
    period_grads = []
    for period in range(periods):
        combined = time_table[0][period] * projected[0]
        step_index = 1
        combined = combined + time_table[step_index][period] * projected[step_index]
        period_grads.append(combined)
    local_grad = jnp.stack(period_grads)
    grad_controls = lax.psum(local_grad, ("lon", "lat"))
    output_scale = 1.0
    return (grad_initial * output_scale, grad_controls * output_scale)


def solution(mesh):
    return jax.shard_map(
        shards,
        mesh=mesh,
        in_specs=(
            P(None, None, "lon", "lat"),
            P("lon", "lat"),
            P("lon", "lat"),
            P(),
            P(None, ("lon", "lat")),
            P(None, ("lon", "lat")),
            P(None, None, ("lon", "lat")),
            P(None, None, ("lon", "lat")),
            P(None, ("lon", "lat")),
        ),
        out_specs=(P(None, None, "lon", "lat"), P()),
        check_vma=False,
    )
```

profile of v0, /device:TPU:24, one launch (start us, length us, event | category | flops | bytes accessed | tf_op | source)
XLA Modules:
  0.0 995.8 jit_solution(9115113833760600871)
XLA Ops:
  12.4 4.6 reduce-window.6
  19.0 10.7 %scatter_custom_fusion.1 = f32[8,1025]{0,1:T(8,128)S(1)} fusion(s32[4096]{0:T(1024)S(1)} %bitcast.301, f32[4096,8]{1,0:T(8,128)S(1)} %copy.123, f32[]{:T(128)} %constant.358.clone.1), kind=kCustom, calls=%fused_computation.117 | custom fusion | bytes 32804 | tf_op jit(solution)/shard_map/scatter | solution.py:169
  30.6 10.7 %scatter_custom_fusion = f32[8,1025]{0,1:T(8,128)S(1)} fusion(s32[4096]{0:T(1024)S(1)} %bitcast.300, f32[4096,8]{1,0:T(8,128)S(1)} %copy.122, f32[]{:T(128)} %constant.358.clone.1), kind=kCustom, calls=%fused_computation.119 | custom fusion | bytes 32804 | tf_op jit(solution)/shard_map/scatter | solution.py:169
  49.2 4.5 collective-permute-start.6
  59.0 106.3 %psum.14 = f32[]{:T(128)} all-reduce(f32[]{:T(128)} %get-tuple-element.211), channel_id=1, replica_groups=mesh['lon'=128,'lat'=4] {'lon','lat'}, use_global_device_ids=true, to_apply=%region_6.8 | all-reduce | flops 1 | bytes 8 | tf_op jit(solution)/shard_map/psum | solution.py:123
  184.6 4.8 collective-permute-start.11
  194.8 4.2 collective-permute-start.15
  203.8 4.2 collective-permute-done.15
  218.9 4.4 collective-permute-start.18
  225.3 5.1 collective-permute-done.18
  230.5 5.3 collective-permute-done.19
  241.8 15.6 %gather_fusion.7 = f32[5120,2]{1,0:T(8,128)S(1)} fusion(f32[2,8481]{0,1:T(8,128)} %copy.144, s32[5120]{0:T(1024)S(1)} %get-tuple-element.221), kind=kCustom, calls=%fused_computation.7.clone | custom fusion | bytes 102400 | tf_op jit(solution)/shard_map/jit(_take)/gather | solution.py:194
  258.3 15.7 %gather_fusion.6 = f32[5120,2]{1,0:T(8,128)S(1)} fusion(f32[2,8481]{0,1:T(8,128)} %copy.144, s32[5120]{0:T(1024)S(1)} %get-tuple-element.220), kind=kCustom, calls=%fused_computation.6.clone | custom fusion | bytes 102400 | tf_op jit(solution)/shard_map/jit(_take)/gather | solution.py:194
  274.7 15.7 %gather_fusion.5 = f32[5120,2]{1,0:T(8,128)S(1)} fusion(f32[2,8481]{0,1:T(8,128)} %copy.144, s32[5120]{0:T(1024)S(1)} %get-tuple-element.219), kind=kCustom, calls=%fused_computation.5.clone | custom fusion | bytes 102400 | tf_op jit(solution)/shard_map/jit(_take)/gather | solution.py:194
  291.1 15.7 %gather_fusion.4 = f32[5120,2]{1,0:T(8,128)S(1)} fusion(f32[2,8481]{0,1:T(8,128)} %copy.144, s32[5120]{0:T(1024)S(1)} %get-tuple-element.218), kind=kCustom, calls=%fused_computation.4.clone | custom fusion | bytes 102400 | tf_op jit(solution)/shard_map/jit(_take)/gather | solution.py:192
  316.4 30.9 %scatter_custom_fusion.6 = f32[2,8481]{0,1:T(8,128)} fusion(s32[5120]{0:T(1024)} %bitcast.299, f32[5120,2]{1,0:T(8,128)} %copy.152, f32[]{:T(128)} %constant.358.clone.1), kind=kCustom, calls=%fused_computation.18 | custom fusion | flops 10240 | bytes 68360 | tf_op jit(solution)/shard_map/scatter-add | solution.py:199
  347.3 30.3 %scatter_fusion.3 = f32[2,8481]{0,1:T(8,128)} fusion(f32[2,8481]{0,1:T(8,128)} %scatter_custom_fusion.6, s32[5120]{0:T(1024)S(1)} %bitcast.288, f32[5120,2]{1,0:T(8,128)} %copy.153), kind=kCustom, calls=%fused_computation.15 | custom fusion | flops 10240 | bytes 143360 | tf_op jit(solution)/shard_map/scatter-add | solution.py:199
  377.6 30.5 %scatter_fusion.4 = f32[2,8481]{0,1:T(8,128)} fusion(f32[2,8481]{0,1:T(8,128)} %scatter_fusion.3, s32[5120]{0:T(1024)S(1)} %bitcast.287, f32[5120,2]{1,0:T(8,128)} %copy.154), kind=kCustom, calls=%fused_computation.16 | custom fusion | flops 10240 | bytes 143360 | tf_op jit(solution)/shard_map/scatter-add | solution.py:199
  408.1 30.0 %scatter_fusion.5 = f32[2,8481]{0,1:T(8,128)} fusion(f32[2,8481]{0,1:T(8,128)} %scatter_fusion.4, s32[5120]{0:T(1024)S(1)} %bitcast.290, f32[5120,2]{1,0:T(8,128)S(1)} %copy.155), kind=kCustom, calls=%fused_computation.17 | custom fusion | flops 10240 | bytes 143360 | tf_op jit(solution)/shard_map/scatter-add | solution.py:199
  452.8 15.7 %gather_fusion.3 = f32[5120,2]{1,0:T(8,128)S(1)} fusion(f32[2,8481]{0,1:T(8,128)} %copy.129, s32[5120]{0:T(1024)S(1)} %copy-done.6), kind=kCustom, calls=%fused_computation.3.clone | custom fusion | bytes 102400 | tf_op jit(solution)/shard_map/jit(_take)/gather | solution.py:194
  469.3 15.7 %gather_fusion.2 = f32[5120,2]{1,0:T(8,128)S(1)} fusion(f32[2,8481]{0,1:T(8,128)} %copy.129, s32[5120]{0:T(1024)S(1)} %copy-done.5), kind=kCustom, calls=%fused_computation.2.clone | custom fusion | bytes 102400 | tf_op jit(solution)/shard_map/jit(_take)/gather | solution.py:194
  485.7 15.7 %gather_fusion.1 = f32[5120,2]{1,0:T(8,128)S(1)} fusion(f32[2,8481]{0,1:T(8,128)} %copy.129, s32[5120]{0:T(1024)S(1)} %get-tuple-element.229), kind=kCustom, calls=%fused_computation.1.clone | custom fusion | bytes 102400 | tf_op jit(solution)/shard_map/jit(_take)/gather | solution.py:194
  502.2 15.7 %gather_fusion = f32[5120,2]{1,0:T(8,128)S(1)} fusion(f32[2,8481]{0,1:T(8,128)} %copy.129, s32[5120]{0:T(1024)S(1)} %get-tuple-element.228), kind=kCustom, calls=%fused_computation.clone | custom fusion | bytes 102400 | tf_op jit(solution)/shard_map/jit(_take)/gather | solution.py:192
  527.3 30.9 %scatter_custom_fusion.2 = f32[2,8481]{0,1:T(8,128)} fusion(s32[5120]{0:T(1024)} %bitcast.298, f32[5120,2]{1,0:T(8,128)} %copy.137, f32[]{:T(128)} %constant.358.clone.1), kind=kCustom, calls=%fused_computation.20 | custom fusion | flops 10240 | bytes 68360 | tf_op jit(solution)/shard_map/scatter-add | solution.py:199
  558.2 30.5 %scatter_fusion = f32[2,8481]{0,1:T(8,128)} fusion(f32[2,8481]{0,1:T(8,128)} %scatter_custom_fusion.2, s32[5120]{0:T(1024)S(1)} %bitcast.286, f32[5120,2]{1,0:T(8,128)} %copy.138), kind=kCustom, calls=%fused_computation.11 | custom fusion | flops 10240 | bytes 143360 | tf_op jit(solution)/shard_map/scatter-add | solution.py:199
  588.8 30.3 %scatter_fusion.1 = f32[2,8481]{0,1:T(8,128)} fusion(f32[2,8481]{0,1:T(8,128)} %scatter_fusion, s32[5120]{0:T(1024)S(1)} %bitcast.285, f32[5120,2]{1,0:T(8,128)} %copy.139), kind=kCustom, calls=%fused_computation.12 | custom fusion | flops 10240 | bytes 143360 | tf_op jit(solution)/shard_map/scatter-add | solution.py:199
  619.1 30.0 %scatter_fusion.2 = f32[2,8481]{0,1:T(8,128)} fusion(f32[2,8481]{0,1:T(8,128)} %scatter_fusion.1, s32[5120]{0:T(1024)S(1)} %bitcast.289, f32[5120,2]{1,0:T(8,128)S(1)} %copy.140), kind=kCustom, calls=%fused_computation.13 | custom fusion | flops 10240 | bytes 143360 | tf_op jit(solution)/shard_map/scatter-add | solution.py:199
  652.4 6.3 collective-permute-start.22
  680.0 4.8 collective-permute-start.26
  684.8 4.5 collective-permute-done.27
  708.4 4.2 collective-permute-done.33
  716.8 269.9 %all-reduce.3.cloned.1.call-done = f32[4,2,256,64]{2,3,1,0:T(8,128)} async-done(((f32[4,2,256,64]{2,3,1,0:T(8,128)}), f32[4,2,256,64]{2,3,1,0:T(8,128)}) %all-reduce.3.cloned.1.call-update) | async-done | bytes 524304 | tf_op jit(solution)/shard_map/psum | solution.py:231
  (284 shorter events, 155.8 us)
Async XLA Ops:
  7.2 979.4 %all-reduce.3.cloned.1.call-start = ((), (), s32[]{:S(2)}) async-start(), calls=%async_computation | async-start | bytes 1048576 | tf_op jit(solution)/shard_map/psum | solution.py:231
  41.6 16.0 %collective-permute-start = (f32[2,8,128]{2,1,0:T(8,128)S(1)}, f32[2,8,128]{2,1,0:T(8,128)S(1)}, u32[]{:S(2)}, u32[]{:S(2)}) collective-permute-start(f32[2,8,128]{2,1,0:T(8,128)S(1)} %bitcast.309), channel_id=1, source_target_pairs={{4,0},{8,4},{12,8},{16,12},{20,16},{24,20},{28,24},{32,28},{36,32}... | collective-permute-start | bytes 24584 | tf_op jit(solution)/shard_map/ppermute | solution.py:42
  43.5 124.5 %collective-permute-start.2 = (f32[2,8,128]{2,1,0:T(8,128)S(1)}, f32[2,8,128]{2,1,0:T(8,128)S(1)}, u32[]{:S(2)}, u32[]{:S(2)}) collective-permute-start(f32[2,8,128]{2,1,0:T(8,128)S(1)} %bitcast.308), channel_id=1, source_target_pairs={{4,0},{8,4},{12,8},{16,12},{20,16},{24,20},{28,24},{32,28},{36,32}... | collective-permute-start | bytes 24584 | tf_op jit(solution)/shard_map/ppermute | solution.py:42
  46.0 125.9 %collective-permute-start.3 = (f32[2,8,128]{2,1,0:T(8,128)S(1)}, f32[2,8,128]{2,1,0:T(8,128)S(1)}, u32[]{:S(2)}, u32[]{:S(2)}) collective-permute-start(f32[2,8,128]{2,1,0:T(8,128)S(1)} %bitcast.307), channel_id=1, source_target_pairs={{4,0},{8,4},{12,8},{16,12},{20,16},{24,20},{28,24},{32,28},{36,32}... | collective-permute-start | bytes 24584 | tf_op jit(solution)/shard_map/ppermute | solution.py:42
  47.9 129.8 %collective-permute-start.5 = (f32[2,8,128]{2,1,0:T(8,128)S(1)}, f32[2,8,128]{2,1,0:T(8,128)S(1)}, u32[]{:S(2)}, u32[]{:S(2)}) collective-permute-start(f32[2,8,128]{2,1,0:T(8,128)S(1)} %bitcast.306), channel_id=1, source_target_pairs={{1,0},{2,1},{3,2},{5,4},{6,5},{7,6},{9,8},{10,9},{11,10},{13,12},{... | collective-permute-start | bytes 24584 | tf_op jit(solution)/shard_map/ppermute | solution.py:36
  49.2 132.2 %collective-permute-start.6 = (f32[2,8,128]{2,1,0:T(8,128)S(1)}, f32[2,8,128]{2,1,0:T(8,128)S(1)}, u32[]{:S(2)}, u32[]{:S(2)}) collective-permute-start(f32[2,8,128]{2,1,0:T(8,128)S(1)} %bitcast.305), channel_id=1, source_target_pairs={{0,1},{1,2},{2,3},{4,5},{5,6},{6,7},{8,9},{9,10},{10,11},{12,13},{... | collective-permute-start | bytes 24584 | tf_op jit(solution)/shard_map/ppermute | solution.py:36
  57.6 108.2 %collective-permute-start.1 = (f32[2,8,128]{2,1,0:T(8,128)S(1)}, f32[2,8,128]{2,1,0:T(8,128)S(1)}, u32[]{:S(2)}, u32[]{:S(2)}) collective-permute-start(f32[2,8,128]{2,1,0:T(8,128)S(1)} %collective-permute-done), channel_id=1, source_target_pairs={{1,0},{2,1},{3,2},{5,4},{6,5},{7,6},{9,8},{10,9},{11,10},{13,12},{... | collective-permute-start | bytes 24584 | tf_op jit(solution)/shard_map/ppermute | solution.py:36
  165.8 17.5 %collective-permute-start.7 = (f32[2,8,128]{2,1,0:T(8,128)S(1)}, f32[2,8,128]{2,1,0:T(8,128)S(1)}, u32[]{:S(2)}, u32[]{:S(2)}) collective-permute-start(f32[2,8,128]{2,1,0:T(8,128)S(1)} %bitcast.304), channel_id=1, source_target_pairs={{508,0},{0,4},{4,8},{8,12},{12,16},{16,20},{20,24},{24,28},{28,32}... | collective-permute-start | bytes 24584 | tf_op jit(solution)/shard_map/ppermute | solution.py:42
  168.0 21.5 %collective-permute-start.9 = (f32[2,8,128]{2,1,0:T(8,128)S(1)}, f32[2,8,128]{2,1,0:T(8,128)S(1)}, u32[]{:S(2)}, u32[]{:S(2)}) collective-permute-start(f32[2,8,128]{2,1,0:T(8,128)S(1)} %bitcast.302), channel_id=1, source_target_pairs={{508,0},{0,4},{4,8},{8,12},{12,16},{16,20},{20,24},{24,28},{28,32}... | collective-permute-start | bytes 24584 | tf_op jit(solution)/shard_map/ppermute | solution.py:42
  175.8 8.9 collective-permute-start.10
  177.7 16.8 %collective-permute-start.12 = (f32[2,8,1,256]{3,2,0,1:T(1,128)S(1)}, f32[2,8,1,256]{3,2,0,1:T(1,128)S(1)}, u32[]{:S(2)}, u32[]{:S(2)}) collective-permute-start(f32[2,8,1,256]{3,2,0,1:T(1,128)S(1)} %get-tuple-element.174), channel_id=1, source_target_pairs={{4,0},{8,4},{12,8},{16,12},{20,16},{24,20},{28,24},{32,28},{36,32}... | collective-permute-start | bytes 49160 | tf_op jit(solution)/shard_map/ppermute | solution.py:26
  181.4 13.1 %collective-permute-start.13 = (f32[2,8,1,256]{3,2,0,1:T(1,128)S(1)}, f32[2,8,1,256]{3,2,0,1:T(1,128)S(1)}, u32[]{:S(2)}, u32[]{:S(2)}) collective-permute-start(f32[2,8,1,256]{3,2,0,1:T(1,128)S(1)} %get-tuple-element.173), channel_id=1, source_target_pairs={{0,4},{4,8},{8,12},{12,16},{16,20},{20,24},{24,28},{28,32},{32,36}... | collective-permute-start | bytes 49160 | tf_op jit(solution)/shard_map/ppermute | solution.py:24
  183.3 6.1 collective-permute-start.8
  184.6 6.2 collective-permute-start.11
  194.8 13.3 %collective-permute-start.15 = (f32[2,8,34,1]{3,2,0,1:T(8,128)S(1)}, f32[2,8,34,1]{3,2,0,1:T(8,128)S(1)}, u32[]{:S(2)}, u32[]{:S(2)}) collective-permute-start(f32[2,8,34,1]{3,2,0,1:T(8,128)S(1)} %get-tuple-element.142), channel_id=1, source_target_pairs={{0,1},{1,2},{2,3},{3,0},{4,5},{5,6},{6,7},{7,4},{8,9},{9,10},{10,1... | collective-permute-start | bytes 6536 | tf_op jit(solution)/shard_map/ppermute | solution.py:24
  199.0 11.6 %collective-permute-start.14 = (f32[2,8,34,1]{3,2,0,1:T(8,128)S(1)}, f32[2,8,34,1]{3,2,0,1:T(8,128)S(1)}, u32[]{:S(2)}, u32[]{:S(2)}) collective-permute-start(f32[2,8,34,1]{3,2,0,1:T(8,128)S(1)} %get-tuple-element.141), channel_id=1, source_target_pairs={{1,0},{2,1},{3,2},{0,3},{5,4},{6,5},{7,6},{4,7},{9,8},{10,9},{11,1... | collective-permute-start | bytes 6536 | tf_op jit(solution)/shard_map/ppermute | solution.py:26
  213.6 5.1 collective-permute-start.17
  218.9 11.5 %collective-permute-start.18 = (f32[2,8,34,1]{3,2,0,1:T(8,128)S(1)}, f32[2,8,34,1]{3,2,0,1:T(8,128)S(1)}, u32[]{:S(2)}, u32[]{:S(2)}) collective-permute-start(f32[2,8,34,1]{3,2,0,1:T(8,128)S(1)} %get-tuple-element.139), channel_id=1, source_target_pairs={{1,0},{2,1},{3,2},{0,3},{5,4},{6,5},{7,6},{4,7},{9,8},{10,9},{11,1... | collective-permute-start | bytes 6536 | tf_op jit(solution)/shard_map/ppermute | solution.py:26
  223.3 12.4 %collective-permute-start.19 = (f32[2,8,34,1]{3,2,0,1:T(8,128)S(1)}, f32[2,8,34,1]{3,2,0,1:T(8,128)S(1)}, u32[]{:S(2)}, u32[]{:S(2)}) collective-permute-start(f32[2,8,34,1]{3,2,0,1:T(8,128)S(1)} %get-tuple-element.140), channel_id=1, source_target_pairs={{0,1},{1,2},{2,3},{3,0},{4,5},{5,6},{6,7},{7,4},{8,9},{9,10},{10,1... | collective-permute-start | bytes 6536 | tf_op jit(solution)/shard_map/ppermute | solution.py:24
  237.3 206.7 %collective-permute-start.20 = (f32[2,32]{1,0:T(2,128)}, f32[2,32]{1,0:T(2,128)}, u32[]{:S(2)}, u32[]{:S(2)}) collective-permute-start(f32[2,32]{1,0:T(2,128)} %slice_reduce_fusion.3), channel_id=1, source_target_pairs={{1,0},{2,1},{3,2},{5,4},{6,5},{7,6},{9,8},{10,9},{11,10},{13,12},{... | collective-permute-start | bytes 776 | tf_op jit(solution)/shard_map/ppermute | solution.py:36
  441.3 6.3 collective-permute-start.28
  444.8 5.0 collective-permute-start.21
  652.4 9.1 collective-permute-start.22
  661.6 5.5 collective-permute-start.23
  668.6 4.8 collective-permute-start.24
  670.5 5.1 collective-permute-start.25
  675.8 13.5 %collective-permute-start.27 = (f32[2,8,34,1]{3,2,0,1:T(8,128)S(1)}, f32[2,8,34,1]{3,2,0,1:T(8,128)S(1)}, u32[]{:S(2)}, u32[]{:S(2)}) collective-permute-start(f32[2,8,34,1]{3,2,0,1:T(8,128)S(1)} %get-tuple-element.138), channel_id=1, source_target_pairs={{0,1},{1,2},{2,3},{3,0},{4,5},{5,6},{6,7},{7,4},{8,9},{9,10},{10,1... | collective-permute-start | bytes 6536 | tf_op jit(solution)/shard_map/ppermute | solution.py:24
  680.0 10.8 %collective-permute-start.26 = (f32[2,8,34,1]{3,2,0,1:T(8,128)S(1)}, f32[2,8,34,1]{3,2,0,1:T(8,128)S(1)}, u32[]{:S(2)}, u32[]{:S(2)}) collective-permute-start(f32[2,8,34,1]{3,2,0,1:T(8,128)S(1)} %get-tuple-element.137), channel_id=1, source_target_pairs={{1,0},{2,1},{3,2},{0,3},{5,4},{6,5},{7,6},{4,7},{9,8},{10,9},{11,1... | collective-permute-start | bytes 6536 | tf_op jit(solution)/shard_map/ppermute | solution.py:26
  692.5 4.9 collective-permute-start.30
  694.5 5.1 collective-permute-start.31
  700.4 12.2 %collective-permute-start.33 = (f32[2,8,34,1]{3,2,0,1:T(8,128)S(1)}, f32[2,8,34,1]{3,2,0,1:T(8,128)}, u32[]{:S(2)}, u32[]{:S(2)}) collective-permute-start(f32[2,8,34,1]{3,2,0,1:T(8,128)S(1)} %get-tuple-element.136), channel_id=1, source_target_pairs={{0,1},{1,2},{2,3},{3,0},{4,5},{5,6},{6,7},{7,4},{8,9},{9,10},{10,1... | collective-permute-start | bytes 6536 | tf_op jit(solution)/shard_map/ppermute | solution.py:24
  703.8 10.4 %collective-permute-start.32 = (f32[2,8,34,1]{3,2,0,1:T(8,128)S(1)}, f32[2,8,34,1]{3,2,0,1:T(8,128)}, u32[]{:S(2)}, u32[]{:S(2)}) collective-permute-start(f32[2,8,34,1]{3,2,0,1:T(8,128)S(1)} %get-tuple-element.135), channel_id=1, source_target_pairs={{1,0},{2,1},{3,2},{0,3},{5,4},{6,5},{7,6},{4,7},{9,8},{10,9},{11,1... | collective-permute-start | bytes 6536 | tf_op jit(solution)/shard_map/ppermute | solution.py:26
  (40 other events, 3284.8 us)
Sparse Core Ops, SparseCore 0:
  708.6 278.0 all-reduce.2
where the time goes:
time: 1010 us; the launch traced here: 996 us
  waiting for transfers between devices  313 us (31%)
  other arithmetic  266 us (26%)
  local copies, waits for them, and re-layouts  194 us (19%)
  blocking collectives  106 us (10%)
  starting transfers between devices  96.8 us (10%)
  between operations  16.8 us (2%)
    psum x1, waiting for transfers between devices, shards(): grad_controls = lax.psum(local_grad, ('lon', 'lat'))  270 us
    scatter-add x8, other arithmetic, shards(): source = source.at[:, corners[corner]].add(records[corner] * scaled_miss)  243 us
    psum x1, blocking collectives, shards(): source_scale = normalizer / lax.psum(weight_local, ('lon', 'lat'))  106 us
    gather x12, local copies, waits for them, and re-layouts, shards(): jnp.take(flattened, corners[corner], axis=1)  98.5 us
    gather x4, local copies, waits for them, and re-layouts, shards(): modeled = records[0] * jnp.take(flattened, corners[0], axis=1)  32.9 us
    ppermute x9, starting transfers between devices, from_behind_2(): return lax.ppermute(block, axis, route)  26.1 us
    ppermute x8, starting transfers between devices, padded_2(): lax.ppermute(head, axis, [((i + 1) % count, i) for i in range(count)])  25.2 us
    ppermute x8, waiting for transfers between devices, padded_2(): lax.ppermute(tail, axis, [(i, (i + 1) % count) for i in range(count)])  25 us
  transfers between devices with their start and end apart: 35, of which 17 were waited for; matrix products, arithmetic and copies ran while one was open for 22% of the time, Pallas kernels for 0%

commit v1 on v0

v1 whole, which is shorter than its diff:
```python
import functools
import math

import jax
import jax.numpy as jnp
from jax import lax
from jax.experimental import pallas as pl
from jax.experimental.pallas import tpu as pltpu
from jax.sharding import PartitionSpec as P

CAPACITY = 128
VISCOUS = 0.1
FRICTION = 0.02
ROTATION = 0.3
STEPS = 2
DEPTH = STEPS + 1
CODES = (0, 1, 2, 3, 5, 6, 7, 8)
FIELDS = 8
PLANES = 2 * DEPTH + 2
LOW, HIGH = 2, 3
X0, Y0 = 8, 128
GROUP = 32
F32, BF16 = jnp.float32, jnp.bfloat16
VMEM = pltpu.CompilerParams(vmem_limit_bytes=48 * 1024 * 1024)


def iota(shape, dim):
    return lax.broadcasted_iota(jnp.int32, shape, dim)


def split(value):
    high = value.astype(BF16)
    return high, (value - high.astype(F32)).astype(BF16)


def dot(a, b):
    return lax.dot_general(a, b, (((1,), (0,)), ((), ())), preferred_element_type=F32)


def dot_lanes(a, b):
    return lax.dot_general(a, b, (((1,), (1,)), ((), ())), preferred_element_type=F32)


def roll(value, shift, axis):
    return pltpu.roll(value, shift % value.shape[axis], axis)


def period_weights(steps_total, periods):
    table = []
    for step in range(steps_total):
        position = (step + 0.5) * (periods - 1) / steps_total
        table.append([max(0.0, 1.0 - abs(position - period)) for period in range(periods)])
    return table


def pack_kernel(move, cell, weight, obs, prec, init, depth, mixing, fields, east, west, south, north):
    count = move.shape[1]
    for step in range(STEPS):
        base = step * FIELDS
        for i in range(4):
            fields[base + i : base + i + 1, :] = weight[i, step : step + 1, :]
        for i in range(2):
            fields[base + 4 + i : base + 5 + i, :] = obs[i, step : step + 1, :]
        fields[base + 6 : base + 7, :] = prec[step : step + 1, :]
        fields[base + 7 : base + 8, :] = cell[step : step + 1, :].astype(F32)
    rows = init.shape[2]
    planes = [init.at[c, k] for c in range(2) for k in range(DEPTH)]
    for p in range(PLANES):
        if p < 2 * DEPTH:
            first, last = planes[p][:HIGH, :], planes[p][rows - LOW :, :]
        elif p == 2 * DEPTH:
            first, last = depth[:HIGH, :].astype(F32), depth[rows - LOW :, :].astype(F32)
        else:
            first, last = mixing[:HIGH, :], mixing[rows - LOW :, :]
        west[3 * FIELDS + HIGH * p : 3 * FIELDS + HIGH * (p + 1), :] = first
        east[3 * FIELDS + LOW * p : 3 * FIELDS + LOW * (p + 1), :] = last
    width = 256
    triangle = (iota((width, width), 0) <= iota((width, width), 1)).astype(F32).astype(BF16)
    code = iota((8, 1), 0)
    code = code + (code >= 4).astype(jnp.int32)
    carry = [jnp.zeros((8, 1), F32) for _ in range(STEPS)]
    packed = [jnp.zeros((8 * 2 * FIELDS, CAPACITY), F32) for _ in range(STEPS)]
    slot = iota((CAPACITY, width), 0)
    for at in range(0, count, width):
        for step in range(STEPS):
            match = (move[step : step + 1, at : at + width] == code).astype(F32)
            rank = dot(match.astype(BF16), triangle) + carry[step]
            carry[step] = rank[:, width - 1 :]
            place = jnp.sum(match * (rank - 1.0), axis=0, keepdims=True).astype(jnp.int32)
            spots = (slot == place).astype(F32).astype(BF16)
            record = fields[step * FIELDS : (step + 1) * FIELDS, at : at + width]
            high, low = split(record)
            both = jnp.concatenate([high.astype(F32), low.astype(F32)], axis=0)
            masked = jnp.concatenate([both * match[d : d + 1] for d in range(8)], axis=0)
            packed[step] = packed[step] + dot_lanes(masked.astype(BF16), spots)
    for step in range(STEPS):
        lanes = slice(step * CAPACITY, (step + 1) * CAPACITY)
        for d in range(8):
            at = d * 2 * FIELDS
            record = packed[step][at : at + FIELDS] + packed[step][at + FIELDS : at + 2 * FIELDS]
            code = CODES[d]
            if code // 3 == 1:
                (south if code % 3 == 0 else north)[:, lanes] = record
            else:
                row = (code % 3) * FIELDS
                (west if code // 3 == 0 else east)[row : row + FIELDS, lanes] = record
    for step in range(STEPS):
        row = step * FIELDS + 6
        fields[row : row + 1, :] = jnp.where(move[step : step + 1, :] == 4, prec[step : step + 1, :], 0.0)


def extend_lon(ext, p, own, from_west, from_east, rows, cells_lat):
    lanes = slice(Y0, Y0 + cells_lat)
    ext[p, X0 : X0 + rows, lanes] = own
    at = 3 * FIELDS + LOW * p
    ext[p, X0 - LOW : X0, lanes] = from_west[at : at + LOW, :]
    at = 3 * FIELDS + HIGH * p
    ext[p, X0 + rows : X0 + rows + HIGH, lanes] = from_east[at : at + HIGH, :]


def merge_kernel(init, depth, mixing, to_south, to_north, from_west, from_east, ext, south, north):
    rows, cells_lat = depth.shape
    ext[...] = jnp.zeros_like(ext)
    for p in range(PLANES):
        if p < 2 * DEPTH:
            own = init[p // DEPTH, p % DEPTH]
        else:
            own = depth[...].astype(F32) if p == 2 * DEPTH else mixing[...]
        extend_lon(ext, p, own, from_west, from_east, rows, cells_lat)
    tall = ext.shape[1]
    lane = iota((tall, 128), 1)
    first = jnp.zeros((tall, 128), F32)
    last = jnp.zeros((tall, 128), F32)
    for p in range(PLANES):
        head = jnp.where(lane < HIGH, ext[p, :, Y0 : Y0 + 128], 0.0)
        tail = jnp.where(lane >= 128 - LOW, ext[p, :, Y0 + cells_lat - 128 : Y0 + cells_lat], 0.0)
        first = first + roll(head, HIGH * p, 1)
        last = last + roll(tail, -LOW * p, 1)
    for out, kept, row, strip in ((south, to_south, 0, first), (north, to_north, 2, last)):
        out[0:FIELDS, :] = kept[...]
        out[FIELDS : 2 * FIELDS, :] = from_west[row * FIELDS : (row + 1) * FIELDS, :]
        out[2 * FIELDS : 3 * FIELDS, :] = from_east[row * FIELDS : (row + 1) * FIELDS, :]
        out[3 * FIELDS :, 0:128] = strip[: tall // 2]
        out[3 * FIELDS :, 128:] = strip[tall // 2 :]


def lap(v):
    return roll(v, 1, 0) + roll(v, -1, 0) + roll(v, 1, 1) + roll(v, -1, 1) - 4.0 * v


def vz(column, k, levels):
    above = column[max(k - 1, 0)]
    below = min(k + 1, levels - 1)
    total = above - 2.0 * column[k] if k < len(column) else above
    return total + column[below] if below < len(column) else total


def tendency(v, k, mixing, rotation, levels):
    out = []
    for c in range(2):
        value = v[c][k] + mixing(v[c][k]) + VISCOUS * vz(v[c], k, levels) - FRICTION * v[c][k]
        turned = rotation * v[1 - c][k]
        out.append(value + turned if c == 0 else value - turned)
    return out


def main_kernel(
    levels, refine, lon_count, lat_count, controls, fields, precision, from_west, from_east, from_south, from_north,
    padded, partial, share, to_west, to_east, ext, spot,
):
    rows, cells_lat = partial.shape[1] - 16, partial.shape[2] - 256
    tall, wide = ext.shape[1:]
    lon_index, lat_index = lax.axis_index("lon"), lax.axis_index("lat")
    grid_lat = cells_lat * lat_count
    periods, _, ctrl_lon, ctrl_lat = controls.shape
    table = period_weights(STEPS, periods)
    lane = iota((tall, 128), 1)
    half = tall // 2
    below = jnp.concatenate([from_south[3 * FIELDS :, 0:128], from_south[3 * FIELDS :, 128:]], axis=0)
    above = jnp.concatenate([from_north[3 * FIELDS :, 0:128], from_north[3 * FIELDS :, 128:]], axis=0)
    full = []
    for p in range(PLANES):
        left = jnp.where(lane >= 128 - LOW, roll(below, LOW * p, 1), 0.0)
        right = jnp.where(lane < HIGH, roll(above, -HIGH * p, 1), 0.0)
        full.append(jnp.concatenate([left, padded[p, :, Y0 : Y0 + cells_lat], right], axis=1))
    mixing = full[2 * DEPTH + 1]
    wet = [(full[2 * DEPTH] > float(k)).astype(F32) for k in range(DEPTH)]
    row_ids = iota((1, wide), 1) - Y0 + lat_index * cells_lat
    rotation = ROTATION * jnp.sin((row_ids.astype(F32) + 0.5) * (math.pi / grid_lat) - 0.5 * math.pi)
    offset = iota((tall, ctrl_lon), 0) - X0 + lon_index * rows - refine // 2
    low = lax.shift_right_arithmetic(offset, refine.bit_length() - 1)
    part = ((offset - low * refine).astype(F32) + 0.5) / refine
    column = iota((tall, ctrl_lon), 1)
    wrapped, after = (low + ctrl_lon) % ctrl_lon, (low + 1 + ctrl_lon) % ctrl_lon
    lon_interp = jnp.where(column == wrapped, 1.0 - part, 0.0) + jnp.where(column == after, part, 0.0)
    offset = iota((ctrl_lat, wide), 1) - Y0 + lat_index * cells_lat - refine // 2
    low = lax.shift_right_arithmetic(offset, refine.bit_length() - 1)
    part = ((offset - low * refine).astype(F32) + 0.5) / refine
    column = iota((ctrl_lat, wide), 0)
    lat_interp = jnp.where(column == low, 1.0 - part, 0.0) + jnp.where(column == low + 1, part, 0.0)
    lon_interp, lat_interp = lon_interp.astype(BF16), lat_interp.astype(BF16)
    forcing = []
    for step in range(STEPS):
        forcing.append([])
        for c in range(2):
            blended = table[step][0] * controls[0, c]
            for period in range(1, periods):
                blended = blended + table[step][period] * controls[period, c]
            high, low = split(blended)
            high, low = split(dot(lon_interp, high) + dot(lon_interp, low))
            forcing[step].append(dot(high, lat_interp) + dot(low, lat_interp))
    state = [[wet[k] * full[c * DEPTH + k] for k in range(DEPTH)] for c in range(2)]
    surfaces = []
    for step in range(STEPS):
        ahead = [[], []]
        for k in range(DEPTH - 1 - step):
            moved = tendency(state, k, lambda v: mixing * lap(v), rotation, levels)
            for c in range(2):
                value = moved[c] + forcing[step][c] if k == 0 else moved[c]
                ahead[c].append(wet[k] * value)
        state = ahead
        surfaces.append([state[0][0], state[1][0]])
    strip = rows + 8
    chunk = 512
    lat_of = iota((cells_lat, chunk), 0)
    lon_of = iota((strip, chunk), 0)
    sources = []
    for step in range(STEPS):
        views = []
        for c in range(2):
            surface = surfaces[step][c][X0 : X0 + strip]
            views += [surface[:, Y0 : Y0 + cells_lat], roll(surface, -1, 1)[:, Y0 : Y0 + cells_lat]]
        views_high, views_low = split(jnp.concatenate(views, axis=0))

        def spread(record, total):
            cell = record[7:8].astype(jnp.int32)
            lon = lax.shift_right_logical(cell, cells_lat.bit_length() - 1)
            lat = cell & (cells_lat - 1)
            hot = (lat_of == lat).astype(F32).astype(BF16)
            found = dot(views_high, hot) + dot(views_low, hot)
            here, there = lon_of == lon, lon_of == lon + 1
            near = jnp.where(here, record[0:1], jnp.where(there, record[1:2], 0.0))
            far = jnp.where(here, record[2:3], jnp.where(there, record[3:4], 0.0))
            terms = []
            for c in range(2):
                at = 2 * c * strip
                seen = near * found[at : at + strip] + far * found[at + strip : at + 2 * strip]
                miss = jnp.sum(seen, axis=0, keepdims=True) - record[4 + c : 5 + c]
                miss = record[6:7] * miss
                terms += [near * miss, far * miss]
            high, low = split(jnp.concatenate(terms, axis=0))
            return total + dot_lanes(high, hot) + dot_lanes(low, hot)

        total = jnp.zeros((4 * strip, cells_lat), F32)
        for at in range(0, fields.shape[1], chunk):
            total = spread(fields[step * FIELDS : (step + 1) * FIELDS, at : at + chunk], total)
        lanes = slice(step * CAPACITY, (step + 1) * CAPACITY)
        came = [from_west[FIELDS : 2 * FIELDS, lanes], from_east[FIELDS : 2 * FIELDS, lanes]]
        came += [message[i * FIELDS : (i + 1) * FIELDS, lanes] for message in (from_south, from_north) for i in range(3)]
        for at in range(0, 8, chunk // CAPACITY):
            total = spread(jnp.concatenate(came[at : at + chunk // CAPACITY], axis=1), total)
        sources.append([])
        for c in range(2):
            at = 2 * c * strip
            spot[...] = jnp.zeros_like(spot)
            spot[0, X0 : X0 + strip, Y0 : Y0 + cells_lat] = total[at : at + strip]
            spot[1, X0 : X0 + strip, Y0 : Y0 + cells_lat] = total[at + strip : at + 2 * strip]
            sources[step].append(spot[0] + roll(spot[1], 1, 1))
    adjoint = None
    nudges = [None] * STEPS
    for step in reversed(range(STEPS)):
        if adjoint is None:
            adjoint = [[sources[step][c]] for c in range(2)]
        else:
            adjoint = [[adjoint[c][0] + sources[step][c]] + adjoint[c][1:] for c in range(2)]
        nudged = [[wet[k] * adjoint[c][k] for k in range(len(adjoint[c]))] for c in range(2)]
        nudges[step] = [nudged[0][0], nudged[1][0]]
        reach = len(nudged[0])
        adjoint = [[], []]
        for k in range(reach):
            moved = tendency(nudged, k, lambda v: lap(mixing * v), -rotation, levels)
            for c in range(2):
                adjoint[c].append(moved[c])
        for c in range(2):
            adjoint[c].append(VISCOUS * vz(nudged[c], reach, levels))
    for c in range(2):
        for k in range(DEPTH):
            p = c * DEPTH + k
            ext[p] = adjoint[c][k]
            partial[p] = adjoint[c][k]
            to_west[LOW * p : LOW * (p + 1), :] = ext[p, X0 - LOW : X0, :]
            to_east[HIGH * p : HIGH * (p + 1), :] = ext[p, X0 + rows : X0 + rows + HIGH, :]
    offset = iota((wide, 128), 0) - Y0 - refine // 2
    low = lax.shift_right_arithmetic(offset, refine.bit_length() - 1)
    part = ((offset - low * refine).astype(F32) + 0.5) / refine
    column = iota((wide, 128), 1) % GROUP - 1
    onto_lat = jnp.where(column == low, 1.0 - part, 0.0) + jnp.where(column == low + 1, part, 0.0)
    onto_lat = onto_lat.astype(BF16)
    offset = iota((tall, 128), 0) - X0 - refine // 2
    low = lax.shift_right_arithmetic(offset, refine.bit_length() - 1)
    part = ((offset - low * refine).astype(F32) + 0.5) / refine
    column = iota((tall, 128), 1) // GROUP - 1
    onto_lon = jnp.where(column == low, 1.0 - part, 0.0) + jnp.where(column == low + 1, part, 0.0)
    for step in range(STEPS):
        for c in range(2):
            high, low = split(nudges[step][c])
            across = dot(high, onto_lat) + dot(low, onto_lat)
            row = 2 * step + c
            share[row : row + 1, :] = jnp.sum(onto_lon * across, axis=0, keepdims=True)
    weight = jnp.sum(jnp.sum(precision[...], axis=0, keepdims=True), axis=1, keepdims=True)
    share[0:1, :] = jnp.where(iota((1, 128), 1) == GROUP - 1, weight, share[0:1, :])


def join_kernel(partial, from_west, from_east, own, south, north):
    rows, cells_lat = own.shape[1:]
    lane = iota((rows, 128), 1)
    first = jnp.zeros((rows, 128), F32)
    last = jnp.zeros((rows, 128), F32)
    for p in range(2 * DEPTH):
        partial[p, X0 : X0 + HIGH, :] += from_west[HIGH * p : HIGH * (p + 1), :]
        partial[p, X0 + rows - LOW : X0 + rows, :] += from_east[LOW * p : LOW * (p + 1), :]
        block = partial[p, X0 : X0 + rows, :]
        own[p] = block[:, Y0 : Y0 + cells_lat]
        tail = jnp.where(lane >= 128 - LOW, block[:, Y0 - 128 : Y0], 0.0)
        head = jnp.where(lane < HIGH, block[:, Y0 + cells_lat : Y0 + cells_lat + 128], 0.0)
        first = first + roll(tail, -LOW * p, 1)
        last = last + roll(head, HIGH * p, 1)
    south[...] = first
    north[...] = last


def finish_kernel(normalizer, lat_count, own, depth, from_south, from_north, shares, grad, out):
    levels, rows, cells_lat = grad.shape[1:]
    periods = out.shape[0]
    table = period_weights(STEPS, periods)
    lon_count = out.shape[2] // 2
    per = out.shape[3] // lat_count
    lane = iota(shares.shape, 1)
    row = iota(shares.shape, 0)
    held = jnp.where((lane == GROUP - 1) & (row % (2 * STEPS) == 0), shares[...], 0.0)
    scale = normalizer / jnp.sum(jnp.sum(held, axis=0, keepdims=True), axis=1, keepdims=True)
    side = iota((rows, 128), 1)
    wet_levels = depth[...]
    for c in range(2):
        for k in range(levels):
            if k >= DEPTH:
                grad[c, k] = jnp.zeros((rows, cells_lat), F32)
                continue
            p = c * DEPTH + k
            low = jnp.where(side < HIGH, roll(from_south[...], -HIGH * p, 1), 0.0)
            high = jnp.where(side >= 128 - LOW, roll(from_north[...], LOW * p, 1), 0.0)
            value = own[p] + jnp.concatenate([low, high], axis=1)
            grad[c, k] = jnp.where(wet_levels > k, value * scale, 0.0)
    source = iota((128, 384), 0)
    target = iota((128, 384), 1)
    a, b = source // GROUP, source % GROUP
    kind, i, column = target // 128, target % 128 // 64, target % 64
    right_row = ((kind == 0) & (a == i + 1)) | ((kind == 1) & (a == 3) & (i == 0)) | ((kind == 2) & (a == 0) & (i == 1))
    right_row = right_row & (b < per + 2)
    gathered = [jnp.zeros((lon_count, 384), F32) for _ in range(2 * STEPS)]
    for m in range(lat_count):
        pick = (right_row & (column == per * m - 1 + b)).astype(F32).astype(BF16)
        for t in range(2 * STEPS):
            high, low = split(shares[pl.ds(m * 2 * STEPS + t, lon_count, stride=lat_count * 2 * STEPS), :])
            gathered[t] = gathered[t] + dot(high, pick) + dot(low, pick)
    scaled = []
    for t in range(2 * STEPS):
        part = gathered[t]
        scaled.append(scale * (part[:, :128] + roll(part[:, 128:256], 1, 0) + roll(part[:, 256:], -1, 0)))
    for period in range(periods):
        for c in range(2):
            value = table[0][period] * scaled[c]
            for step in range(1, STEPS):
                value = value + table[step][period] * scaled[2 * step + c]
            for i in range(2):
                out[period, c, pl.ds(i, lon_count, stride=2), :] = value[:, 64 * i : 64 * i + 64]


def around(value, distance):
    count = lax.axis_size("lon")
    return lax.ppermute(value, "lon", [(i, (i + distance) % count) for i in range(count)])


def along(value, distance):
    count = lax.axis_size("lat")
    return lax.ppermute(value, "lat", [(i, i + distance) for i in range(max(0, -distance), min(count, count - distance))])


def whole(shape):
    return pl.BlockSpec(shape, lambda i: (0,) * len(shape))


def call(kernel, ins, outs, blocks=None, scratch=(), **kwargs):
    blocks = blocks or {}
    return pl.pallas_call(
        kernel,
        grid=(1,),
        out_shape=[jax.ShapeDtypeStruct(shape, F32) for shape in outs],
        in_specs=[whole(blocks.get(i, value.shape)) for i, value in enumerate(ins)],
        out_specs=[whole(shape) for shape in outs],
        scratch_shapes=[pltpu.VMEM(shape, F32) for shape in scratch],
        compiler_params=VMEM,
        **kwargs,
    )(*ins)


def shards(
    initial, depth_levels, mixing, controls, drift_move, drift_cell, drift_weight, drift_obs, drift_precision
):
    _, levels, rows, cells_lat = initial.shape
    periods, _, ctrl_lon, ctrl_lat = controls.shape
    count = drift_move.shape[1]
    lon_count, lat_count = lax.axis_size("lon"), lax.axis_size("lat")
    refine = rows * lon_count // ctrl_lon
    tall, wide = rows + 16, cells_lat + 256
    surface = (2, DEPTH, rows, cells_lat)
    lon_low, lon_high = (3 * FIELDS + LOW * PLANES, 256), (3 * FIELDS + HIGH * PLANES, 256)
    fields, east, west, south, north = call(
        pack_kernel,
        (drift_move, drift_cell, drift_weight, drift_obs, drift_precision, initial, depth_levels, mixing),
        ((STEPS * FIELDS, count), lon_low, lon_high, (FIELDS, 256), (FIELDS, 256)),
        {5: surface},
    )
    from_west, from_east = around(east, 1), around(west, -1)
    message = (3 * FIELDS + tall // 2, 256)
    padded, south, north = call(
        merge_kernel,
        (initial, depth_levels, mixing, south, north, from_west, from_east),
        ((PLANES, tall, wide), message, message),
        {0: surface},
    )
    from_south, from_north = along(north, 1), along(south, -1)
    partial, share, to_west, to_east = call(
        functools.partial(main_kernel, levels, refine, lon_count, lat_count),
        (controls, fields, drift_precision, from_west, from_east, from_south, from_north, padded),
        ((2 * DEPTH, tall, wide), (2 * STEPS, 128), (2 * DEPTH * LOW, wide), (2 * DEPTH * HIGH, wide)),
        scratch=((2 * DEPTH, tall, wide), (2, tall, wide)),
    )
    shares = lax.all_gather(share, ("lon", "lat"), axis=0, tiled=True)
    from_west, from_east = around(to_east, 1), around(to_west, -1)
    own, to_south, to_north = call(
        join_kernel,
        (partial, from_west, from_east),
        ((2 * DEPTH, rows, cells_lat), (rows, 128), (rows, 128)),
    )
    from_south, from_north = along(to_north, 1), along(to_south, -1)
    grad_initial, grad_controls = call(
        functools.partial(finish_kernel, float(STEPS * count * lon_count * lat_count), lat_count),
        (own, depth_levels, from_south, from_north, shares),
        (initial.shape, controls.shape),
    )
    return grad_initial, grad_controls


def solution(mesh):
    return jax.shard_map(
        shards,
        mesh=mesh,
        in_specs=(
            P(None, None, "lon", "lat"),
            P("lon", "lat"),
            P("lon", "lat"),
            P(),
            P(None, ("lon", "lat")),
            P(None, ("lon", "lat")),
            P(None, None, ("lon", "lat")),
            P(None, None, ("lon", "lat")),
            P(None, ("lon", "lat")),
        ),
        out_specs=(P(None, None, "lon", "lat"), P()),
        check_vma=False,
    )
```

time: 1010 us -> 173 us (0.17)
  the two profiles are of different devices: /device:TPU:24 before, /device:TPU:1 now
where the time goes in v1:
time: 173 us; the launch traced here: 172 us
  waiting for transfers between devices  103 us (60%)
  starting transfers between devices  31 us (18%)
  between operations  14.2 us (8%)
  Pallas kernels  13.9 us (8%)
  local copies, waits for them, and re-layouts  9.25 us (5%)
    all_gather x1, waiting for transfers between devices, shards(): shares = lax.all_gather(share, ('lon', 'lat'), axis=0, tiled=True)  89.1 us
    ppermute x4, starting transfers between devices, around(): lax.ppermute(value, 'lon', [(i, (i + distance) % count) for i in range(co...  22.1 us
    pallas_call x5, Pallas kernels, call(): pl.pallas_call(kernel, grid=(1,), out_shape=[jax.ShapeDtypeStruct(shape,...  13.9 us
    ppermute x4, starting transfers between devices, along(): lax.ppermute(value, 'lat', [(i, i + distance) for i in range(max(0, -dist...  8.83 us
    unnamed x27, local copies, waits for them, and re-layouts  8.14 us
    ppermute x4, waiting for transfers between devices, around(): lax.ppermute(value, 'lon', [(i, (i + distance) % count) for i in range(co...  7.54 us
    ppermute x4, waiting for transfers between devices, along(): lax.ppermute(value, 'lat', [(i, i + distance) for i in range(max(0, -dist...  6.76 us
  transfers between devices with their start and end apart: 9, of which 5 were waited for; matrix products, arithmetic and copies ran while one was open for 0% of the time, Pallas kernels for 0%

profile of v1, /device:TPU:1, one launch (start us, length us, event | category | flops | bytes accessed | tf_op | source)
XLA Modules:
  0.0 171.7 jit_solution(11840006457161367992)
XLA Ops:
  7.2 0.0 all-gather.3.cloned.1.call-start
  7.2 1.0 copy-done
  8.3 0.8 copy-done.3
  9.0 0.8 copy-done.5
  9.8 0.8 copy-done.7
  10.5 0.9 copy-done.8
  11.4 0.8 copy-done.9
  12.3 0.8 copy-done.10
  13.0 0.8 copy-done.11
  13.8 3.3 %shard_map.104 = (f32[16,4096]{1,0:T(8,128)S(1)}, f32[40,256]{1,0:T(8,128)S(1)}, f32[48,256]{1,0:T(8,128)S(1)}, f32[8,256]{1,0:T(8,128)S(1)}, f32[8,256]{1,0:T(8,128)S(1)}) custom-call(s32[2,4096]{1,0:T(2,128)S(1)} %copy-done.10, s32[2,4096]{1,0:T(2,128)S(1)} %copy-done.11, f32[4,2,4096]{2,1,0:T(2,128)S(1)} %copy-done.8, f32[2,2,4096]{2,1,0:T(2,128)S(1)} %copy-done.9, ...), custom_call_target="tpu_custom_call" | custom-call | tf_op jit(solution)/shard_map/pallas_call | solution.py:395
  17.1 0.0 copy-start.12
  17.1 8.9 %collective-permute-start.1 = (f32[48,256]{1,0:T(8,128)S(1)}, f32[48,256]{1,0:T(8,128)S(1)}, u32[]{:S(2)}, u32[]{:S(2)}) collective-permute-start(f32[48,256]{1,0:T(8,128)S(1)} %get-tuple-element.19), channel_id=1, source_target_pairs={{0,508},{4,0},{8,4},{12,8},{16,12},{20,16},{24,20},{28,24},{32,28}... | collective-permute-start | bytes 147464 | tf_op jit(solution)/shard_map/ppermute | solution.py:381
  26.0 1.9 %collective-permute-start = (f32[40,256]{1,0:T(8,128)S(1)}, f32[40,256]{1,0:T(8,128)S(1)}, u32[]{:S(2)}, u32[]{:S(2)}) collective-permute-start(f32[40,256]{1,0:T(8,128)S(1)} %get-tuple-element.18), channel_id=1, source_target_pairs={{0,4},{4,8},{8,12},{12,16},{16,20},{20,24},{24,28},{28,32},{32,36}... | collective-permute-start | bytes 122888 | tf_op jit(solution)/shard_map/ppermute | solution.py:381
  27.9 6.7 %collective-permute-done.from_west = f32[40,256]{1,0:T(8,128)S(1)} collective-permute-done((f32[40,256]{1,0:T(8,128)S(1)}, f32[40,256]{1,0:T(8,128)S(1)}, u32[]{:S(2)}, u32[]{:S(2)}) %collective-permute-start) | collective-permute-done | bytes 40992 | tf_op jit(solution)/shard_map/ppermute | solution.py:381
  34.6 0.2 shard_map.105
  34.8 3.1 %collective-permute-start.2 = (f32[48,256]{1,0:T(8,128)S(1)}, f32[48,256]{1,0:T(8,128)S(1)}, u32[]{:S(2)}, u32[]{:S(2)}) collective-permute-start(f32[48,256]{1,0:T(8,128)S(1)} %get-tuple-element.22), channel_id=1, source_target_pairs={{0,1},{1,2},{2,3},{4,5},{5,6},{6,7},{8,9},{9,10},{10,11},{12,13},{... | collective-permute-start | bytes 147464 | tf_op jit(solution)/shard_map/ppermute | solution.py:386
  38.0 1.3 collective-permute-start.3
  39.3 0.3 copy.13.controls
  39.6 3.2 %collective-permute-done.3.from_north = f32[48,256]{1,0:T(8,128)S(1)} collective-permute-done((f32[48,256]{1,0:T(8,128)S(1)}, f32[48,256]{1,0:T(8,128)S(1)}, u32[]{:S(2)}, u32[]{:S(2)}) %collective-permute-start.3) | collective-permute-done | bytes 49184 | tf_op jit(solution)/shard_map/ppermute | solution.py:386
  42.8 8.4 %shard_map.106 = (f32[6,48,512]{2,1,0:T(8,128)S(1)}, f32[4,128]{1,0:T(4,128)}, f32[12,512]{1,0:T(8,128)S(1)}, f32[18,512]{1,0:T(8,128)S(1)}) custom-call(f32[4,2,256,64]{3,2,1,0:T(8,128)S(1)} %copy.13.controls, f32[16,4096]{1,0:T(8,128)S(1)} %get-tuple-element.17.fields, f32[2,4096]{1,0:T(2,128)S(1)} %copy-done.6, ...), custom_call_target="tpu_custom_call" | custom-call | tf_op jit(solution)/shard_map/pallas_call | solution.py:395
  51.2 0.0 all-gather.3.cloned.1.call-update
  51.2 1.9 %collective-permute-start.4 = (f32[18,512]{1,0:T(8,128)S(1)}, f32[18,512]{1,0:T(8,128)S(1)}, u32[]{:S(2)}, u32[]{:S(2)}) collective-permute-start(f32[18,512]{1,0:T(8,128)S(1)} %get-tuple-element.26), channel_id=1, source_target_pairs={{0,4},{4,8},{8,12},{12,16},{16,20},{20,24},{24,28},{28,32},{32,36}... | collective-permute-start | bytes 110600 | tf_op jit(solution)/shard_map/ppermute | solution.py:381
  53.2 9.4 %collective-permute-start.5 = (f32[12,512]{1,0:T(8,128)S(1)}, f32[12,512]{1,0:T(8,128)S(1)}, u32[]{:S(2)}, u32[]{:S(2)}) collective-permute-start(f32[12,512]{1,0:T(8,128)S(1)} %get-tuple-element.27), channel_id=1, source_target_pairs={{0,508},{4,0},{8,4},{12,8},{16,12},{20,16},{24,20},{28,24},{32,28}... | collective-permute-start | bytes 73736 | tf_op jit(solution)/shard_map/ppermute | solution.py:381
  62.5 0.8 collective-permute-done.5.from_east
  63.4 0.1 shard_map.107
  63.5 3.1 %collective-permute-start.6 = (f32[32,128]{1,0:T(8,128)S(1)}, f32[32,128]{1,0:T(8,128)S(1)}, u32[]{:S(2)}, u32[]{:S(2)}) collective-permute-start(f32[32,128]{1,0:T(8,128)S(1)} %get-tuple-element.29), channel_id=1, source_target_pairs={{0,1},{1,2},{2,3},{4,5},{5,6},{6,7},{8,9},{9,10},{10,11},{12,13},{... | collective-permute-start | bytes 49160 | tf_op jit(solution)/shard_map/ppermute | solution.py:386
  66.6 1.3 collective-permute-start.7
  68.0 3.6 %collective-permute-done.7.from_north = f32[32,128]{1,0:T(8,128)S(1)} collective-permute-done((f32[32,128]{1,0:T(8,128)S(1)}, f32[32,128]{1,0:T(8,128)S(1)}, u32[]{:S(2)}, u32[]{:S(2)}) %collective-permute-start.7) | collective-permute-done | bytes 16416 | tf_op jit(solution)/shard_map/ppermute | solution.py:386
  71.5 89.1 %all-gather.3.cloned.1.call-done = f32[512,4,128]{2,1,0:T(4,128)} async-done(((f32[1,4,128]{2,1,0:T(4,128)}), f32[512,4,128]{2,1,0:T(4,128)}) %all-gather.3.cloned.1.call-update) | async-done | bytes 1048592 | tf_op jit(solution)/shard_map/all_gather | solution.py:439
  160.6 1.2 copy-done.2
  161.9 1.9 %shard_map.108 = (f32[2,8,32,256]{3,2,1,0:T(8,128)}, f32[4,2,256,64]{3,2,1,0:T(8,128)S(1)}) custom-call(f32[6,32,256]{2,1,0:T(8,128)S(1)} %get-tuple-element.28.own, s32[32,256]{1,0:T(8,128)S(1)} %copy-done.4, f32[32,128]{1,0:T(8,128)S(1)} %collective-permute-done.6.from_south, f32[32,128]{1,0:T(8,128)S(1)} %collective-permute-done.7.from_north, ...), custom_call_target="tpu_custom_call" | custom-call | tf_op jit(solution)/shard_map/pallas_call | solution.py:395
  163.8 1.1 copy.14
  (20 shorter events, 0.0 us)
Async XLA Ops:
  7.2 153.5 %all-gather.3.cloned.1.call-start = ((), (), s32[]{:S(2)}) async-start(), calls=%async_computation | async-start | bytes 1050624 | tf_op jit(solution)/shard_map/all_gather | solution.py:439
  7.2 1.0 copy-start
  8.3 0.8 copy-start.3
  9.0 0.8 copy-start.5
  9.8 0.8 copy-start.7
  10.5 0.9 copy-start.8
  11.4 0.8 copy-start.9
  12.3 0.8 copy-start.10
  13.0 0.8 copy-start.11
  13.8 20.8 %copy-start.1 = (f32[2,8,32,256]{3,2,1,0:T(8,128)S(1)}, f32[2,8,32,256]{3,2,1,0:T(8,128)}, u32[]{:S(2)}) copy-start(f32[2,8,32,256]{3,2,1,0:T(8,128)} %init.3) | copy-start | bytes 1572868
  17.1 22.2 %copy-start.12 = (f32[4,2,256,64]{2,3,1,0:T(8,128)S(1)}, f32[4,2,256,64]{2,3,1,0:T(8,128)}, u32[]{:S(2)}) copy-start(f32[4,2,256,64]{2,3,1,0:T(8,128)} %param.12) | copy-start | bytes 1572868
  17.1 17.6 %collective-permute-start.1 = (f32[48,256]{1,0:T(8,128)S(1)}, f32[48,256]{1,0:T(8,128)S(1)}, u32[]{:S(2)}, u32[]{:S(2)}) collective-permute-start(f32[48,256]{1,0:T(8,128)S(1)} %get-tuple-element.19), channel_id=1, source_target_pairs={{0,508},{4,0},{8,4},{12,8},{16,12},{20,16},{24,20},{28,24},{32,28}... | collective-permute-start | bytes 147464 | tf_op jit(solution)/shard_map/ppermute | solution.py:381
  26.0 8.6 %collective-permute-start = (f32[40,256]{1,0:T(8,128)S(1)}, f32[40,256]{1,0:T(8,128)S(1)}, u32[]{:S(2)}, u32[]{:S(2)}) collective-permute-start(f32[40,256]{1,0:T(8,128)S(1)} %get-tuple-element.18), channel_id=1, source_target_pairs={{0,4},{4,8},{8,12},{12,16},{16,20},{20,24},{24,28},{28,32},{32,36}... | collective-permute-start | bytes 122888 | tf_op jit(solution)/shard_map/ppermute | solution.py:381
  34.8 4.8 %collective-permute-start.2 = (f32[48,256]{1,0:T(8,128)S(1)}, f32[48,256]{1,0:T(8,128)S(1)}, u32[]{:S(2)}, u32[]{:S(2)}) collective-permute-start(f32[48,256]{1,0:T(8,128)S(1)} %get-tuple-element.22), channel_id=1, source_target_pairs={{0,1},{1,2},{2,3},{4,5},{5,6},{6,7},{8,9},{9,10},{10,11},{12,13},{... | collective-permute-start | bytes 147464 | tf_op jit(solution)/shard_map/ppermute | solution.py:386
  38.0 4.8 %copy-start.6 = (f32[2,4096]{1,0:T(2,128)S(1)}, f32[2,4096]{1,0:T(2,128)}, u32[]{:S(2)}) copy-start(f32[2,4096]{1,0:T(2,128)} %precision.1) | copy-start | bytes 98308
  38.0 4.8 %collective-permute-start.3 = (f32[48,256]{1,0:T(8,128)S(1)}, f32[48,256]{1,0:T(8,128)S(1)}, u32[]{:S(2)}, u32[]{:S(2)}) collective-permute-start(f32[48,256]{1,0:T(8,128)S(1)} %get-tuple-element.23), channel_id=1, source_target_pairs={{1,0},{2,1},{3,2},{5,4},{6,5},{7,6},{9,8},{10,9},{11,10},{13,12},{... | collective-permute-start | bytes 147464 | tf_op jit(solution)/shard_map/ppermute | solution.py:386
  51.2 12.1 %collective-permute-start.4 = (f32[18,512]{1,0:T(8,128)S(1)}, f32[18,512]{1,0:T(8,128)S(1)}, u32[]{:S(2)}, u32[]{:S(2)}) collective-permute-start(f32[18,512]{1,0:T(8,128)S(1)} %get-tuple-element.26), channel_id=1, source_target_pairs={{0,4},{4,8},{8,12},{12,16},{16,20},{20,24},{24,28},{28,32},{32,36}... | collective-permute-start | bytes 110600 | tf_op jit(solution)/shard_map/ppermute | solution.py:381
  53.2 10.2 %collective-permute-start.5 = (f32[12,512]{1,0:T(8,128)S(1)}, f32[12,512]{1,0:T(8,128)S(1)}, u32[]{:S(2)}, u32[]{:S(2)}) collective-permute-start(f32[12,512]{1,0:T(8,128)S(1)} %get-tuple-element.27), channel_id=1, source_target_pairs={{0,508},{4,0},{8,4},{12,8},{16,12},{20,16},{24,20},{28,24},{32,28}... | collective-permute-start | bytes 73736 | tf_op jit(solution)/shard_map/ppermute | solution.py:381
  63.4 97.3 %copy-start.4 = (s32[32,256]{1,0:T(8,128)S(1)}, s32[32,256]{1,0:T(8,128)}, u32[]{:S(2)}) copy-start(s32[32,256]{1,0:T(8,128)} %depth.5) | copy-start | bytes 98308
  63.5 4.4 %collective-permute-start.6 = (f32[32,128]{1,0:T(8,128)S(1)}, f32[32,128]{1,0:T(8,128)S(1)}, u32[]{:S(2)}, u32[]{:S(2)}) collective-permute-start(f32[32,128]{1,0:T(8,128)S(1)} %get-tuple-element.29), channel_id=1, source_target_pairs={{0,1},{1,2},{2,3},{4,5},{5,6},{6,7},{8,9},{9,10},{10,11},{12,13},{... | collective-permute-start | bytes 49160 | tf_op jit(solution)/shard_map/ppermute | solution.py:386
  66.6 4.9 %collective-permute-start.7 = (f32[32,128]{1,0:T(8,128)S(1)}, f32[32,128]{1,0:T(8,128)S(1)}, u32[]{:S(2)}, u32[]{:S(2)}) collective-permute-start(f32[32,128]{1,0:T(8,128)S(1)} %get-tuple-element.30), channel_id=1, source_target_pairs={{1,0},{2,1},{3,2},{5,4},{6,5},{7,6},{9,8},{10,9},{11,10},{13,12},{... | collective-permute-start | bytes 49160 | tf_op jit(solution)/shard_map/ppermute | solution.py:386
  160.6 1.2 copy-start.2
Sparse Core Ops, SparseCore 0:
  51.4 109.2 all-gather.2

commit v2 on v1

--- a/solution.py
+++ b/solution.py
@@ -19,9 +19,11 @@
 PLANES = 2 * DEPTH + 2
 LOW, HIGH = 2, 3
 X0, Y0 = 8, 128
+CORES = 2
+RING = 8
 GROUP = 32
 F32, BF16 = jnp.float32, jnp.bfloat16
-VMEM = pltpu.CompilerParams(vmem_limit_bytes=48 * 1024 * 1024)
+MIB = 1024 * 1024
 
 
 def iota(shape, dim):
@@ -43,6 +45,27 @@
 
 def roll(value, shift, axis):
     return pltpu.roll(value, shift % value.shape[axis], axis)
+
+
+def parity():
+    return lax.axis_index("lon") % CORES
+
+
+def pick(first, second):
+    even = parity() == 0
+    inner, outer = first[...], second[...]
+    return jnp.where(even, outer, inner), jnp.where(even, inner, outer)
+
+
+def address(east, west, first, second):
+    even = parity() == 0
+    first[...] = jnp.where(even, east[...], west[...])
+    second[...] = jnp.where(even, west[...], east[...])
+
+
+def interpolation(offset, refine):
+    low = lax.shift_right_arithmetic(offset, refine.bit_length() - 1)
+    return low, ((offset - low * refine).astype(F32) + 0.5) / refine
 
 
 def period_weights(steps_total, periods):
@@ -53,7 +76,7 @@
     return table
 
 
-def pack_kernel(move, cell, weight, obs, prec, init, depth, mixing, fields, east, west, south, north):
+def pack_kernel(move, cell, weight, obs, prec, init, depth, mixing, fields, inner, outer, south, north, east, west):
     count = move.shape[1]
     for step in range(STEPS):
         base = step * FIELDS
@@ -107,6 +130,7 @@
     for step in range(STEPS):
         row = step * FIELDS + 6
         fields[row : row + 1, :] = jnp.where(move[step : step + 1, :] == 4, prec[step : step + 1, :], 0.0)
+    address(east, west, inner, outer)
 
 
 def extend_lon(ext, p, own, from_west, from_east, rows, cells_lat):
@@ -118,7 +142,8 @@
     ext[p, X0 + rows : X0 + rows + HIGH, lanes] = from_east[at : at + HIGH, :]
 
 
-def merge_kernel(init, depth, mixing, to_south, to_north, from_west, from_east, ext, south, north):
+def merge_kernel(init, depth, mixing, to_south, to_north, inner, outer, ext, south, north):
+    from_west, from_east = pick(inner, outer)
     rows, cells_lat = depth.shape
     ext[...] = jnp.zeros_like(ext)
     for p in range(PLANES):
@@ -165,14 +190,15 @@
 
 
 def main_kernel(
-    levels, refine, lon_count, lat_count, controls, fields, precision, from_west, from_east, from_south, from_north,
-    padded, partial, share, to_west, to_east, ext, spot,
+    levels, refine, lon_count, lat_count, controls, fields, precision, inner, outer, from_south, from_north,
+    padded, partial, share, to_inner, to_outer, ext, spot, to_west, to_east,
 ):
+    from_west, from_east = pick(inner, outer)
     rows, cells_lat = partial.shape[1] - 16, partial.shape[2] - 256
     tall, wide = ext.shape[1:]
     lon_index, lat_index = lax.axis_index("lon"), lax.axis_index("lat")
     grid_lat = cells_lat * lat_count
-    periods, _, ctrl_lon, ctrl_lat = controls.shape
+    periods, _, ctrl_lat, ctrl_lon = controls.shape
     table = period_weights(STEPS, periods)
     lane = iota((tall, 128), 1)
     half = tall // 2
@@ -188,14 +214,12 @@
     row_ids = iota((1, wide), 1) - Y0 + lat_index * cells_lat
     rotation = ROTATION * jnp.sin((row_ids.astype(F32) + 0.5) * (math.pi / grid_lat) - 0.5 * math.pi)
     offset = iota((tall, ctrl_lon), 0) - X0 + lon_index * rows - refine // 2
-    low = lax.shift_right_arithmetic(offset, refine.bit_length() - 1)
-    part = ((offset - low * refine).astype(F32) + 0.5) / refine
+    low, part = interpolation(offset, refine)
     column = iota((tall, ctrl_lon), 1)
     wrapped, after = (low + ctrl_lon) % ctrl_lon, (low + 1 + ctrl_lon) % ctrl_lon
     lon_interp = jnp.where(column == wrapped, 1.0 - part, 0.0) + jnp.where(column == after, part, 0.0)
     offset = iota((ctrl_lat, wide), 1) - Y0 + lat_index * cells_lat - refine // 2
-    low = lax.shift_right_arithmetic(offset, refine.bit_length() - 1)
-    part = ((offset - low * refine).astype(F32) + 0.5) / refine
+    low, part = interpolation(offset, refine)
     column = iota((ctrl_lat, wide), 0)
     lat_interp = jnp.where(column == low, 1.0 - part, 0.0) + jnp.where(column == low + 1, part, 0.0)
     lon_interp, lat_interp = lon_interp.astype(BF16), lat_interp.astype(BF16)
@@ -207,7 +231,7 @@
             for period in range(1, periods):
                 blended = blended + table[step][period] * controls[period, c]
             high, low = split(blended)
-            high, low = split(dot(lon_interp, high) + dot(lon_interp, low))
+            high, low = split(dot_lanes(lon_interp, high) + dot_lanes(lon_interp, low))
             forcing[step].append(dot(high, lat_interp) + dot(low, lat_interp))
     state = [[wet[k] * full[c * DEPTH + k] for k in range(DEPTH)] for c in range(2)]
     surfaces = []
@@ -290,28 +314,60 @@
             partial[p] = adjoint[c][k]
             to_west[LOW * p : LOW * (p + 1), :] = ext[p, X0 - LOW : X0, :]
             to_east[HIGH * p : HIGH * (p + 1), :] = ext[p, X0 + rows : X0 + rows + HIGH, :]
-    offset = iota((wide, 128), 0) - Y0 - refine // 2
-    low = lax.shift_right_arithmetic(offset, refine.bit_length() - 1)
-    part = ((offset - low * refine).astype(F32) + 0.5) / refine
-    column = iota((wide, 128), 1) % GROUP - 1
+    address(to_east, to_west, to_inner, to_outer)
+    low, part = interpolation(iota((wide, 4 * GROUP), 0) - Y0 - refine // 2, refine)
+    column = iota((wide, 4 * GROUP), 1) % GROUP - 1
     onto_lat = jnp.where(column == low, 1.0 - part, 0.0) + jnp.where(column == low + 1, part, 0.0)
     onto_lat = onto_lat.astype(BF16)
-    offset = iota((tall, 128), 0) - X0 - refine // 2
-    low = lax.shift_right_arithmetic(offset, refine.bit_length() - 1)
-    part = ((offset - low * refine).astype(F32) + 0.5) / refine
-    column = iota((tall, 128), 1) // GROUP - 1
+    low, part = interpolation(iota((tall, 4 * GROUP), 0) - X0 - refine // 2, refine)
+    column = iota((tall, 4 * GROUP), 1) // GROUP - 1
     onto_lon = jnp.where(column == low, 1.0 - part, 0.0) + jnp.where(column == low + 1, part, 0.0)
+    weight = jnp.sum(jnp.sum(precision[...], axis=0, keepdims=True), axis=1, keepdims=True)
+    parts = []
     for step in range(STEPS):
         for c in range(2):
-            high, low = split(nudges[step][c])
-            across = dot(high, onto_lat) + dot(low, onto_lat)
-            row = 2 * step + c
-            share[row : row + 1, :] = jnp.sum(onto_lon * across, axis=0, keepdims=True)
-    weight = jnp.sum(jnp.sum(precision[...], axis=0, keepdims=True), axis=1, keepdims=True)
-    share[0:1, :] = jnp.where(iota((1, 128), 1) == GROUP - 1, weight, share[0:1, :])
-
-
-def join_kernel(partial, from_west, from_east, own, south, north):
+            high, rest = split(nudges[step][c])
+            across = dot(high, onto_lat) + dot(rest, onto_lat)
+            parts.append(jnp.sum(onto_lon * across, axis=0, keepdims=True))
+    parts[0] = jnp.where(iota((1, 4 * GROUP), 1) == 4 * GROUP - 1, weight, parts[0])
+    share[...] = jnp.broadcast_to(jnp.concatenate(parts, axis=0)[None], share.shape)
+
+
+def plane_kernel(lat_count, per, shares, out, rows, total):
+    members = shares.shape[0]
+    ring = members // (CORES * lat_count)
+    ctrl_lat = per * lat_count
+    for m in range(members):
+        rows[4 * m : 4 * m + 4, :] = shares[m]
+    total[...] = jnp.zeros_like(total)
+    lane = iota((ring, 4 * GROUP), 1)
+    height = total.shape[0] // STEPS
+    weight = jnp.zeros((ring, 4 * GROUP), F32)
+    for core in range(CORES):
+        for step in range(STEPS):
+            sums = [jnp.zeros((ring, 4 * GROUP), F32) for _ in range(4)]
+            for band in range(lat_count):
+                for c in range(2):
+                    at = 4 * (core * lat_count + band) + 2 * step + c
+                    held = rows[pl.ds(at, ring, stride=4 * CORES * lat_count), :]
+                    if step == 0 and c == 0:
+                        weight = weight + held
+                    start = c * ctrl_lat + per * band - 1
+                    first, last = max(start, c * ctrl_lat), min(start + per + 1, (c + 1) * ctrl_lat - 1)
+                    mine = (lane >= first) & (lane <= last)
+                    for a in range(4):
+                        sums[a] = sums[a] + jnp.where(mine, roll(held, start - GROUP * a, 1), 0.0)
+            for a in range(4):
+                at = step * height + 2 * core + a
+                total[pl.ds(at, ring, stride=4), :] = total[pl.ds(at, ring, stride=4), :] + sums[a]
+    weight = jnp.sum(jnp.where(lane == 4 * GROUP - 1, weight, 0.0), axis=0, keepdims=True)
+    weight = jnp.sum(weight, axis=1, keepdims=True)
+    total[4 * ring + 2 : 4 * ring + 3, :] = jnp.broadcast_to(weight, (1, 4 * GROUP))
+    out[...] = jnp.broadcast_to(total[...][None], out.shape)
+
+
+def join_kernel(partial, inner, outer, own, south, north):
+    from_west, from_east = pick(inner, outer)
     rows, cells_lat = own.shape[1:]
     lane = iota((rows, 128), 1)
     first = jnp.zeros((rows, 128), F32)
@@ -329,16 +385,16 @@
     north[...] = last
 
 
-def finish_kernel(normalizer, lat_count, own, depth, from_south, from_north, shares, grad, out):
+def finish_kernel(normalizer, own, depth, from_south, from_north, shares, grad, out, full):
     levels, rows, cells_lat = grad.shape[1:]
-    periods = out.shape[0]
+    periods, _, ctrl_lat, ctrl_lon = out.shape
     table = period_weights(STEPS, periods)
-    lon_count = out.shape[2] // 2
-    per = out.shape[3] // lat_count
-    lane = iota(shares.shape, 1)
-    row = iota(shares.shape, 0)
-    held = jnp.where((lane == GROUP - 1) & (row % (2 * STEPS) == 0), shares[...], 0.0)
-    scale = normalizer / jnp.sum(jnp.sum(held, axis=0, keepdims=True), axis=1, keepdims=True)
+    members, size = shares.shape[:2]
+    span = ctrl_lon // members
+    total = shares[0, span + 2 : span + 3, :]
+    for m in range(1, members):
+        total = total + shares[m, span + 2 : span + 3, :]
+    scale = normalizer / total[:, 0:1]
     side = iota((rows, 128), 1)
     wet_levels = depth[...]
     for c in range(2):
@@ -351,34 +407,43 @@
             high = jnp.where(side >= 128 - LOW, roll(from_north[...], LOW * p, 1), 0.0)
             value = own[p] + jnp.concatenate([low, high], axis=1)
             grad[c, k] = jnp.where(wet_levels > k, value * scale, 0.0)
-    source = iota((128, 384), 0)
-    target = iota((128, 384), 1)
-    a, b = source // GROUP, source % GROUP
-    kind, i, column = target // 128, target % 128 // 64, target % 64
-    right_row = ((kind == 0) & (a == i + 1)) | ((kind == 1) & (a == 3) & (i == 0)) | ((kind == 2) & (a == 0) & (i == 1))
-    right_row = right_row & (b < per + 2)
-    gathered = [jnp.zeros((lon_count, 384), F32) for _ in range(2 * STEPS)]
-    for m in range(lat_count):
-        pick = (right_row & (column == per * m - 1 + b)).astype(F32).astype(BF16)
-        for t in range(2 * STEPS):
-            high, low = split(shares[pl.ds(m * 2 * STEPS + t, lon_count, stride=lat_count * 2 * STEPS), :])
-            gathered[t] = gathered[t] + dot(high, pick) + dot(low, pick)
-    scaled = []
-    for t in range(2 * STEPS):
-        part = gathered[t]
-        scaled.append(scale * (part[:, :128] + roll(part[:, 128:256], 1, 0) + roll(part[:, 256:], -1, 0)))
+    for step in range(STEPS):
+        at = step * size // STEPS
+        for m in range(members):
+            full[step, m * span : (m + 1) * span, :] = shares[m, at + 1 : at + 1 + span, :]
+        for m in range(members):
+            before, after = (m * span + ctrl_lon - 1) % ctrl_lon, (m + 1) * span % ctrl_lon
+            full[step, before : before + 1, :] += shares[m, at : at + 1, :]
+            full[step, after : after + 1, :] += shares[m, at + span + 1 : at + span + 2, :]
+    scaled = [scale * full[step] for step in range(STEPS)]
     for period in range(periods):
+        value = table[0][period] * scaled[0]
+        for step in range(1, STEPS):
+            value = value + table[step][period] * scaled[step]
+        value = value.T
         for c in range(2):
-            value = table[0][period] * scaled[c]
-            for step in range(1, STEPS):
-                value = value + table[step][period] * scaled[2 * step + c]
-            for i in range(2):
-                out[period, c, pl.ds(i, lon_count, stride=2), :] = value[:, 64 * i : 64 * i + 64]
-
-
-def around(value, distance):
+            out[period, c] = value[c * ctrl_lat : (c + 1) * ctrl_lat]
+
+
+def swap(inner, outer):
     count = lax.axis_size("lon")
-    return lax.ppermute(value, "lon", [(i, (i + distance) % count) for i in range(count)])
+    inner = lax.ppermute(inner, "lon", [(i, i ^ 1) for i in range(count)])
+    outer = lax.ppermute(outer, "lon", [((i + 1) % count, ((i ^ 1) + 1) % count) for i in range(count)])
+    return inner, outer
+
+
+def gather(copies, chips, stride, whole_chips):
+    if copies.shape[0] == 1:
+        return copies
+    count = lax.axis_size("lat")
+    per_chip = CORES * count
+    inside = [range(per_chip)] if whole_chips else [(i,) for i in range(per_chip)]
+    groups = []
+    for base in range(lax.axis_size("lon") // CORES):
+        if base // stride % chips == 0:
+            for few in inside:
+                groups.append([(base + chip * stride) * per_chip + i for chip in range(chips) for i in few])
+    return lax.all_to_all(copies, ("lon", "lat"), 0, 0, axis_index_groups=groups, tiled=True)
 
 
 def along(value, distance):
@@ -390,7 +455,7 @@
     return pl.BlockSpec(shape, lambda i: (0,) * len(shape))
 
 
-def call(kernel, ins, outs, blocks=None, scratch=(), **kwargs):
+def call(kernel, ins, outs, blocks=None, scratch=(), vmem=16):
     blocks = blocks or {}
     return pl.pallas_call(
         kernel,
@@ -399,8 +464,7 @@
         in_specs=[whole(blocks.get(i, value.shape)) for i, value in enumerate(ins)],
         out_specs=[whole(shape) for shape in outs],
         scratch_shapes=[pltpu.VMEM(shape, F32) for shape in scratch],
-        compiler_params=VMEM,
-        **kwargs,
+        compiler_params=pltpu.CompilerParams(vmem_limit_bytes=vmem * MIB),
     )(*ins)
 
 
@@ -414,42 +478,56 @@
     refine = rows * lon_count // ctrl_lon
     tall, wide = rows + 16, cells_lat + 256
     surface = (2, DEPTH, rows, cells_lat)
-    lon_low, lon_high = (3 * FIELDS + LOW * PLANES, 256), (3 * FIELDS + HIGH * PLANES, 256)
-    fields, east, west, south, north = call(
+    lon_message = (3 * FIELDS + HIGH * PLANES, 256)
+    fields, inner, outer, south, north = call(
         pack_kernel,
         (drift_move, drift_cell, drift_weight, drift_obs, drift_precision, initial, depth_levels, mixing),
-        ((STEPS * FIELDS, count), lon_low, lon_high, (FIELDS, 256), (FIELDS, 256)),
+        ((STEPS * FIELDS, count), lon_message, lon_message, (FIELDS, 256), (FIELDS, 256)),
         {5: surface},
-    )
-    from_west, from_east = around(east, 1), around(west, -1)
+        scratch=(lon_message, lon_message),
+        vmem=60,
+    )
+    inner, outer = swap(inner, outer)
     message = (3 * FIELDS + tall // 2, 256)
     padded, south, north = call(
         merge_kernel,
-        (initial, depth_levels, mixing, south, north, from_west, from_east),
+        (initial, depth_levels, mixing, south, north, inner, outer),
         ((PLANES, tall, wide), message, message),
         {0: surface},
     )
     from_south, from_north = along(north, 1), along(south, -1)
-    partial, share, to_west, to_east = call(
+    edge = (2 * DEPTH * HIGH, wide)
+    ring = min(RING, lon_count // CORES)
+    members = lon_count // (CORES * ring)
+    partial, share, inner, outer = call(
         functools.partial(main_kernel, levels, refine, lon_count, lat_count),
-        (controls, fields, drift_precision, from_west, from_east, from_south, from_north, padded),
-        ((2 * DEPTH, tall, wide), (2 * STEPS, 128), (2 * DEPTH * LOW, wide), (2 * DEPTH * HIGH, wide)),
-        scratch=((2 * DEPTH, tall, wide), (2, tall, wide)),
-    )
-    shares = lax.all_gather(share, ("lon", "lat"), axis=0, tiled=True)
-    from_west, from_east = around(to_east, 1), around(to_west, -1)
+        (jnp.swapaxes(controls, 2, 3), fields, drift_precision, inner, outer, from_south, from_north, padded),
+        ((2 * DEPTH, tall, wide), (ring * CORES * lat_count, 2 * STEPS, 4 * GROUP), edge, edge),
+        scratch=((2 * DEPTH, tall, wide), (2, tall, wide), edge, edge),
+    )
+    shares = gather(share, ring, 1, True)
+    height = -(-(4 * ring + 3) // 8) * 8
+    (share,) = call(
+        functools.partial(plane_kernel, lat_count, ctrl_lat // lat_count),
+        (shares,),
+        ((members, STEPS * height, 2 * ctrl_lat),),
+        scratch=((4 * ring * CORES * lat_count, 4 * GROUP), (STEPS * height, 2 * ctrl_lat)),
+    )
+    shares = gather(share, members, ring, False)
+    inner, outer = swap(inner, outer)
     own, to_south, to_north = call(
         join_kernel,
-        (partial, from_west, from_east),
+        (partial, inner, outer),
         ((2 * DEPTH, rows, cells_lat), (rows, 128), (rows, 128)),
     )
     from_south, from_north = along(to_north, 1), along(to_south, -1)
     grad_initial, grad_controls = call(
-        functools.partial(finish_kernel, float(STEPS * count * lon_count * lat_count), lat_count),
+        functools.partial(finish_kernel, float(STEPS * count * lon_count * lat_count)),
         (own, depth_levels, from_south, from_north, shares),
-        (initial.shape, controls.shape),
-    )
-    return grad_initial, grad_controls
+        (initial.shape, (periods, 2, ctrl_lat, ctrl_lon)),
+        scratch=((STEPS, ctrl_lon, 2 * ctrl_lat),),
+    )
+    return grad_initial, jnp.swapaxes(grad_controls, 2, 3)
 
 
 def solution(mesh):

time: 173 us -> 86.7 us (0.50)
  the two profiles are of different devices: /device:TPU:1 before, /device:TPU:2 now
where the time goes in v2:
time: 86.7 us; the launch traced here: 86.1 us
  starting transfers between devices  40.2 us (46%)
  blocking collectives  15.2 us (18%)
  Pallas kernels  15.1 us (17%)
  waiting for transfers between devices  12.4 us (14%)
  local copies, waits for them, and re-layouts  2.36 us (3%)
    ppermute x2, starting transfers between devices, swap(): lax.ppermute(outer, 'lon', [((i + 1) % count, ((i ^ 1) + 1) % count) for...  18.2 us
    all_to_all x1, blocking collectives, gather(): lax.all_to_all(copies, ('lon', 'lat'), 0, 0, axis_index_groups=groups, ti...  15.2 us
    pallas_call x6, Pallas kernels, call(): pl.pallas_call(kernel, grid=(1,), out_shape=[jax.ShapeDtypeStruct(shape,...  15.1 us
    ppermute x4, starting transfers between devices, along(): lax.ppermute(value, 'lat', [(i, i + distance) for i in range(max(0, -dist...  11.7 us
    ppermute x2, waiting for transfers between devices, swap(): lax.ppermute(outer, 'lon', [((i + 1) % count, ((i ^ 1) + 1) % count) for...  6.5 us
    all_to_all x1, starting transfers between devices, gather(): lax.all_to_all(copies, ('lon', 'lat'), 0, 0, axis_index_groups=groups, ti...  6.4 us
    ppermute x4, waiting for transfers between devices, along(): lax.ppermute(value, 'lat', [(i, i + distance) for i in range(max(0, -dist...  5.91 us
    ppermute x2, starting transfers between devices, swap(): inner = lax.ppermute(inner, 'lon', [(i, i ^ 1) for i in range(count)])  3.95 us
  transfers between devices with their start and end apart: 9, of which 5 were waited for; matrix products, arithmetic and copies ran while one was open for 0% of the time, Pallas kernels for 0%

profile of v2, /device:TPU:2, one launch (start us, length us, event | category | flops | bytes accessed | tf_op | source)
XLA Modules:
  0.0 86.1 jit_solution(5237865306838021763)
XLA Ops:
  0.6 0.0 copy-start.2
  0.6 0.0 copy-start.5
  0.7 0.0 copy-start
  0.7 5.0 %shard_map.104 = (f32[16,4096]{1,0:T(8,128)}, f32[48,256]{1,0:T(8,128)}, f32[48,256]{1,0:T(8,128)}, f32[8,256]{1,0:T(8,128)}, f32[8,256]{1,0:T(8,128)}) custom-call(s32[2,4096]{1,0:T(2,128)} %move.1, s32[2,4096]{1,0:T(2,128)} %cell.1, f32[4,2,4096]{2,1,0:T(2,128)} %weight.1, f32[2,2,4096]{2,1,0:T(2,128)} %obs.1, f32[2,4096]{1,0:T(2,128)} %precision.1, ...), custom_call_target="tpu_custom_call" | custom-call | tf_op jit(solution)/shard_map/pallas_call | solution.py:460
  5.7 2.0 %collective-permute-start = (f32[48,256]{1,0:T(8,128)}, f32[48,256]{1,0:T(8,128)S(1)}, u32[]{:S(2)}, u32[]{:S(2)}) collective-permute-start(f32[48,256]{1,0:T(8,128)} %get-tuple-element.20), channel_id=1, source_target_pairs={{0,4},{4,0},{8,12},{12,8},{16,20},{20,16},{24,28},{28,24},{32,36},... | collective-permute-start | bytes 147464 | tf_op jit(solution)/shard_map/ppermute | solution.py:430
  7.7 14.0 %collective-permute-start.1 = (f32[48,256]{1,0:T(8,128)}, f32[48,256]{1,0:T(8,128)S(1)}, u32[]{:S(2)}, u32[]{:S(2)}) collective-permute-start(f32[48,256]{1,0:T(8,128)} %get-tuple-element.21), channel_id=1, source_target_pairs={{4,8},{8,4},{12,16},{16,12},{20,24},{24,20},{28,32},{32,28},{36,40... | collective-permute-start | bytes 147464 | tf_op jit(solution)/shard_map/ppermute | solution.py:431
  21.7 0.0 collective-permute-done.inner
  21.7 2.0 %collective-permute-done.1.outer = f32[48,256]{1,0:T(8,128)S(1)} collective-permute-done((f32[48,256]{1,0:T(8,128)}, f32[48,256]{1,0:T(8,128)S(1)}, u32[]{:S(2)}, u32[]{:S(2)}) %collective-permute-start.1) | collective-permute-done | bytes 49184 | tf_op jit(solution)/shard_map/ppermute | solution.py:431
  23.8 0.7 copy-done.6
  24.5 0.7 copy-done.7
  25.2 0.2 shard_map.105
  25.4 3.4 %collective-permute-start.2 = (f32[48,256]{1,0:T(8,128)S(1)}, f32[48,256]{1,0:T(8,128)S(1)}, u32[]{:S(2)}, u32[]{:S(2)}) collective-permute-start(f32[48,256]{1,0:T(8,128)S(1)} %get-tuple-element.24), channel_id=1, source_target_pairs={{0,1},{1,2},{2,3},{4,5},{5,6},{6,7},{8,9},{9,10},{10,11},{12,13},{... | collective-permute-start | bytes 147464 | tf_op jit(solution)/shard_map/ppermute | solution.py:451
  28.8 2.4 %collective-permute-start.3 = (f32[48,256]{1,0:T(8,128)S(1)}, f32[48,256]{1,0:T(8,128)S(1)}, u32[]{:S(2)}, u32[]{:S(2)}) collective-permute-start(f32[48,256]{1,0:T(8,128)S(1)} %get-tuple-element.25), channel_id=1, source_target_pairs={{1,0},{2,1},{3,2},{5,4},{6,5},{7,6},{9,8},{10,9},{11,10},{13,12},{... | collective-permute-start | bytes 147464 | tf_op jit(solution)/shard_map/ppermute | solution.py:451
  31.2 0.1 collective-permute-done.2.from_south
  31.3 3.4 %collective-permute-done.3.from_north = f32[48,256]{1,0:T(8,128)S(1)} collective-permute-done((f32[48,256]{1,0:T(8,128)S(1)}, f32[48,256]{1,0:T(8,128)S(1)}, u32[]{:S(2)}, u32[]{:S(2)}) %collective-permute-start.3) | collective-permute-done | bytes 49184 | tf_op jit(solution)/shard_map/ppermute | solution.py:451
  34.8 0.0 copy-done.4
  34.8 0.9 %copy-done.3 = f32[16,4096]{1,0:T(8,128)S(1)} copy-done((f32[16,4096]{1,0:T(8,128)S(1)}, f32[16,4096]{1,0:T(8,128)}, u32[]{:S(2)}) %copy-start.3) | copy-done | bytes 262168
  35.7 7.6 %shard_map.106 = (f32[6,48,512]{2,1,0:T(8,128)S(1)}, f32[64,4,128]{2,1,0:T(4,128)S(1)}, f32[18,512]{1,0:T(8,128)S(1)}, f32[18,512]{1,0:T(8,128)S(1)}) custom-call(f32[4,2,64,256]{3,2,1,0:T(8,128)S(1)} %bitcast.2, f32[16,4096]{1,0:T(8,128)S(1)} %copy-done.3, f32[2,4096]{1,0:T(2,128)S(1)} %copy-done.4, f32[48,256]{1,0:T(8,128)S(1)} %collective-permute-done.inner, ...), custom_call_target="tpu_custom_call" | custom-call | tf_op jit(solution)/shard_map/pallas_call | solution.py:460
  43.3 15.2 %all_to_all.10.shares = f32[64,4,128]{2,1,0:T(4,128)S(1)} all-to-all(f32[64,4,128]{2,1,0:T(4,128)S(1)} %get-tuple-element.33), channel_id=1, replica_groups={{0,1,2,3,4,5,6,7,8,9,10,11,12,13,14,15,16,17,18,19,20,21,22,23,24,25,26..., dimensions={0} | all-to-all | bytes 262144 | tf_op jit(solution)/shard_map/all_to_all | solution.py:446
  58.5 1.0 %shard_map.108 = f32[8,80,128]{2,1,0:T(8,128)} custom-call(f32[64,4,128]{2,1,0:T(4,128)S(1)} %all_to_all.10.shares), custom_call_target="tpu_custom_call" | custom-call | tf_op jit(solution)/shard_map/pallas_call | solution.py:460
  59.5 6.4 %all-to-all-start.1 = ((f32[8,80,128]{2,1,0:T(8,128)}), f32[8,80,128]{2,1,0:T(8,128)S(1)}, u32[]{:S(2)}, u32[]{:S(2)}) async-start(f32[8,80,128]{2,1,0:T(8,128)} %shard_map.108), calls=%async_computation.1 | async-start | bytes 655360 | tf_op jit(solution)/shard_map/all_to_all | solution.py:446
  65.9 1.9 %collective-permute-start.4 = (f32[18,512]{1,0:T(8,128)S(1)}, f32[18,512]{1,0:T(8,128)S(1)}, u32[]{:S(2)}, u32[]{:S(2)}) collective-permute-start(f32[18,512]{1,0:T(8,128)S(1)} %get-tuple-element.28), channel_id=1, source_target_pairs={{0,4},{4,0},{8,12},{12,8},{16,20},{20,16},{24,28},{28,24},{32,36},... | collective-permute-start | bytes 110600 | tf_op jit(solution)/shard_map/ppermute | solution.py:430
  67.8 4.2 %collective-permute-start.5 = (f32[18,512]{1,0:T(8,128)S(1)}, f32[18,512]{1,0:T(8,128)S(1)}, u32[]{:S(2)}, u32[]{:S(2)}) collective-permute-start(f32[18,512]{1,0:T(8,128)S(1)} %get-tuple-element.29), channel_id=1, source_target_pairs={{4,8},{8,4},{12,16},{16,12},{20,24},{24,20},{28,32},{32,28},{36,40... | collective-permute-start | bytes 110600 | tf_op jit(solution)/shard_map/ppermute | solution.py:431
  72.0 0.0 collective-permute-done.4.inner
  72.1 4.5 %collective-permute-done.5.outer = f32[18,512]{1,0:T(8,128)S(1)} collective-permute-done((f32[18,512]{1,0:T(8,128)S(1)}, f32[18,512]{1,0:T(8,128)S(1)}, u32[]{:S(2)}, u32[]{:S(2)}) %collective-permute-start.5) | collective-permute-done | bytes 36896 | tf_op jit(solution)/shard_map/ppermute | solution.py:431
  76.5 0.1 shard_map.107
  76.7 2.6 %collective-permute-start.6 = (f32[32,128]{1,0:T(8,128)S(1)}, f32[32,128]{1,0:T(8,128)S(1)}, u32[]{:S(2)}, u32[]{:S(2)}) collective-permute-start(f32[32,128]{1,0:T(8,128)S(1)} %get-tuple-element.31), channel_id=1, source_target_pairs={{0,1},{1,2},{2,3},{4,5},{5,6},{6,7},{8,9},{9,10},{10,11},{12,13},{... | collective-permute-start | bytes 49160 | tf_op jit(solution)/shard_map/ppermute | solution.py:451
  79.3 3.2 %collective-permute-start.7 = (f32[32,128]{1,0:T(8,128)S(1)}, f32[32,128]{1,0:T(8,128)S(1)}, u32[]{:S(2)}, u32[]{:S(2)}) collective-permute-start(f32[32,128]{1,0:T(8,128)S(1)} %get-tuple-element.32), channel_id=1, source_target_pairs={{1,0},{2,1},{3,2},{5,4},{6,5},{7,6},{9,8},{10,9},{11,10},{13,12},{... | collective-permute-start | bytes 49160 | tf_op jit(solution)/shard_map/ppermute | solution.py:451
  82.5 0.0 collective-permute-done.6.from_south
  82.5 2.4 %collective-permute-done.7.from_north = f32[32,128]{1,0:T(8,128)S(1)} collective-permute-done((f32[32,128]{1,0:T(8,128)S(1)}, f32[32,128]{1,0:T(8,128)S(1)}, u32[]{:S(2)}, u32[]{:S(2)}) %collective-permute-start.7) | collective-permute-done | bytes 16416 | tf_op jit(solution)/shard_map/ppermute | solution.py:451
  84.9 0.0 all-to-all-done.1.shares
  84.9 1.2 %shard_map.109 = (f32[2,8,32,256]{3,2,1,0:T(8,128)}, f32[4,2,64,256]{3,2,1,0:T(8,128)}) custom-call(f32[6,32,256]{2,1,0:T(8,128)S(1)} %get-tuple-element.30.own, s32[32,256]{1,0:T(8,128)S(1)} %copy-done.2, f32[32,128]{1,0:T(8,128)S(1)} %collective-permute-done.6.from_south, f32[32,128]{1,0:T(8,128)S(1)} %collective-permute-done.7.from_north, ...), custom_call_target="tpu_custom_call" | custom-call | tf_op jit(solution)/shard_map/pallas_call | solution.py:460
  (9 shorter events, 0.0 us)
Async XLA Ops:
  0.6 23.1 %copy-start.2 = (s32[32,256]{1,0:T(8,128)S(1)}, s32[32,256]{1,0:T(8,128)}, u32[]{:S(2)}) copy-start(s32[32,256]{1,0:T(8,128)} %depth.5) | copy-start | bytes 98308
  0.6 23.1 %copy-start.5 = (f32[32,256]{1,0:T(8,128)S(1)}, f32[32,256]{1,0:T(8,128)}, u32[]{:S(2)}) copy-start(f32[32,256]{1,0:T(8,128)} %mixing.3) | copy-start | bytes 98308
  0.7 23.1 %copy-start = (f32[2,8,32,256]{3,2,1,0:T(8,128)S(1)}, f32[2,8,32,256]{3,2,1,0:T(8,128)}, u32[]{:S(2)}) copy-start(f32[2,8,32,256]{3,2,1,0:T(8,128)} %init.3) | copy-start | bytes 1572868
  5.7 29.1 %copy-start.1 = (f32[4,2,256,64]{2,3,1,0:T(8,128)S(1)}, f32[4,2,256,64]{2,3,1,0:T(8,128)}, u32[]{:S(2)}) copy-start(f32[4,2,256,64]{2,3,1,0:T(8,128)} %param.12) | copy-start | bytes 1572868
  5.7 16.0 %collective-permute-start = (f32[48,256]{1,0:T(8,128)}, f32[48,256]{1,0:T(8,128)S(1)}, u32[]{:S(2)}, u32[]{:S(2)}) collective-permute-start(f32[48,256]{1,0:T(8,128)} %get-tuple-element.20), channel_id=1, source_target_pairs={{0,4},{4,0},{8,12},{12,8},{16,20},{20,16},{24,28},{28,24},{32,36},... | collective-permute-start | bytes 147464 | tf_op jit(solution)/shard_map/ppermute | solution.py:430
  7.7 16.0 %collective-permute-start.1 = (f32[48,256]{1,0:T(8,128)}, f32[48,256]{1,0:T(8,128)S(1)}, u32[]{:S(2)}, u32[]{:S(2)}) collective-permute-start(f32[48,256]{1,0:T(8,128)} %get-tuple-element.21), channel_id=1, source_target_pairs={{4,8},{8,4},{12,16},{16,12},{20,24},{24,20},{28,32},{32,28},{36,40... | collective-permute-start | bytes 147464 | tf_op jit(solution)/shard_map/ppermute | solution.py:431
  23.8 0.7 copy-start.6
  24.5 0.7 copy-start.7
  25.1 9.6 %copy-start.4 = (f32[2,4096]{1,0:T(2,128)S(1)}, f32[2,4096]{1,0:T(2,128)}, u32[]{:S(2)}) copy-start(f32[2,4096]{1,0:T(2,128)} %precision.1) | copy-start | bytes 98308
  25.4 6.0 %collective-permute-start.2 = (f32[48,256]{1,0:T(8,128)S(1)}, f32[48,256]{1,0:T(8,128)S(1)}, u32[]{:S(2)}, u32[]{:S(2)}) collective-permute-start(f32[48,256]{1,0:T(8,128)S(1)} %get-tuple-element.24), channel_id=1, source_target_pairs={{0,1},{1,2},{2,3},{4,5},{5,6},{6,7},{8,9},{9,10},{10,11},{12,13},{... | collective-permute-start | bytes 147464 | tf_op jit(solution)/shard_map/ppermute | solution.py:451
  28.8 6.0 %collective-permute-start.3 = (f32[48,256]{1,0:T(8,128)S(1)}, f32[48,256]{1,0:T(8,128)S(1)}, u32[]{:S(2)}, u32[]{:S(2)}) collective-permute-start(f32[48,256]{1,0:T(8,128)S(1)} %get-tuple-element.25), channel_id=1, source_target_pairs={{1,0},{2,1},{3,2},{5,4},{6,5},{7,6},{9,8},{10,9},{11,10},{13,12},{... | collective-permute-start | bytes 147464 | tf_op jit(solution)/shard_map/ppermute | solution.py:451
  34.8 1.0 %copy-start.3 = (f32[16,4096]{1,0:T(8,128)S(1)}, f32[16,4096]{1,0:T(8,128)}, u32[]{:S(2)}) copy-start(f32[16,4096]{1,0:T(8,128)} %get-tuple-element.19.fields) | copy-start | bytes 786436
  59.5 25.4 %all-to-all-start.1 = ((f32[8,80,128]{2,1,0:T(8,128)}), f32[8,80,128]{2,1,0:T(8,128)S(1)}, u32[]{:S(2)}, u32[]{:S(2)}) async-start(f32[8,80,128]{2,1,0:T(8,128)} %shard_map.108), calls=%async_computation.1 | async-start | bytes 655360 | tf_op jit(solution)/shard_map/all_to_all | solution.py:446
  65.9 6.2 %collective-permute-start.4 = (f32[18,512]{1,0:T(8,128)S(1)}, f32[18,512]{1,0:T(8,128)S(1)}, u32[]{:S(2)}, u32[]{:S(2)}) collective-permute-start(f32[18,512]{1,0:T(8,128)S(1)} %get-tuple-element.28), channel_id=1, source_target_pairs={{0,4},{4,0},{8,12},{12,8},{16,20},{20,16},{24,28},{28,24},{32,36},... | collective-permute-start | bytes 110600 | tf_op jit(solution)/shard_map/ppermute | solution.py:430
  67.8 8.7 %collective-permute-start.5 = (f32[18,512]{1,0:T(8,128)S(1)}, f32[18,512]{1,0:T(8,128)S(1)}, u32[]{:S(2)}, u32[]{:S(2)}) collective-permute-start(f32[18,512]{1,0:T(8,128)S(1)} %get-tuple-element.29), channel_id=1, source_target_pairs={{4,8},{8,4},{12,16},{16,12},{20,24},{24,20},{28,32},{32,28},{36,40... | collective-permute-start | bytes 110600 | tf_op jit(solution)/shard_map/ppermute | solution.py:431
  76.7 5.9 %collective-permute-start.6 = (f32[32,128]{1,0:T(8,128)S(1)}, f32[32,128]{1,0:T(8,128)S(1)}, u32[]{:S(2)}, u32[]{:S(2)}) collective-permute-start(f32[32,128]{1,0:T(8,128)S(1)} %get-tuple-element.31), channel_id=1, source_target_pairs={{0,1},{1,2},{2,3},{4,5},{5,6},{6,7},{8,9},{9,10},{10,11},{12,13},{... | collective-permute-start | bytes 49160 | tf_op jit(solution)/shard_map/ppermute | solution.py:451
  79.3 5.6 %collective-permute-start.7 = (f32[32,128]{1,0:T(8,128)S(1)}, f32[32,128]{1,0:T(8,128)S(1)}, u32[]{:S(2)}, u32[]{:S(2)}) collective-permute-start(f32[32,128]{1,0:T(8,128)S(1)} %get-tuple-element.32), channel_id=1, source_target_pairs={{1,0},{2,1},{3,2},{5,4},{6,5},{7,6},{9,8},{10,9},{11,10},{13,12},{... | collective-permute-start | bytes 49160 | tf_op jit(solution)/shard_map/ppermute | solution.py:451

commit v3 on v2

--- a/solution.py
+++ b/solution.py
@@ -76,16 +76,48 @@
     return table
 
 
-def pack_kernel(move, cell, weight, obs, prec, init, depth, mixing, fields, inner, outer, south, north, east, west):
-    count = move.shape[1]
+def stage(fields, cell, weight, obs):
     for step in range(STEPS):
         base = step * FIELDS
         for i in range(4):
             fields[base + i : base + i + 1, :] = weight[i, step : step + 1, :]
         for i in range(2):
             fields[base + 4 + i : base + 5 + i, :] = obs[i, step : step + 1, :]
-        fields[base + 6 : base + 7, :] = prec[step : step + 1, :]
         fields[base + 7 : base + 8, :] = cell[step : step + 1, :].astype(F32)
+
+
+def own_kernel(refine, lat_count, controls, move, cell, weight, obs, prec, fields, forcing):
+    stage(fields, cell, weight, obs)
+    for step in range(STEPS):
+        row = step * FIELDS + 6
+        fields[row : row + 1, :] = jnp.where(move[step : step + 1, :] == 4, prec[step : step + 1, :], 0.0)
+    tall, wide = forcing.shape[1:]
+    rows, cells_lat = tall - 16, wide - 256
+    periods, _, ctrl_lat, ctrl_lon = controls.shape
+    table = period_weights(STEPS, periods)
+    low, part = interpolation(iota((tall, ctrl_lon), 0) - X0 + lax.axis_index("lon") * rows - refine // 2, refine)
+    column = iota((tall, ctrl_lon), 1)
+    wrapped, after = (low + ctrl_lon) % ctrl_lon, (low + 1 + ctrl_lon) % ctrl_lon
+    lon_interp = jnp.where(column == wrapped, 1.0 - part, 0.0) + jnp.where(column == after, part, 0.0)
+    low, part = interpolation(iota((ctrl_lat, wide), 1) - Y0 + lax.axis_index("lat") * cells_lat - refine // 2, refine)
+    column = iota((ctrl_lat, wide), 0)
+    lat_interp = jnp.where(column == low, 1.0 - part, 0.0) + jnp.where(column == low + 1, part, 0.0)
+    lon_interp, lat_interp = lon_interp.astype(BF16), lat_interp.astype(BF16)
+    for step in range(STEPS):
+        for c in range(2):
+            blended = table[step][0] * controls[0, c]
+            for period in range(1, periods):
+                blended = blended + table[step][period] * controls[period, c]
+            high, low = split(blended)
+            high, low = split(dot_lanes(lon_interp, high) + dot_lanes(lon_interp, low))
+            forcing[2 * step + c] = dot(high, lat_interp) + dot(low, lat_interp)
+
+
+def pack_kernel(move, cell, weight, obs, prec, init, depth, mixing, inner, outer, beside, fields, east, west):
+    count = move.shape[1]
+    stage(fields, cell, weight, obs)
+    for step in range(STEPS):
+        fields[step * FIELDS + 6 : step * FIELDS + 7, :] = prec[step : step + 1, :]
     rows = init.shape[2]
     planes = [init.at[c, k] for c in range(2) for k in range(DEPTH)]
     for p in range(PLANES):
@@ -123,13 +155,11 @@
             record = packed[step][at : at + FIELDS] + packed[step][at + FIELDS : at + 2 * FIELDS]
             code = CODES[d]
             if code // 3 == 1:
-                (south if code % 3 == 0 else north)[:, lanes] = record
+                row = code % 3 // 2 * FIELDS
+                beside[row : row + FIELDS, lanes] = record
             else:
                 row = (code % 3) * FIELDS
                 (west if code // 3 == 0 else east)[row : row + FIELDS, lanes] = record
-    for step in range(STEPS):
-        row = step * FIELDS + 6
-        fields[row : row + 1, :] = jnp.where(move[step : step + 1, :] == 4, prec[step : step + 1, :], 0.0)
     address(east, west, inner, outer)
 
 
@@ -142,7 +172,7 @@
     ext[p, X0 + rows : X0 + rows + HIGH, lanes] = from_east[at : at + HIGH, :]
 
 
-def merge_kernel(init, depth, mixing, to_south, to_north, inner, outer, ext, south, north):
+def merge_kernel(init, depth, mixing, beside, inner, outer, ext, south, north):
     from_west, from_east = pick(inner, outer)
     rows, cells_lat = depth.shape
     ext[...] = jnp.zeros_like(ext)
@@ -161,8 +191,8 @@
         tail = jnp.where(lane >= 128 - LOW, ext[p, :, Y0 + cells_lat - 128 : Y0 + cells_lat], 0.0)
         first = first + roll(head, HIGH * p, 1)
         last = last + roll(tail, -LOW * p, 1)
-    for out, kept, row, strip in ((south, to_south, 0, first), (north, to_north, 2, last)):
-        out[0:FIELDS, :] = kept[...]
+    for out, kept, row, strip in ((south, 0, 0, first), (north, 1, 2, last)):
+        out[0:FIELDS, :] = beside[kept * FIELDS : (kept + 1) * FIELDS, :]
         out[FIELDS : 2 * FIELDS, :] = from_west[row * FIELDS : (row + 1) * FIELDS, :]
         out[2 * FIELDS : 3 * FIELDS, :] = from_east[row * FIELDS : (row + 1) * FIELDS, :]
         out[3 * FIELDS :, 0:128] = strip[: tall // 2]
@@ -190,16 +220,14 @@
 
 
 def main_kernel(
-    levels, refine, lon_count, lat_count, controls, fields, precision, inner, outer, from_south, from_north,
+    levels, refine, lat_count, forcing, fields, precision, inner, outer, from_south, from_north,
     padded, partial, share, to_inner, to_outer, ext, spot, to_west, to_east,
 ):
     from_west, from_east = pick(inner, outer)
     rows, cells_lat = partial.shape[1] - 16, partial.shape[2] - 256
     tall, wide = ext.shape[1:]
-    lon_index, lat_index = lax.axis_index("lon"), lax.axis_index("lat")
+    lat_index = lax.axis_index("lat")
     grid_lat = cells_lat * lat_count
-    periods, _, ctrl_lat, ctrl_lon = controls.shape
-    table = period_weights(STEPS, periods)
     lane = iota((tall, 128), 1)
     half = tall // 2
     below = jnp.concatenate([from_south[3 * FIELDS :, 0:128], from_south[3 * FIELDS :, 128:]], axis=0)
@@ -213,26 +241,6 @@
     wet = [(full[2 * DEPTH] > float(k)).astype(F32) for k in range(DEPTH)]
     row_ids = iota((1, wide), 1) - Y0 + lat_index * cells_lat
     rotation = ROTATION * jnp.sin((row_ids.astype(F32) + 0.5) * (math.pi / grid_lat) - 0.5 * math.pi)
-    offset = iota((tall, ctrl_lon), 0) - X0 + lon_index * rows - refine // 2
-    low, part = interpolation(offset, refine)
-    column = iota((tall, ctrl_lon), 1)
-    wrapped, after = (low + ctrl_lon) % ctrl_lon, (low + 1 + ctrl_lon) % ctrl_lon
-    lon_interp = jnp.where(column == wrapped, 1.0 - part, 0.0) + jnp.where(column == after, part, 0.0)
-    offset = iota((ctrl_lat, wide), 1) - Y0 + lat_index * cells_lat - refine // 2
-    low, part = interpolation(offset, refine)
-    column = iota((ctrl_lat, wide), 0)
-    lat_interp = jnp.where(column == low, 1.0 - part, 0.0) + jnp.where(column == low + 1, part, 0.0)
-    lon_interp, lat_interp = lon_interp.astype(BF16), lat_interp.astype(BF16)
-    forcing = []
-    for step in range(STEPS):
-        forcing.append([])
-        for c in range(2):
-            blended = table[step][0] * controls[0, c]
-            for period in range(1, periods):
-                blended = blended + table[step][period] * controls[period, c]
-            high, low = split(blended)
-            high, low = split(dot_lanes(lon_interp, high) + dot_lanes(lon_interp, low))
-            forcing[step].append(dot(high, lat_interp) + dot(low, lat_interp))
     state = [[wet[k] * full[c * DEPTH + k] for k in range(DEPTH)] for c in range(2)]
     surfaces = []
     for step in range(STEPS):
@@ -240,42 +248,48 @@
         for k in range(DEPTH - 1 - step):
             moved = tendency(state, k, lambda v: mixing * lap(v), rotation, levels)
             for c in range(2):
-                value = moved[c] + forcing[step][c] if k == 0 else moved[c]
+                value = moved[c] + forcing[2 * step + c] if k == 0 else moved[c]
                 ahead[c].append(wet[k] * value)
         state = ahead
         surfaces.append([state[0][0], state[1][0]])
-    strip = rows + 8
+    strip, tiles = rows + 8, rows + 16
     chunk = 512
-    lat_of = iota((cells_lat, chunk), 0)
-    lon_of = iota((strip, chunk), 0)
+    lat_of = iota((cells_lat, chunk), 0).astype(F32).astype(BF16)
+    lon_of = iota((strip, chunk), 0).astype(F32)
+    lon_tile = iota((tiles, chunk), 0).astype(F32).astype(BF16)
+    one, nought = jnp.ones((), BF16), jnp.zeros((), BF16)
     sources = []
     for step in range(STEPS):
         views = []
         for c in range(2):
             surface = surfaces[step][c][X0 : X0 + strip]
             views += [surface[:, Y0 : Y0 + cells_lat], roll(surface, -1, 1)[:, Y0 : Y0 + cells_lat]]
-        views_high, views_low = split(jnp.concatenate(views, axis=0))
+        views = jnp.concatenate(split(jnp.concatenate(views, axis=0)), axis=0)
 
         def spread(record, total):
             cell = record[7:8].astype(jnp.int32)
-            lon = lax.shift_right_logical(cell, cells_lat.bit_length() - 1)
-            lat = cell & (cells_lat - 1)
-            hot = (lat_of == lat).astype(F32).astype(BF16)
-            found = dot(views_high, hot) + dot(views_low, hot)
-            here, there = lon_of == lon, lon_of == lon + 1
+            lon = lax.shift_right_logical(cell, cells_lat.bit_length() - 1).astype(F32)
+            lat = (cell & (cells_lat - 1)).astype(F32).astype(BF16)
+            hot = jnp.where(lat_of == lat, one, nought)
+            found = dot(views, hot)
+            found = found[: 4 * strip] + found[4 * strip :]
+            here, there = lon_of == lon, lon_of == lon + 1.0
             near = jnp.where(here, record[0:1], jnp.where(there, record[1:2], 0.0))
             far = jnp.where(here, record[2:3], jnp.where(there, record[3:4], 0.0))
-            terms = []
+            lon = lon.astype(BF16)
+            here, there = lon_tile == lon, lon_tile == lon + one
+            terms = [[], []]
             for c in range(2):
                 at = 2 * c * strip
                 seen = near * found[at : at + strip] + far * found[at + strip : at + 2 * strip]
                 miss = jnp.sum(seen, axis=0, keepdims=True) - record[4 + c : 5 + c]
-                miss = record[6:7] * miss
-                terms += [near * miss, far * miss]
-            high, low = split(jnp.concatenate(terms, axis=0))
-            return total + dot_lanes(high, hot) + dot_lanes(low, hot)
-
-        total = jnp.zeros((4 * strip, cells_lat), F32)
+                parts = split(record[0:4] * (record[6:7] * miss))
+                for part, term in zip(parts, terms):
+                    for d in (0, 2):
+                        term.append(jnp.where(here, part[d : d + 1], jnp.where(there, part[d + 1 : d + 2], nought)))
+            return total + dot_lanes(jnp.concatenate(terms[0] + terms[1], axis=0), hot)
+
+        total = jnp.zeros((8 * tiles, cells_lat), F32)
         for at in range(0, fields.shape[1], chunk):
             total = spread(fields[step * FIELDS : (step + 1) * FIELDS, at : at + chunk], total)
         lanes = slice(step * CAPACITY, (step + 1) * CAPACITY)
@@ -284,11 +298,12 @@
         for at in range(0, 8, chunk // CAPACITY):
             total = spread(jnp.concatenate(came[at : at + chunk // CAPACITY], axis=1), total)
         sources.append([])
+        total = total[: 4 * tiles] + total[4 * tiles :]
         for c in range(2):
-            at = 2 * c * strip
+            at = 2 * c * tiles
             spot[...] = jnp.zeros_like(spot)
             spot[0, X0 : X0 + strip, Y0 : Y0 + cells_lat] = total[at : at + strip]
-            spot[1, X0 : X0 + strip, Y0 : Y0 + cells_lat] = total[at + strip : at + 2 * strip]
+            spot[1, X0 : X0 + strip, Y0 : Y0 + cells_lat] = total[at + tiles : at + tiles + strip]
             sources[step].append(spot[0] + roll(spot[1], 1, 1))
     adjoint = None
     nudges = [None] * STEPS
@@ -333,7 +348,8 @@
     share[...] = jnp.broadcast_to(jnp.concatenate(parts, axis=0)[None], share.shape)
 
 
-def plane_kernel(lat_count, per, shares, out, rows, total):
+def plane_kernel(lat_count, per, shares, partial, inner, outer, out, own, south, north, rows, total):
+    join(partial, inner, outer, own, south, north)
     members = shares.shape[0]
     ring = members // (CORES * lat_count)
     ctrl_lat = per * lat_count
@@ -366,7 +382,7 @@
     out[...] = jnp.broadcast_to(total[...][None], out.shape)
 
 
-def join_kernel(partial, inner, outer, own, south, north):
+def join(partial, inner, outer, own, south, north):
     from_west, from_east = pick(inner, outer)
     rows, cells_lat = own.shape[1:]
     lane = iota((rows, 128), 1)
@@ -479,19 +495,24 @@
     tall, wide = rows + 16, cells_lat + 256
     surface = (2, DEPTH, rows, cells_lat)
     lon_message = (3 * FIELDS + HIGH * PLANES, 256)
-    fields, inner, outer, south, north = call(
+    inner, outer, beside = call(
         pack_kernel,
         (drift_move, drift_cell, drift_weight, drift_obs, drift_precision, initial, depth_levels, mixing),
-        ((STEPS * FIELDS, count), lon_message, lon_message, (FIELDS, 256), (FIELDS, 256)),
+        (lon_message, lon_message, (2 * FIELDS, 256)),
         {5: surface},
-        scratch=(lon_message, lon_message),
+        scratch=((STEPS * FIELDS, count), lon_message, lon_message),
         vmem=60,
     )
     inner, outer = swap(inner, outer)
+    fields, forcing = call(
+        functools.partial(own_kernel, refine, lat_count),
+        (jnp.swapaxes(controls, 2, 3), drift_move, drift_cell, drift_weight, drift_obs, drift_precision),
+        ((STEPS * FIELDS, count), (2 * STEPS, tall, wide)),
+    )
     message = (3 * FIELDS + tall // 2, 256)
     padded, south, north = call(
         merge_kernel,
-        (initial, depth_levels, mixing, south, north, inner, outer),
+        (initial, depth_levels, mixing, beside, inner, outer),
         ((PLANES, tall, wide), message, message),
         {0: surface},
     )
@@ -500,27 +521,22 @@
     ring = min(RING, lon_count // CORES)
     members = lon_count // (CORES * ring)
     partial, share, inner, outer = call(
-        functools.partial(main_kernel, levels, refine, lon_count, lat_count),
-        (jnp.swapaxes(controls, 2, 3), fields, drift_precision, inner, outer, from_south, from_north, padded),
+        functools.partial(main_kernel, levels, refine, lat_count),
+        (forcing, fields, drift_precision, inner, outer, from_south, from_north, padded),
         ((2 * DEPTH, tall, wide), (ring * CORES * lat_count, 2 * STEPS, 4 * GROUP), edge, edge),
         scratch=((2 * DEPTH, tall, wide), (2, tall, wide), edge, edge),
     )
     shares = gather(share, ring, 1, True)
+    inner, outer = swap(inner, outer)
     height = -(-(4 * ring + 3) // 8) * 8
-    (share,) = call(
+    share, own, to_south, to_north = call(
         functools.partial(plane_kernel, lat_count, ctrl_lat // lat_count),
-        (shares,),
-        ((members, STEPS * height, 2 * ctrl_lat),),
+        (shares, partial, inner, outer),
+        ((members, STEPS * height, 2 * ctrl_lat), (2 * DEPTH, rows, cells_lat), (rows, 128), (rows, 128)),
         scratch=((4 * ring * CORES * lat_count, 4 * GROUP), (STEPS * height, 2 * ctrl_lat)),
     )
+    from_south, from_north = along(to_north, 1), along(to_south, -1)
     shares = gather(share, members, ring, False)
-    inner, outer = swap(inner, outer)
-    own, to_south, to_north = call(
-        join_kernel,
-        (partial, inner, outer),
-        ((2 * DEPTH, rows, cells_lat), (rows, 128), (rows, 128)),
-    )
-    from_south, from_north = along(to_north, 1), along(to_south, -1)
     grad_initial, grad_controls = call(
         functools.partial(finish_kernel, float(STEPS * count * lon_count * lat_count)),
         (own, depth_levels, from_south, from_north, shares),

time: 86.7 us -> 78.6 us (0.907)
  the two profiles are of different devices: /device:TPU:2 before, /device:TPU:8 now
where the time goes in v3:
time: 78.6 us; the launch traced here: 78.1 us
  starting transfers between devices  40.2 us (51%)
  waiting for transfers between devices  21.6 us (27%)
  Pallas kernels  14.6 us (19%)
  between operations  0.85 us (1%)
    all_to_all x2, starting transfers between devices, gather(): lax.all_to_all(copies, ('lon', 'lat'), 0, 0, axis_index_groups=groups, ti...  19.6 us
    pallas_call x6, Pallas kernels, call(): pl.pallas_call(kernel, grid=(1,), out_shape=[jax.ShapeDtypeStruct(shape,...  14.6 us
    ppermute x2, starting transfers between devices, swap(): lax.ppermute(outer, 'lon', [((i + 1) % count, ((i ^ 1) + 1) % count) for...  10.2 us
    ppermute x4, waiting for transfers between devices, along(): lax.ppermute(value, 'lat', [(i, i + distance) for i in range(max(0, -dist...  8.26 us
    all_to_all x2, waiting for transfers between devices, gather(): lax.all_to_all(copies, ('lon', 'lat'), 0, 0, axis_index_groups=groups, ti...  8.2 us
    ppermute x4, starting transfers between devices, along(): lax.ppermute(value, 'lat', [(i, i + distance) for i in range(max(0, -dist...  6.35 us
    ppermute x2, waiting for transfers between devices, swap(): lax.ppermute(outer, 'lon', [((i + 1) % count, ((i ^ 1) + 1) % count) for...  5.1 us
    ppermute x2, starting transfers between devices, swap(): inner = lax.ppermute(inner, 'lon', [(i, i ^ 1) for i in range(count)])  4.1 us
  transfers between devices with their start and end apart: 10, of which 7 were waited for; matrix products, arithmetic and copies ran while one was open for 0% of the time, Pallas kernels for 1%

profile of v3, /device:TPU:8, one launch (start us, length us, event | category | flops | bytes accessed | tf_op | source)
XLA Modules:
  0.0 78.1 jit_solution(13729880510316548741)
XLA Ops:
  0.6 0.0 copy-start.4
  0.6 0.0 copy-start.6
  0.7 0.0 copy-start
  0.7 0.0 copy-start.5
  0.7 5.0 %shard_map.105 = (f32[48,256]{1,0:T(8,128)}, f32[48,256]{1,0:T(8,128)}, f32[16,256]{1,0:T(8,128)}) custom-call(s32[2,4096]{1,0:T(2,128)} %move.3, s32[2,4096]{1,0:T(2,128)} %cell.3, f32[4,2,4096]{2,1,0:T(2,128)} %weight.3, f32[2,2,4096]{2,1,0:T(2,128)} %obs.3, f32[2,4096]{1,0:T(2,128)} %precision.1, f32[2,8,32,256]{3,2,1,0:T(8,128)} %init.3, ...), custom_call_target="tpu_custom_call" | custom-call | tf_op jit(solution)/shard_map/pallas_call | solution.py:476
  5.7 2.0 %collective-permute-start = (f32[48,256]{1,0:T(8,128)}, f32[48,256]{1,0:T(8,128)S(1)}, u32[]{:S(2)}, u32[]{:S(2)}) collective-permute-start(f32[48,256]{1,0:T(8,128)} %get-tuple-element.22), channel_id=1, source_target_pairs={{0,4},{4,0},{8,12},{12,8},{16,20},{20,16},{24,28},{28,24},{32,36},... | collective-permute-start | bytes 147464 | tf_op jit(solution)/shard_map/ppermute | solution.py:446
  7.8 7.8 %collective-permute-start.1 = (f32[48,256]{1,0:T(8,128)}, f32[48,256]{1,0:T(8,128)S(1)}, u32[]{:S(2)}, u32[]{:S(2)}) collective-permute-start(f32[48,256]{1,0:T(8,128)} %get-tuple-element.23), channel_id=1, source_target_pairs={{4,8},{8,4},{12,16},{16,12},{20,24},{24,20},{28,32},{32,28},{36,40... | collective-permute-start | bytes 147464 | tf_op jit(solution)/shard_map/ppermute | solution.py:447
  15.6 0.0 collective-permute-done.inner
  15.6 2.0 %collective-permute-done.1.outer = f32[48,256]{1,0:T(8,128)S(1)} collective-permute-done((f32[48,256]{1,0:T(8,128)}, f32[48,256]{1,0:T(8,128)S(1)}, u32[]{:S(2)}, u32[]{:S(2)}) %collective-permute-start.1) | collective-permute-done | bytes 49184 | tf_op jit(solution)/shard_map/ppermute | solution.py:447
  17.7 0.0 copy-done.4
  17.7 0.7 copy-done.9
  18.4 0.2 shard_map.106
  18.6 1.3 %collective-permute-start.2 = (f32[48,256]{1,0:T(8,128)S(1)}, f32[48,256]{1,0:T(8,128)S(1)}, u32[]{:S(2)}, u32[]{:S(2)}) collective-permute-start(f32[48,256]{1,0:T(8,128)S(1)} %get-tuple-element.25), channel_id=1, source_target_pairs={{0,1},{1,2},{2,3},{4,5},{5,6},{6,7},{8,9},{9,10},{10,11},{12,13},{... | collective-permute-start | bytes 147464 | tf_op jit(solution)/shard_map/ppermute | solution.py:467
  19.9 1.3 %collective-permute-start.3 = (f32[48,256]{1,0:T(8,128)S(1)}, f32[48,256]{1,0:T(8,128)S(1)}, u32[]{:S(2)}, u32[]{:S(2)}) collective-permute-start(f32[48,256]{1,0:T(8,128)S(1)} %get-tuple-element.26), channel_id=1, source_target_pairs={{1,0},{2,1},{3,2},{5,4},{6,5},{7,6},{9,8},{10,9},{11,10},{13,12},{... | collective-permute-start | bytes 147464 | tf_op jit(solution)/shard_map/ppermute | solution.py:467
  21.3 0.7 shard_map.104
  22.0 0.0 collective-permute-done.2.from_south
  22.0 3.9 %collective-permute-done.3.from_north = f32[48,256]{1,0:T(8,128)S(1)} collective-permute-done((f32[48,256]{1,0:T(8,128)S(1)}, f32[48,256]{1,0:T(8,128)S(1)}, u32[]{:S(2)}, u32[]{:S(2)}) %collective-permute-start.3) | collective-permute-done | bytes 49184 | tf_op jit(solution)/shard_map/ppermute | solution.py:467
  25.9 6.5 %shard_map.107 = (f32[6,48,512]{2,1,0:T(8,128)S(1)}, f32[64,4,128]{2,1,0:T(4,128)}, f32[18,512]{1,0:T(8,128)S(1)}, f32[18,512]{1,0:T(8,128)S(1)}) custom-call(f32[4,48,512]{2,1,0:T(8,128)S(1)} %get-tuple-element.20.forcing, f32[16,4096]{1,0:T(8,128)S(1)} %get-tuple-element.21.fields, f32[2,4096]{1,0:T(2,128)S(1)} %copy-done.3, ...), custom_call_target="tpu_custom_call" | custom-call | tf_op jit(solution)/shard_map/pallas_call | solution.py:476
  32.4 13.2 %all-to-all-start = ((f32[64,4,128]{2,1,0:T(4,128)}), f32[64,4,128]{2,1,0:T(4,128)S(1)}, u32[]{:S(2)}, u32[]{:S(2)}) async-start(f32[64,4,128]{2,1,0:T(4,128)} %get-tuple-element.28), calls=%async_computation | async-start | bytes 262144 | tf_op jit(solution)/shard_map/all_to_all | solution.py:462
  45.7 2.1 %collective-permute-start.4 = (f32[18,512]{1,0:T(8,128)S(1)}, f32[18,512]{1,0:T(8,128)S(1)}, u32[]{:S(2)}, u32[]{:S(2)}) collective-permute-start(f32[18,512]{1,0:T(8,128)S(1)} %get-tuple-element.30), channel_id=1, source_target_pairs={{0,4},{4,0},{8,12},{12,8},{16,20},{20,16},{24,28},{28,24},{32,36},... | collective-permute-start | bytes 110600 | tf_op jit(solution)/shard_map/ppermute | solution.py:446
  47.7 2.3 %collective-permute-start.5 = (f32[18,512]{1,0:T(8,128)S(1)}, f32[18,512]{1,0:T(8,128)S(1)}, u32[]{:S(2)}, u32[]{:S(2)}) collective-permute-start(f32[18,512]{1,0:T(8,128)S(1)} %get-tuple-element.31), channel_id=1, source_target_pairs={{4,8},{8,4},{12,16},{16,12},{20,24},{24,20},{28,32},{32,28},{36,40... | collective-permute-start | bytes 110600 | tf_op jit(solution)/shard_map/ppermute | solution.py:447
  50.1 0.0 collective-permute-done.4.inner
  50.1 3.1 %collective-permute-done.5.outer = f32[18,512]{1,0:T(8,128)S(1)} collective-permute-done((f32[18,512]{1,0:T(8,128)S(1)}, f32[18,512]{1,0:T(8,128)S(1)}, u32[]{:S(2)}, u32[]{:S(2)}) %collective-permute-start.5) | collective-permute-done | bytes 36896 | tf_op jit(solution)/shard_map/ppermute | solution.py:447
  53.1 3.1 %all-to-all-done.shares = f32[64,4,128]{2,1,0:T(4,128)S(1)} async-done(((f32[64,4,128]{2,1,0:T(4,128)}), f32[64,4,128]{2,1,0:T(4,128)S(1)}, u32[]{:S(2)}, u32[]{:S(2)}) %all-to-all-start) | async-done | bytes 131104 | tf_op jit(solution)/shard_map/all_to_all | solution.py:462
  56.2 1.0 %shard_map.108 = (f32[8,80,128]{2,1,0:T(8,128)}, f32[6,32,256]{2,1,0:T(8,128)S(1)}, f32[32,128]{1,0:T(8,128)S(1)}, f32[32,128]{1,0:T(8,128)S(1)}) custom-call(f32[64,4,128]{2,1,0:T(4,128)S(1)} %all-to-all-done.shares, f32[6,48,512]{2,1,0:T(8,128)S(1)} %get-tuple-element.29.partial, f32[18,512]{1,0:T(8,128)S(1)} %collective-permute-done.4.inner, ...), custom_call_target="tpu_custom_call" | custom-call | tf_op jit(solution)/shard_map/pallas_call | solution.py:476
  57.2 6.4 %all-to-all-start.1 = ((f32[8,80,128]{2,1,0:T(8,128)}), f32[8,80,128]{2,1,0:T(8,128)S(1)}, u32[]{:S(2)}, u32[]{:S(2)}) async-start(f32[8,80,128]{2,1,0:T(8,128)} %get-tuple-element.35), calls=%async_computation.1 | async-start | bytes 655360 | tf_op jit(solution)/shard_map/all_to_all | solution.py:462
  63.6 2.5 %collective-permute-start.6 = (f32[32,128]{1,0:T(8,128)S(1)}, f32[32,128]{1,0:T(8,128)S(1)}, u32[]{:S(2)}, u32[]{:S(2)}) collective-permute-start(f32[32,128]{1,0:T(8,128)S(1)} %get-tuple-element.33), channel_id=1, source_target_pairs={{0,1},{1,2},{2,3},{4,5},{5,6},{6,7},{8,9},{9,10},{10,11},{12,13},{... | collective-permute-start | bytes 49160 | tf_op jit(solution)/shard_map/ppermute | solution.py:467
  66.1 1.3 %collective-permute-start.7 = (f32[32,128]{1,0:T(8,128)S(1)}, f32[32,128]{1,0:T(8,128)S(1)}, u32[]{:S(2)}, u32[]{:S(2)}) collective-permute-start(f32[32,128]{1,0:T(8,128)S(1)} %get-tuple-element.34), channel_id=1, source_target_pairs={{1,0},{2,1},{3,2},{5,4},{6,5},{7,6},{9,8},{10,9},{11,10},{13,12},{... | collective-permute-start | bytes 49160 | tf_op jit(solution)/shard_map/ppermute | solution.py:467
  67.4 0.1 collective-permute-done.6.from_south
  67.5 4.2 %collective-permute-done.7.from_north = f32[32,128]{1,0:T(8,128)S(1)} collective-permute-done((f32[32,128]{1,0:T(8,128)S(1)}, f32[32,128]{1,0:T(8,128)S(1)}, u32[]{:S(2)}, u32[]{:S(2)}) %collective-permute-start.7) | collective-permute-done | bytes 16416 | tf_op jit(solution)/shard_map/ppermute | solution.py:467
  71.7 5.1 %all-to-all-done.1.shares = f32[8,80,128]{2,1,0:T(8,128)S(1)} async-done(((f32[8,80,128]{2,1,0:T(8,128)}), f32[8,80,128]{2,1,0:T(8,128)S(1)}, u32[]{:S(2)}, u32[]{:S(2)}) %all-to-all-start.1) | async-done | bytes 327712 | tf_op jit(solution)/shard_map/all_to_all | solution.py:462
  76.9 1.2 %shard_map.109 = (f32[2,8,32,256]{3,2,1,0:T(8,128)}, f32[4,2,64,256]{3,2,1,0:T(8,128)}) custom-call(f32[6,32,256]{2,1,0:T(8,128)S(1)} %get-tuple-element.32.own, s32[32,256]{1,0:T(8,128)S(1)} %copy-done.4, f32[32,128]{1,0:T(8,128)S(1)} %collective-permute-done.6.from_south, f32[32,128]{1,0:T(8,128)S(1)} %collective-permute-done.7.from_north, ...), custom_call_target="tpu_custom_call" | custom-call | tf_op jit(solution)/shard_map/pallas_call | solution.py:476
  (14 shorter events, 0.0 us)
Async XLA Ops:
  0.6 17.0 %copy-start.4 = (s32[32,256]{1,0:T(8,128)S(1)}, s32[32,256]{1,0:T(8,128)}, u32[]{:S(2)}) copy-start(s32[32,256]{1,0:T(8,128)} %depth.5) | copy-start | bytes 98308
  0.6 17.0 %copy-start.6 = (f32[32,256]{1,0:T(8,128)S(1)}, f32[32,256]{1,0:T(8,128)}, u32[]{:S(2)}) copy-start(f32[32,256]{1,0:T(8,128)} %mixing.3) | copy-start | bytes 98308
  0.7 17.0 %copy-start = (f32[2,8,32,256]{3,2,1,0:T(8,128)S(1)}, f32[2,8,32,256]{3,2,1,0:T(8,128)}, u32[]{:S(2)}) copy-start(f32[2,8,32,256]{3,2,1,0:T(8,128)} %init.3) | copy-start | bytes 1572868
  0.7 20.5 %copy-start.5 = (f32[2,2,4096]{2,1,0:T(2,128)S(1)}, f32[2,2,4096]{2,1,0:T(2,128)}, u32[]{:S(2)}) copy-start(f32[2,2,4096]{2,1,0:T(2,128)} %obs.3) | copy-start | bytes 196612
  0.7 20.5 %copy-start.7 = (s32[2,4096]{1,0:T(2,128)S(1)}, s32[2,4096]{1,0:T(2,128)}, u32[]{:S(2)}) copy-start(s32[2,4096]{1,0:T(2,128)} %move.3) | copy-start | bytes 98308
  0.7 20.5 %copy-start.8 = (s32[2,4096]{1,0:T(2,128)S(1)}, s32[2,4096]{1,0:T(2,128)}, u32[]{:S(2)}) copy-start(s32[2,4096]{1,0:T(2,128)} %cell.3) | copy-start | bytes 98308
  5.7 15.5 %copy-start.2 = (f32[4,2,256,64]{2,3,1,0:T(8,128)S(1)}, f32[4,2,256,64]{2,3,1,0:T(8,128)}, u32[]{:S(2)}) copy-start(f32[4,2,256,64]{2,3,1,0:T(8,128)} %param.12) | copy-start | bytes 1572868
  5.7 9.9 %collective-permute-start = (f32[48,256]{1,0:T(8,128)}, f32[48,256]{1,0:T(8,128)S(1)}, u32[]{:S(2)}, u32[]{:S(2)}) collective-permute-start(f32[48,256]{1,0:T(8,128)} %get-tuple-element.22), channel_id=1, source_target_pairs={{0,4},{4,0},{8,12},{12,8},{16,20},{20,16},{24,28},{28,24},{32,36},... | collective-permute-start | bytes 147464 | tf_op jit(solution)/shard_map/ppermute | solution.py:446
  7.8 9.9 %collective-permute-start.1 = (f32[48,256]{1,0:T(8,128)}, f32[48,256]{1,0:T(8,128)S(1)}, u32[]{:S(2)}, u32[]{:S(2)}) collective-permute-start(f32[48,256]{1,0:T(8,128)} %get-tuple-element.23), channel_id=1, source_target_pairs={{4,8},{8,4},{12,16},{16,12},{20,24},{24,20},{28,32},{32,28},{36,40... | collective-permute-start | bytes 147464 | tf_op jit(solution)/shard_map/ppermute | solution.py:447
  17.7 0.7 copy-start.9
  18.4 2.9 %copy-start.1 = (f32[4,2,4096]{2,1,0:T(2,128)S(1)}, f32[4,2,4096]{2,1,0:T(2,128)}, u32[]{:S(2)}) copy-start(f32[4,2,4096]{2,1,0:T(2,128)} %weight.3) | copy-start | bytes 393220
  18.4 2.9 %copy-start.3 = (f32[2,4096]{1,0:T(2,128)S(1)}, f32[2,4096]{1,0:T(2,128)}, u32[]{:S(2)}) copy-start(f32[2,4096]{1,0:T(2,128)} %precision.1) | copy-start | bytes 98308
  18.6 3.4 %collective-permute-start.2 = (f32[48,256]{1,0:T(8,128)S(1)}, f32[48,256]{1,0:T(8,128)S(1)}, u32[]{:S(2)}, u32[]{:S(2)}) collective-permute-start(f32[48,256]{1,0:T(8,128)S(1)} %get-tuple-element.25), channel_id=1, source_target_pairs={{0,1},{1,2},{2,3},{4,5},{5,6},{6,7},{8,9},{9,10},{10,11},{12,13},{... | collective-permute-start | bytes 147464 | tf_op jit(solution)/shard_map/ppermute | solution.py:467
  19.9 6.0 %collective-permute-start.3 = (f32[48,256]{1,0:T(8,128)S(1)}, f32[48,256]{1,0:T(8,128)S(1)}, u32[]{:S(2)}, u32[]{:S(2)}) collective-permute-start(f32[48,256]{1,0:T(8,128)S(1)} %get-tuple-element.26), channel_id=1, source_target_pairs={{1,0},{2,1},{3,2},{5,4},{6,5},{7,6},{9,8},{10,9},{11,10},{13,12},{... | collective-permute-start | bytes 147464 | tf_op jit(solution)/shard_map/ppermute | solution.py:467
  32.4 23.8 %all-to-all-start = ((f32[64,4,128]{2,1,0:T(4,128)}), f32[64,4,128]{2,1,0:T(4,128)S(1)}, u32[]{:S(2)}, u32[]{:S(2)}) async-start(f32[64,4,128]{2,1,0:T(4,128)} %get-tuple-element.28), calls=%async_computation | async-start | bytes 262144 | tf_op jit(solution)/shard_map/all_to_all | solution.py:462
  45.7 4.4 %collective-permute-start.4 = (f32[18,512]{1,0:T(8,128)S(1)}, f32[18,512]{1,0:T(8,128)S(1)}, u32[]{:S(2)}, u32[]{:S(2)}) collective-permute-start(f32[18,512]{1,0:T(8,128)S(1)} %get-tuple-element.30), channel_id=1, source_target_pairs={{0,4},{4,0},{8,12},{12,8},{16,20},{20,16},{24,28},{28,24},{32,36},... | collective-permute-start | bytes 110600 | tf_op jit(solution)/shard_map/ppermute | solution.py:446
  47.7 5.4 %collective-permute-start.5 = (f32[18,512]{1,0:T(8,128)S(1)}, f32[18,512]{1,0:T(8,128)S(1)}, u32[]{:S(2)}, u32[]{:S(2)}) collective-permute-start(f32[18,512]{1,0:T(8,128)S(1)} %get-tuple-element.31), channel_id=1, source_target_pairs={{4,8},{8,4},{12,16},{16,12},{20,24},{24,20},{28,32},{32,28},{36,40... | collective-permute-start | bytes 110600 | tf_op jit(solution)/shard_map/ppermute | solution.py:447
  57.2 19.6 %all-to-all-start.1 = ((f32[8,80,128]{2,1,0:T(8,128)}), f32[8,80,128]{2,1,0:T(8,128)S(1)}, u32[]{:S(2)}, u32[]{:S(2)}) async-start(f32[8,80,128]{2,1,0:T(8,128)} %get-tuple-element.35), calls=%async_computation.1 | async-start | bytes 655360 | tf_op jit(solution)/shard_map/all_to_all | solution.py:462
  63.6 3.9 %collective-permute-start.6 = (f32[32,128]{1,0:T(8,128)S(1)}, f32[32,128]{1,0:T(8,128)S(1)}, u32[]{:S(2)}, u32[]{:S(2)}) collective-permute-start(f32[32,128]{1,0:T(8,128)S(1)} %get-tuple-element.33), channel_id=1, source_target_pairs={{0,1},{1,2},{2,3},{4,5},{5,6},{6,7},{8,9},{9,10},{10,11},{12,13},{... | collective-permute-start | bytes 49160 | tf_op jit(solution)/shard_map/ppermute | solution.py:467
  66.1 5.6 %collective-permute-start.7 = (f32[32,128]{1,0:T(8,128)S(1)}, f32[32,128]{1,0:T(8,128)S(1)}, u32[]{:S(2)}, u32[]{:S(2)}) collective-permute-start(f32[32,128]{1,0:T(8,128)S(1)} %get-tuple-element.34), channel_id=1, source_target_pairs={{1,0},{2,1},{3,2},{5,4},{6,5},{7,6},{9,8},{10,9},{11,10},{13,12},{... | collective-permute-start | bytes 49160 | tf_op jit(solution)/shard_map/ppermute | solution.py:467

commit v4 on v3

--- a/solution.py
+++ b/solution.py
@@ -23,7 +23,6 @@
 RING = 8
 GROUP = 32
 F32, BF16 = jnp.float32, jnp.bfloat16
-MIB = 1024 * 1024
 
 
 def iota(shape, dim):
@@ -86,7 +85,8 @@
         fields[base + 7 : base + 8, :] = cell[step : step + 1, :].astype(F32)
 
 
-def own_kernel(refine, lat_count, controls, move, cell, weight, obs, prec, fields, forcing):
+def own_kernel(refine, lat_count, controls, move, cell, weight, obs, prec, beside, fields, forcing, near):
+    near[...] = beside[...]
     stage(fields, cell, weight, obs)
     for step in range(STEPS):
         row = step * FIELDS + 6
@@ -113,53 +113,78 @@
             forcing[2 * step + c] = dot(high, lat_interp) + dot(low, lat_interp)
 
 
-def pack_kernel(move, cell, weight, obs, prec, init, depth, mixing, inner, outer, beside, fields, east, west):
+def pack_kernel(
+    move_far, cell_far, weight_far, obs_far, prec_far, init_far, depth_far, mixing_far, inner, outer, beside,
+    move, cell, weight, obs, prec, init, depth, mixing, fields, east, west, arrived,
+):
     count = move.shape[1]
-    stage(fields, cell, weight, obs)
-    for step in range(STEPS):
-        fields[step * FIELDS + 6 : step * FIELDS + 7, :] = prec[step : step + 1, :]
-    rows = init.shape[2]
-    planes = [init.at[c, k] for c in range(2) for k in range(DEPTH)]
-    for p in range(PLANES):
-        if p < 2 * DEPTH:
-            first, last = planes[p][:HIGH, :], planes[p][rows - LOW :, :]
-        elif p == 2 * DEPTH:
-            first, last = depth[:HIGH, :].astype(F32), depth[rows - LOW :, :].astype(F32)
-        else:
-            first, last = mixing[:HIGH, :], mixing[rows - LOW :, :]
-        west[3 * FIELDS + HIGH * p : 3 * FIELDS + HIGH * (p + 1), :] = first
-        east[3 * FIELDS + LOW * p : 3 * FIELDS + LOW * (p + 1), :] = last
+    rows = depth_far.shape[0]
+    whole_arrays = [(move_far, move), (cell_far, cell), (weight_far, weight), (obs_far, obs), (prec_far, prec)]
+    edges = []
+    for end, first in enumerate((0, rows - 8)):
+        edges.append((init_far.at[:, :DEPTH, pl.ds(first, 8), :], init.at[end]))
+        edges.append((depth_far.at[pl.ds(first, 8), :], depth.at[end]))
+        edges.append((mixing_far.at[pl.ds(first, 8), :], mixing.at[end]))
+    copies = [pltpu.make_async_copy(far, near, arrived.at[i]) for i, (far, near) in enumerate(whole_arrays + edges)]
+    for copy in copies:
+        copy.start()
+    copies[0].wait()
     width = 256
+    blocks = count // width
     triangle = (iota((width, width), 0) <= iota((width, width), 1)).astype(F32).astype(BF16)
     code = iota((8, 1), 0)
     code = code + (code >= 4).astype(jnp.int32)
-    carry = [jnp.zeros((8, 1), F32) for _ in range(STEPS)]
-    packed = [jnp.zeros((8 * 2 * FIELDS, CAPACITY), F32) for _ in range(STEPS)]
-    slot = iota((CAPACITY, width), 0)
-    for at in range(0, count, width):
-        for step in range(STEPS):
-            match = (move[step : step + 1, at : at + width] == code).astype(F32)
-            rank = dot(match.astype(BF16), triangle) + carry[step]
-            carry[step] = rank[:, width - 1 :]
-            place = jnp.sum(match * (rank - 1.0), axis=0, keepdims=True).astype(jnp.int32)
-            spots = (slot == place).astype(F32).astype(BF16)
-            record = fields[step * FIELDS : (step + 1) * FIELDS, at : at + width]
-            high, low = split(record)
-            both = jnp.concatenate([high.astype(F32), low.astype(F32)], axis=0)
-            masked = jnp.concatenate([both * match[d : d + 1] for d in range(8)], axis=0)
-            packed[step] = packed[step] + dot_lanes(masked.astype(BF16), spots)
-    for step in range(STEPS):
+    matches = []
+    for step in range(STEPS):
+        for block in range(blocks):
+            matches.append((move[step : step + 1, block * width : (block + 1) * width] == code).astype(F32))
+    ranks = dot(jnp.concatenate(matches, axis=0).astype(BF16), triangle)
+    places = []
+    for step in range(STEPS):
+        carry = jnp.full((8, 1), -1.0, F32)
+        for block in range(blocks):
+            at = step * blocks + block
+            rank = ranks[8 * at : 8 * at + 8]
+            places.append(jnp.sum(matches[at] * (rank + carry), axis=0, keepdims=True))
+            carry = carry + rank[:, width - 1 :]
+    for copy in copies[1:]:
+        copy.wait()
+    stage(fields, cell, weight, obs)
+    for step in range(STEPS):
+        fields[step * FIELDS + 6 : step * FIELDS + 7, :] = prec[step : step + 1, :]
+    for p in range(PLANES):
+        for end, strip, first, size in ((0, west, 0, HIGH), (1, east, 8 - LOW, LOW)):
+            if p < 2 * DEPTH:
+                line = init[end, p // DEPTH, p % DEPTH, first : first + size, :]
+            elif p == 2 * DEPTH:
+                line = depth[end, first : first + size, :].astype(F32)
+            else:
+                line = mixing[end, first : first + size, :]
+            strip[3 * FIELDS + size * p : 3 * FIELDS + size * (p + 1), :] = line
+    joined = 2
+    slot = iota((CAPACITY, joined * width), 0).astype(F32).astype(BF16)
+    one, nought = jnp.ones((), BF16), jnp.zeros((), BF16)
+    for step in range(STEPS):
+        packed = jnp.zeros((8 * 2 * FIELDS, CAPACITY), F32)
+        for block in range(0, blocks, joined):
+            at = step * blocks + block
+            place = jnp.concatenate(places[at : at + joined], axis=1).astype(BF16)
+            spots = jnp.where(slot == place, one, nought)
+            lanes = slice(block * width, (block + joined) * width)
+            both = jnp.concatenate(split(fields[step * FIELDS : (step + 1) * FIELDS, lanes]), axis=0)
+            kind = jnp.broadcast_to(move[step : step + 1, lanes].astype(F32), both.shape).astype(BF16)
+            masked = jnp.concatenate([jnp.where(kind == jnp.full((), c, BF16), both, nought) for c in CODES], axis=0)
+            packed = packed + dot_lanes(masked, spots)
         lanes = slice(step * CAPACITY, (step + 1) * CAPACITY)
         for d in range(8):
             at = d * 2 * FIELDS
-            record = packed[step][at : at + FIELDS] + packed[step][at + FIELDS : at + 2 * FIELDS]
-            code = CODES[d]
-            if code // 3 == 1:
-                row = code % 3 // 2 * FIELDS
+            record = packed[at : at + FIELDS] + packed[at + FIELDS : at + 2 * FIELDS]
+            if CODES[d] // 3 == 1:
+                row = CODES[d] % 3 // 2 * FIELDS
                 beside[row : row + FIELDS, lanes] = record
             else:
-                row = (code % 3) * FIELDS
-                (west if code // 3 == 0 else east)[row : row + FIELDS, lanes] = record
+                row = (CODES[d] % 3) * FIELDS
+                (west if CODES[d] // 3 == 0 else east)[row : row + FIELDS, lanes] = record
     address(east, west, inner, outer)
 
 
@@ -252,19 +277,23 @@
                 ahead[c].append(wet[k] * value)
         state = ahead
         surfaces.append([state[0][0], state[1][0]])
-    strip, tiles = rows + 8, rows + 16
     chunk = 512
     lat_of = iota((cells_lat, chunk), 0).astype(F32).astype(BF16)
-    lon_of = iota((strip, chunk), 0).astype(F32)
-    lon_tile = iota((tiles, chunk), 0).astype(F32).astype(BF16)
+    lon_of = iota((rows, chunk), 0).astype(F32)
+    lon_tile = lon_of.astype(BF16)
     one, nought = jnp.ones((), BF16), jnp.zeros((), BF16)
     sources = []
     for step in range(STEPS):
-        views = []
+        views, edges = [], []
         for c in range(2):
-            surface = surfaces[step][c][X0 : X0 + strip]
-            views += [surface[:, Y0 : Y0 + cells_lat], roll(surface, -1, 1)[:, Y0 : Y0 + cells_lat]]
-        views = jnp.concatenate(split(jnp.concatenate(views, axis=0)), axis=0)
+            surface = surfaces[step][c][X0 : X0 + rows + 8]
+            for view in (surface, roll(surface, -1, 1)):
+                views.append(view[:rows, Y0 : Y0 + cells_lat])
+                edges.append(view[rows : rows + 1, Y0 : Y0 + cells_lat])
+        views = jnp.concatenate(views + edges + [jnp.zeros((4, cells_lat), F32)], axis=0)
+        high, low = split(views)
+        views = jnp.concatenate([high.astype(F32), low.astype(F32)], axis=0).astype(BF16)
+        seen_rows = 4 * rows + 8
 
         def spread(record, total):
             cell = record[7:8].astype(jnp.int32)
@@ -272,24 +301,28 @@
             lat = (cell & (cells_lat - 1)).astype(F32).astype(BF16)
             hot = jnp.where(lat_of == lat, one, nought)
             found = dot(views, hot)
-            found = found[: 4 * strip] + found[4 * strip :]
-            here, there = lon_of == lon, lon_of == lon + 1.0
+            found = found[:seen_rows] + found[seen_rows:]
+            here, there, edge = lon_of == lon, lon_of == lon + 1.0, lon == rows - 1.0
             near = jnp.where(here, record[0:1], jnp.where(there, record[1:2], 0.0))
             far = jnp.where(here, record[2:3], jnp.where(there, record[3:4], 0.0))
+            near_edge, far_edge = jnp.where(edge, record[1:2], 0.0), jnp.where(edge, record[3:4], 0.0)
             lon = lon.astype(BF16)
             here, there = lon_tile == lon, lon_tile == lon + one
-            terms = [[], []]
+            terms, outside = [[], []], []
             for c in range(2):
-                at = 2 * c * strip
-                seen = near * found[at : at + strip] + far * found[at + strip : at + 2 * strip]
+                at, last = 2 * c * rows, 4 * rows + 2 * c
+                seen = near * found[at : at + rows] + far * found[at + rows : at + 2 * rows]
                 miss = jnp.sum(seen, axis=0, keepdims=True) - record[4 + c : 5 + c]
+                miss = miss + near_edge * found[last : last + 1] + far_edge * found[last + 1 : last + 2]
                 parts = split(record[0:4] * (record[6:7] * miss))
                 for part, term in zip(parts, terms):
+                    outside.append(jnp.where(edge, part.astype(F32), 0.0))
                     for d in (0, 2):
                         term.append(jnp.where(here, part[d : d + 1], jnp.where(there, part[d + 1 : d + 2], nought)))
-            return total + dot_lanes(jnp.concatenate(terms[0] + terms[1], axis=0), hot)
-
-        total = jnp.zeros((8 * tiles, cells_lat), F32)
+            outside = jnp.concatenate(outside, axis=0).astype(BF16)
+            return total + dot_lanes(jnp.concatenate(terms[0] + terms[1] + [outside], axis=0), hot)
+
+        total = jnp.zeros((8 * rows + 16, cells_lat), F32)
         for at in range(0, fields.shape[1], chunk):
             total = spread(fields[step * FIELDS : (step + 1) * FIELDS, at : at + chunk], total)
         lanes = slice(step * CAPACITY, (step + 1) * CAPACITY)
@@ -298,12 +331,15 @@
         for at in range(0, 8, chunk // CAPACITY):
             total = spread(jnp.concatenate(came[at : at + chunk // CAPACITY], axis=1), total)
         sources.append([])
-        total = total[: 4 * tiles] + total[4 * tiles :]
+        outside = total[8 * rows :]
+        total = total[: 4 * rows] + total[4 * rows : 8 * rows]
         for c in range(2):
-            at = 2 * c * tiles
             spot[...] = jnp.zeros_like(spot)
-            spot[0, X0 : X0 + strip, Y0 : Y0 + cells_lat] = total[at : at + strip]
-            spot[1, X0 : X0 + strip, Y0 : Y0 + cells_lat] = total[at + tiles : at + tiles + strip]
+            for d in range(2):
+                at, last = (2 * c + d) * rows, 8 * c + 2 * d + 1
+                spot[d, X0 : X0 + rows, Y0 : Y0 + cells_lat] = total[at : at + rows]
+                edge = outside[last : last + 1] + outside[last + 4 : last + 5]
+                spot[d, X0 + rows : X0 + rows + 1, Y0 : Y0 + cells_lat] = edge
             sources[step].append(spot[0] + roll(spot[1], 1, 1))
     adjoint = None
     nudges = [None] * STEPS
@@ -471,16 +507,19 @@
     return pl.BlockSpec(shape, lambda i: (0,) * len(shape))
 
 
-def call(kernel, ins, outs, blocks=None, scratch=(), vmem=16):
+def call(kernel, ins, outs, blocks=None, scratch=(), far=False, vmem=16):
     blocks = blocks or {}
+    specs = [whole(blocks.get(i, value.shape)) for i, value in enumerate(ins)]
+    if far:
+        specs = [pl.BlockSpec(memory_space=pltpu.HBM) for _ in ins]
     return pl.pallas_call(
         kernel,
         grid=(1,),
         out_shape=[jax.ShapeDtypeStruct(shape, F32) for shape in outs],
-        in_specs=[whole(blocks.get(i, value.shape)) for i, value in enumerate(ins)],
+        in_specs=specs,
         out_specs=[whole(shape) for shape in outs],
-        scratch_shapes=[pltpu.VMEM(shape, F32) for shape in scratch],
-        compiler_params=pltpu.CompilerParams(vmem_limit_bytes=vmem * MIB),
+        scratch_shapes=[pltpu.VMEM(shape, F32) if isinstance(shape, tuple) else shape for shape in scratch],
+        compiler_params=pltpu.CompilerParams(vmem_limit_bytes=vmem * 1024 * 1024),
     )(*ins)
 
 
@@ -499,15 +538,28 @@
         pack_kernel,
         (drift_move, drift_cell, drift_weight, drift_obs, drift_precision, initial, depth_levels, mixing),
         (lon_message, lon_message, (2 * FIELDS, 256)),
-        {5: surface},
-        scratch=((STEPS * FIELDS, count), lon_message, lon_message),
+        scratch=(
+            pltpu.VMEM(drift_move.shape, jnp.int32),
+            pltpu.VMEM(drift_cell.shape, jnp.int32),
+            drift_weight.shape,
+            drift_obs.shape,
+            drift_precision.shape,
+            (2, 2, DEPTH, 8, cells_lat),
+            pltpu.VMEM((2, 8, cells_lat), jnp.int32),
+            (2, 8, cells_lat),
+            (STEPS * FIELDS, count),
+            lon_message,
+            lon_message,
+            pltpu.SemaphoreType.DMA((11,)),
+        ),
+        far=True,
         vmem=60,
     )
     inner, outer = swap(inner, outer)
-    fields, forcing = call(
+    fields, forcing, beside = call(
         functools.partial(own_kernel, refine, lat_count),
-        (jnp.swapaxes(controls, 2, 3), drift_move, drift_cell, drift_weight, drift_obs, drift_precision),
-        ((STEPS * FIELDS, count), (2 * STEPS, tall, wide)),
+        (jnp.swapaxes(controls, 2, 3), drift_move, drift_cell, drift_weight, drift_obs, drift_precision, beside),
+        ((STEPS * FIELDS, count), (2 * STEPS, tall, wide), (2 * FIELDS, 256)),
     )
     message = (3 * FIELDS + tall // 2, 256)
     padded, south, north = call(
@@ -528,7 +580,7 @@
     )
     shares = gather(share, ring, 1, True)
     inner, outer = swap(inner, outer)
-    height = -(-(4 * ring + 3) // 8) * 8
+    height = -(-(4 * ring + 3) // 4) * 4
     share, own, to_south, to_north = call(
         functools.partial(plane_kernel, lat_count, ctrl_lat // lat_count),
         (shares, partial, inner, outer),

time: 78.6 us -> 73.8 us (0.939)
  Pallas kernels: 14.6 us -> 11.2 us
  waiting for transfers between devices: 21.6 us -> 20.1 us
    pallas_call x6, Pallas kernels: 14.6 us -> 11.2 us  [call(): pl.pallas_call(kernel, grid=(1,), out_shape=[jax.ShapeDtypeStruct(shape,...]
    ppermute x2, waiting for transfers between devices: 5.1 us -> 3.63 us  [swap(): lax.ppermute(outer, 'lon', [((i + 1) % count, ((i ^ 1) + 1) % count) for...]
  transfers between devices with their start and end apart: 10 -> 10, of which waited for: 7 -> 8; matrix products, arithmetic and copies ran while one was open for 0% -> 0% of each run, Pallas kernels for 1% -> 1%
where the time goes in v4:
time: 73.8 us; the launch traced here: 73.2 us
  starting transfers between devices  40.3 us (55%)
  waiting for transfers between devices  20.1 us (27%)
  Pallas kernels  11.2 us (15%)
  between operations  0.86 us (1%)
  local copies, waits for them, and re-layouts  0.75 us (1%)
    all_to_all x2, starting transfers between devices, gather(): lax.all_to_all(copies, ('lon', 'lat'), 0, 0, axis_index_groups=groups, ti...  19.6 us
    pallas_call x6, Pallas kernels, call(): pl.pallas_call(kernel, grid=(1,), out_shape=[jax.ShapeDtypeStruct(shape,...  11.2 us
    ppermute x2, starting transfers between devices, swap(): lax.ppermute(outer, 'lon', [((i + 1) % count, ((i ^ 1) + 1) % count) for...  10.2 us
    ppermute x4, waiting for transfers between devices, along(): lax.ppermute(value, 'lat', [(i, i + distance) for i in range(max(0, -dist...  9.02 us
    all_to_all x2, waiting for transfers between devices, gather(): lax.all_to_all(copies, ('lon', 'lat'), 0, 0, axis_index_groups=groups, ti...  7.49 us
    ppermute x4, starting transfers between devices, along(): lax.ppermute(value, 'lat', [(i, i + distance) for i in range(max(0, -dist...  6.35 us
    ppermute x2, starting transfers between devices, swap(): inner = lax.ppermute(inner, 'lon', [(i, i ^ 1) for i in range(count)])  4.11 us
    ppermute x2, waiting for transfers between devices, swap(): lax.ppermute(outer, 'lon', [((i + 1) % count, ((i ^ 1) + 1) % count) for...  3.63 us
  transfers between devices with their start and end apart: 10, of which 8 were waited for; matrix products, arithmetic and copies ran while one was open for 0% of the time, Pallas kernels for 1%

profile of v4, /device:TPU:8, one launch (start us, length us, event | category | flops | bytes accessed | tf_op | source)
XLA Modules:
  0.0 73.2 jit_solution(7314979814664099729)
XLA Ops:
  0.6 0.0 copy-start.3
  0.6 0.0 copy-start.5
  0.7 0.0 copy-start.1
  0.7 0.0 copy-start.7
  0.7 2.6 %shard_map.104 = (f32[48,256]{1,0:T(8,128)}, f32[48,256]{1,0:T(8,128)}, f32[16,256]{1,0:T(8,128)}) custom-call(s32[2,4096]{1,0:T(2,128)} %move.1, s32[2,4096]{1,0:T(2,128)} %cell.1, f32[4,2,4096]{2,1,0:T(2,128)} %weight.1, f32[2,2,4096]{2,1,0:T(2,128)} %obs.1, f32[2,4096]{1,0:T(2,128)} %precision.1, f32[2,8,32,256]{3,2,1,0:T(8,128)} %init.1, ...), custom_call_target="tpu_custom_call" | custom-call | tf_op jit(solution)/shard_map/pallas_call | solution.py:515
  3.3 0.0 copy-start
  3.3 2.1 %collective-permute-start = (f32[48,256]{1,0:T(8,128)}, f32[48,256]{1,0:T(8,128)S(1)}, u32[]{:S(2)}, u32[]{:S(2)}) collective-permute-start(f32[48,256]{1,0:T(8,128)} %get-tuple-element.24), channel_id=1, source_target_pairs={{0,4},{4,0},{8,12},{12,8},{16,20},{20,16},{24,28},{28,24},{32,36},... | collective-permute-start | bytes 147464 | tf_op jit(solution)/shard_map/ppermute | solution.py:482
  5.4 7.8 %collective-permute-start.1 = (f32[48,256]{1,0:T(8,128)}, f32[48,256]{1,0:T(8,128)S(1)}, u32[]{:S(2)}, u32[]{:S(2)}) collective-permute-start(f32[48,256]{1,0:T(8,128)} %get-tuple-element.25), channel_id=1, source_target_pairs={{4,8},{8,4},{12,16},{16,12},{20,24},{24,20},{28,32},{32,28},{36,40... | collective-permute-start | bytes 147464 | tf_op jit(solution)/shard_map/ppermute | solution.py:483
  13.3 0.7 copy-done.9
  14.0 0.7 shard_map.105
  14.7 0.0 collective-permute-done.inner
  14.7 0.6 collective-permute-done.1.outer
  15.3 0.2 shard_map.106
  15.5 1.3 %collective-permute-start.2 = (f32[48,256]{1,0:T(8,128)S(1)}, f32[48,256]{1,0:T(8,128)S(1)}, u32[]{:S(2)}, u32[]{:S(2)}) collective-permute-start(f32[48,256]{1,0:T(8,128)S(1)} %get-tuple-element.27), channel_id=1, source_target_pairs={{0,1},{1,2},{2,3},{4,5},{5,6},{6,7},{8,9},{9,10},{10,11},{12,13},{... | collective-permute-start | bytes 147464 | tf_op jit(solution)/shard_map/ppermute | solution.py:503
  16.8 1.3 %collective-permute-start.3 = (f32[48,256]{1,0:T(8,128)S(1)}, f32[48,256]{1,0:T(8,128)S(1)}, u32[]{:S(2)}, u32[]{:S(2)}) collective-permute-start(f32[48,256]{1,0:T(8,128)S(1)} %get-tuple-element.28), channel_id=1, source_target_pairs={{1,0},{2,1},{3,2},{5,4},{6,5},{7,6},{9,8},{10,9},{11,10},{13,12},{... | collective-permute-start | bytes 147464 | tf_op jit(solution)/shard_map/ppermute | solution.py:503
  18.1 0.4 collective-permute-done.2.from_south
  18.5 4.3 %collective-permute-done.3.from_north = f32[48,256]{1,0:T(8,128)S(1)} collective-permute-done((f32[48,256]{1,0:T(8,128)S(1)}, f32[48,256]{1,0:T(8,128)S(1)}, u32[]{:S(2)}, u32[]{:S(2)}) %collective-permute-start.3) | collective-permute-done | bytes 49184 | tf_op jit(solution)/shard_map/ppermute | solution.py:503
  22.8 5.5 %shard_map.107 = (f32[6,48,512]{2,1,0:T(8,128)S(1)}, f32[64,4,128]{2,1,0:T(4,128)}, f32[18,512]{1,0:T(8,128)S(1)}, f32[18,512]{1,0:T(8,128)S(1)}) custom-call(f32[4,48,512]{2,1,0:T(8,128)S(1)} %get-tuple-element.22.forcing, f32[16,4096]{1,0:T(8,128)S(1)} %get-tuple-element.23.fields, f32[2,4096]{1,0:T(2,128)S(1)} %copy-done.3, ...), custom_call_target="tpu_custom_call" | custom-call | tf_op jit(solution)/shard_map/pallas_call | solution.py:515
  28.3 13.2 %all-to-all-start = ((f32[64,4,128]{2,1,0:T(4,128)}), f32[64,4,128]{2,1,0:T(4,128)S(1)}, u32[]{:S(2)}, u32[]{:S(2)}) async-start(f32[64,4,128]{2,1,0:T(4,128)} %get-tuple-element.30), calls=%async_computation | async-start | bytes 262144 | tf_op jit(solution)/shard_map/all_to_all | solution.py:498
  41.6 2.1 %collective-permute-start.4 = (f32[18,512]{1,0:T(8,128)S(1)}, f32[18,512]{1,0:T(8,128)S(1)}, u32[]{:S(2)}, u32[]{:S(2)}) collective-permute-start(f32[18,512]{1,0:T(8,128)S(1)} %get-tuple-element.32), channel_id=1, source_target_pairs={{0,4},{4,0},{8,12},{12,8},{16,20},{20,16},{24,28},{28,24},{32,36},... | collective-permute-start | bytes 110600 | tf_op jit(solution)/shard_map/ppermute | solution.py:482
  43.6 2.3 %collective-permute-start.5 = (f32[18,512]{1,0:T(8,128)S(1)}, f32[18,512]{1,0:T(8,128)S(1)}, u32[]{:S(2)}, u32[]{:S(2)}) collective-permute-start(f32[18,512]{1,0:T(8,128)S(1)} %get-tuple-element.33), channel_id=1, source_target_pairs={{4,8},{8,4},{12,16},{16,12},{20,24},{24,20},{28,32},{32,28},{36,40... | collective-permute-start | bytes 110600 | tf_op jit(solution)/shard_map/ppermute | solution.py:483
  46.0 0.0 collective-permute-done.4.inner
  46.0 3.1 %collective-permute-done.5.outer = f32[18,512]{1,0:T(8,128)S(1)} collective-permute-done((f32[18,512]{1,0:T(8,128)S(1)}, f32[18,512]{1,0:T(8,128)S(1)}, u32[]{:S(2)}, u32[]{:S(2)}) %collective-permute-start.5) | collective-permute-done | bytes 36896 | tf_op jit(solution)/shard_map/ppermute | solution.py:483
  49.0 3.1 %all-to-all-done.shares = f32[64,4,128]{2,1,0:T(4,128)S(1)} async-done(((f32[64,4,128]{2,1,0:T(4,128)}), f32[64,4,128]{2,1,0:T(4,128)S(1)}, u32[]{:S(2)}, u32[]{:S(2)}) %all-to-all-start) | async-done | bytes 131104 | tf_op jit(solution)/shard_map/all_to_all | solution.py:498
  52.1 1.0 %shard_map.108 = (f32[8,72,128]{2,1,0:T(8,128)}, f32[6,32,256]{2,1,0:T(8,128)S(1)}, f32[32,128]{1,0:T(8,128)S(1)}, f32[32,128]{1,0:T(8,128)S(1)}) custom-call(f32[64,4,128]{2,1,0:T(4,128)S(1)} %all-to-all-done.shares, f32[6,48,512]{2,1,0:T(8,128)S(1)} %get-tuple-element.31.partial, f32[18,512]{1,0:T(8,128)S(1)} %collective-permute-done.4.inner, ...), custom_call_target="tpu_custom_call" | custom-call | tf_op jit(solution)/shard_map/pallas_call | solution.py:515
  53.1 6.4 %all-to-all-start.1 = ((f32[8,72,128]{2,1,0:T(8,128)}), f32[8,72,128]{2,1,0:T(8,128)S(1)}, u32[]{:S(2)}, u32[]{:S(2)}) async-start(f32[8,72,128]{2,1,0:T(8,128)} %get-tuple-element.37), calls=%async_computation.1 | async-start | bytes 589824 | tf_op jit(solution)/shard_map/all_to_all | solution.py:498
  59.5 2.5 %collective-permute-start.6 = (f32[32,128]{1,0:T(8,128)S(1)}, f32[32,128]{1,0:T(8,128)S(1)}, u32[]{:S(2)}, u32[]{:S(2)}) collective-permute-start(f32[32,128]{1,0:T(8,128)S(1)} %get-tuple-element.35), channel_id=1, source_target_pairs={{0,1},{1,2},{2,3},{4,5},{5,6},{6,7},{8,9},{9,10},{10,11},{12,13},{... | collective-permute-start | bytes 49160 | tf_op jit(solution)/shard_map/ppermute | solution.py:503
  62.0 1.3 %collective-permute-start.7 = (f32[32,128]{1,0:T(8,128)S(1)}, f32[32,128]{1,0:T(8,128)S(1)}, u32[]{:S(2)}, u32[]{:S(2)}) collective-permute-start(f32[32,128]{1,0:T(8,128)S(1)} %get-tuple-element.36), channel_id=1, source_target_pairs={{1,0},{2,1},{3,2},{5,4},{6,5},{7,6},{9,8},{10,9},{11,10},{13,12},{... | collective-permute-start | bytes 49160 | tf_op jit(solution)/shard_map/ppermute | solution.py:503
  63.3 0.1 collective-permute-done.6.from_south
  63.4 4.2 %collective-permute-done.7.from_north = f32[32,128]{1,0:T(8,128)S(1)} collective-permute-done((f32[32,128]{1,0:T(8,128)S(1)}, f32[32,128]{1,0:T(8,128)S(1)}, u32[]{:S(2)}, u32[]{:S(2)}) %collective-permute-start.7) | collective-permute-done | bytes 16416 | tf_op jit(solution)/shard_map/ppermute | solution.py:503
  67.6 4.4 %all-to-all-done.1.shares = f32[8,72,128]{2,1,0:T(8,128)S(1)} async-done(((f32[8,72,128]{2,1,0:T(8,128)}), f32[8,72,128]{2,1,0:T(8,128)S(1)}, u32[]{:S(2)}, u32[]{:S(2)}) %all-to-all-start.1) | async-done | bytes 294944 | tf_op jit(solution)/shard_map/all_to_all | solution.py:498
  72.0 1.2 %shard_map.109 = (f32[2,8,32,256]{3,2,1,0:T(8,128)}, f32[4,2,64,256]{3,2,1,0:T(8,128)}) custom-call(f32[6,32,256]{2,1,0:T(8,128)S(1)} %get-tuple-element.34.own, s32[32,256]{1,0:T(8,128)S(1)} %copy-done.4, f32[32,128]{1,0:T(8,128)S(1)} %collective-permute-done.6.from_south, f32[32,128]{1,0:T(8,128)S(1)} %collective-permute-done.7.from_north, ...), custom_call_target="tpu_custom_call" | custom-call | tf_op jit(solution)/shard_map/pallas_call | solution.py:515
  (14 shorter events, 0.0 us)
Async XLA Ops:
  0.6 12.6 %copy-start.3 = (f32[2,4096]{1,0:T(2,128)S(1)}, f32[2,4096]{1,0:T(2,128)}, u32[]{:S(2)}) copy-start(f32[2,4096]{1,0:T(2,128)} %precision.1) | copy-start | bytes 98308
  0.6 12.6 %copy-start.5 = (f32[2,2,4096]{2,1,0:T(2,128)S(1)}, f32[2,2,4096]{2,1,0:T(2,128)}, u32[]{:S(2)}) copy-start(f32[2,2,4096]{2,1,0:T(2,128)} %obs.1) | copy-start | bytes 196612
  0.7 12.6 %copy-start.1 = (f32[4,2,4096]{2,1,0:T(2,128)S(1)}, f32[4,2,4096]{2,1,0:T(2,128)}, u32[]{:S(2)}) copy-start(f32[4,2,4096]{2,1,0:T(2,128)} %weight.1) | copy-start | bytes 393220
  0.7 12.6 %copy-start.7 = (s32[2,4096]{1,0:T(2,128)S(1)}, s32[2,4096]{1,0:T(2,128)}, u32[]{:S(2)}) copy-start(s32[2,4096]{1,0:T(2,128)} %cell.1) | copy-start | bytes 98308
  0.7 12.6 %copy-start.6 = (s32[2,4096]{1,0:T(2,128)S(1)}, s32[2,4096]{1,0:T(2,128)}, u32[]{:S(2)}) copy-start(s32[2,4096]{1,0:T(2,128)} %move.1) | copy-start | bytes 98308
  0.7 12.6 %copy-start.2 = (f32[4,2,256,64]{2,3,1,0:T(8,128)S(1)}, f32[4,2,256,64]{2,3,1,0:T(8,128)}, u32[]{:S(2)}) copy-start(f32[4,2,256,64]{2,3,1,0:T(8,128)} %param.12) | copy-start | bytes 1572868
  3.3 12.0 %copy-start = (f32[2,8,32,256]{3,2,1,0:T(8,128)S(1)}, f32[2,8,32,256]{3,2,1,0:T(8,128)}, u32[]{:S(2)}) copy-start(f32[2,8,32,256]{3,2,1,0:T(8,128)} %init.1) | copy-start | bytes 1572868
  3.3 11.4 %collective-permute-start = (f32[48,256]{1,0:T(8,128)}, f32[48,256]{1,0:T(8,128)S(1)}, u32[]{:S(2)}, u32[]{:S(2)}) collective-permute-start(f32[48,256]{1,0:T(8,128)} %get-tuple-element.24), channel_id=1, source_target_pairs={{0,4},{4,0},{8,12},{12,8},{16,20},{20,16},{24,28},{28,24},{32,36},... | collective-permute-start | bytes 147464 | tf_op jit(solution)/shard_map/ppermute | solution.py:482
  5.4 9.9 %collective-permute-start.1 = (f32[48,256]{1,0:T(8,128)}, f32[48,256]{1,0:T(8,128)S(1)}, u32[]{:S(2)}, u32[]{:S(2)}) collective-permute-start(f32[48,256]{1,0:T(8,128)} %get-tuple-element.25), channel_id=1, source_target_pairs={{4,8},{8,4},{12,16},{16,12},{20,24},{24,20},{28,32},{32,28},{36,40... | collective-permute-start | bytes 147464 | tf_op jit(solution)/shard_map/ppermute | solution.py:483
  13.3 0.7 copy-start.9
  14.0 1.3 %copy-start.4 = (s32[32,256]{1,0:T(8,128)S(1)}, s32[32,256]{1,0:T(8,128)}, u32[]{:S(2)}) copy-start(s32[32,256]{1,0:T(8,128)} %depth.3) | copy-start | bytes 98308
  14.0 1.3 %copy-start.8 = (f32[32,256]{1,0:T(8,128)S(1)}, f32[32,256]{1,0:T(8,128)}, u32[]{:S(2)}) copy-start(f32[32,256]{1,0:T(8,128)} %mixing.1) | copy-start | bytes 98308
  15.5 3.0 %collective-permute-start.2 = (f32[48,256]{1,0:T(8,128)S(1)}, f32[48,256]{1,0:T(8,128)S(1)}, u32[]{:S(2)}, u32[]{:S(2)}) collective-permute-start(f32[48,256]{1,0:T(8,128)S(1)} %get-tuple-element.27), channel_id=1, source_target_pairs={{0,1},{1,2},{2,3},{4,5},{5,6},{6,7},{8,9},{9,10},{10,11},{12,13},{... | collective-permute-start | bytes 147464 | tf_op jit(solution)/shard_map/ppermute | solution.py:503
  16.8 6.0 %collective-permute-start.3 = (f32[48,256]{1,0:T(8,128)S(1)}, f32[48,256]{1,0:T(8,128)S(1)}, u32[]{:S(2)}, u32[]{:S(2)}) collective-permute-start(f32[48,256]{1,0:T(8,128)S(1)} %get-tuple-element.28), channel_id=1, source_target_pairs={{1,0},{2,1},{3,2},{5,4},{6,5},{7,6},{9,8},{10,9},{11,10},{13,12},{... | collective-permute-start | bytes 147464 | tf_op jit(solution)/shard_map/ppermute | solution.py:503
  28.3 23.8 %all-to-all-start = ((f32[64,4,128]{2,1,0:T(4,128)}), f32[64,4,128]{2,1,0:T(4,128)S(1)}, u32[]{:S(2)}, u32[]{:S(2)}) async-start(f32[64,4,128]{2,1,0:T(4,128)} %get-tuple-element.30), calls=%async_computation | async-start | bytes 262144 | tf_op jit(solution)/shard_map/all_to_all | solution.py:498
  41.6 4.4 %collective-permute-start.4 = (f32[18,512]{1,0:T(8,128)S(1)}, f32[18,512]{1,0:T(8,128)S(1)}, u32[]{:S(2)}, u32[]{:S(2)}) collective-permute-start(f32[18,512]{1,0:T(8,128)S(1)} %get-tuple-element.32), channel_id=1, source_target_pairs={{0,4},{4,0},{8,12},{12,8},{16,20},{20,16},{24,28},{28,24},{32,36},... | collective-permute-start | bytes 110600 | tf_op jit(solution)/shard_map/ppermute | solution.py:482
  43.6 5.4 %collective-permute-start.5 = (f32[18,512]{1,0:T(8,128)S(1)}, f32[18,512]{1,0:T(8,128)S(1)}, u32[]{:S(2)}, u32[]{:S(2)}) collective-permute-start(f32[18,512]{1,0:T(8,128)S(1)} %get-tuple-element.33), channel_id=1, source_target_pairs={{4,8},{8,4},{12,16},{16,12},{20,24},{24,20},{28,32},{32,28},{36,40... | collective-permute-start | bytes 110600 | tf_op jit(solution)/shard_map/ppermute | solution.py:483
  53.1 18.9 %all-to-all-start.1 = ((f32[8,72,128]{2,1,0:T(8,128)}), f32[8,72,128]{2,1,0:T(8,128)S(1)}, u32[]{:S(2)}, u32[]{:S(2)}) async-start(f32[8,72,128]{2,1,0:T(8,128)} %get-tuple-element.37), calls=%async_computation.1 | async-start | bytes 589824 | tf_op jit(solution)/shard_map/all_to_all | solution.py:498
  59.5 3.9 %collective-permute-start.6 = (f32[32,128]{1,0:T(8,128)S(1)}, f32[32,128]{1,0:T(8,128)S(1)}, u32[]{:S(2)}, u32[]{:S(2)}) collective-permute-start(f32[32,128]{1,0:T(8,128)S(1)} %get-tuple-element.35), channel_id=1, source_target_pairs={{0,1},{1,2},{2,3},{4,5},{5,6},{6,7},{8,9},{9,10},{10,11},{12,13},{... | collective-permute-start | bytes 49160 | tf_op jit(solution)/shard_map/ppermute | solution.py:503
  62.0 5.6 %collective-permute-start.7 = (f32[32,128]{1,0:T(8,128)S(1)}, f32[32,128]{1,0:T(8,128)S(1)}, u32[]{:S(2)}, u32[]{:S(2)}) collective-permute-start(f32[32,128]{1,0:T(8,128)S(1)} %get-tuple-element.36), channel_id=1, source_target_pairs={{1,0},{2,1},{3,2},{5,4},{6,5},{7,6},{9,8},{10,9},{11,10},{13,12},{... | collective-permute-start | bytes 49160 | tf_op jit(solution)/shard_map/ppermute | solution.py:503

commit v5 on v4

--- a/solution.py
+++ b/solution.py
@@ -46,20 +46,20 @@
     return pltpu.roll(value, shift % value.shape[axis], axis)
 
 
-def parity():
-    return lax.axis_index("lon") % CORES
-
-
-def pick(first, second):
-    even = parity() == 0
-    inner, outer = first[...], second[...]
-    return jnp.where(even, outer, inner), jnp.where(even, inner, outer)
-
-
-def address(east, west, first, second):
-    even = parity() == 0
-    first[...] = jnp.where(even, east[...], west[...])
-    second[...] = jnp.where(even, west[...], east[...])
+def parity(axis):
+    return lax.axis_index(axis) % 2
+
+
+def pick(axis, first, second):
+    even = parity(axis) == 0
+    one, other = first[...], second[...]
+    return jnp.where(even, other, one), jnp.where(even, one, other)
+
+
+def address(axis, behind, ahead, first, second):
+    even = parity(axis) == 0
+    first[...] = jnp.where(even, ahead[...], behind[...])
+    second[...] = jnp.where(even, behind[...], ahead[...])
 
 
 def interpolation(offset, refine):
@@ -85,8 +85,7 @@
         fields[base + 7 : base + 8, :] = cell[step : step + 1, :].astype(F32)
 
 
-def own_kernel(refine, lat_count, controls, move, cell, weight, obs, prec, beside, fields, forcing, near):
-    near[...] = beside[...]
+def own_kernel(refine, lat_count, controls, move, cell, weight, obs, prec, fields, forcing):
     stage(fields, cell, weight, obs)
     for step in range(STEPS):
         row = step * FIELDS + 6
@@ -111,6 +110,10 @@
             high, low = split(blended)
             high, low = split(dot_lanes(lon_interp, high) + dot_lanes(lon_interp, low))
             forcing[2 * step + c] = dot(high, lat_interp) + dot(low, lat_interp)
+
+
+def near_kernel(beside, near):
+    near[...] = beside[...]
 
 
 def pack_kernel(
@@ -185,7 +188,7 @@
             else:
                 row = (CODES[d] % 3) * FIELDS
                 (west if CODES[d] // 3 == 0 else east)[row : row + FIELDS, lanes] = record
-    address(east, west, inner, outer)
+    address("lon", west, east, inner, outer)
 
 
 def extend_lon(ext, p, own, from_west, from_east, rows, cells_lat):
@@ -197,8 +200,8 @@
     ext[p, X0 + rows : X0 + rows + HIGH, lanes] = from_east[at : at + HIGH, :]
 
 
-def merge_kernel(init, depth, mixing, beside, inner, outer, ext, south, north):
-    from_west, from_east = pick(inner, outer)
+def merge_kernel(init, depth, mixing, beside, outer, inner, ext, first_out, second_out, south, north):
+    from_west, from_east = pick("lon", inner, outer)
     rows, cells_lat = depth.shape
     ext[...] = jnp.zeros_like(ext)
     for p in range(PLANES):
@@ -220,8 +223,11 @@
         out[0:FIELDS, :] = beside[kept * FIELDS : (kept + 1) * FIELDS, :]
         out[FIELDS : 2 * FIELDS, :] = from_west[row * FIELDS : (row + 1) * FIELDS, :]
         out[2 * FIELDS : 3 * FIELDS, :] = from_east[row * FIELDS : (row + 1) * FIELDS, :]
-        out[3 * FIELDS :, 0:128] = strip[: tall // 2]
-        out[3 * FIELDS :, 128:] = strip[tall // 2 :]
+        third = tall // 3
+        strip = strip[:third] + roll(strip[third : 2 * third], 32, 1) + roll(strip[2 * third :], 64, 1)
+        out[3 * FIELDS :, 0:128] = strip[: third // 2]
+        out[3 * FIELDS :, 128:] = strip[third // 2 :]
+    address("lat", south, north, first_out, second_out)
 
 
 def lap(v):
@@ -245,18 +251,21 @@
 
 
 def main_kernel(
-    levels, refine, lat_count, forcing, fields, precision, inner, outer, from_south, from_north,
+    levels, refine, lat_count, forcing, fields, precision, outer, inner, first, second,
     padded, partial, share, to_inner, to_outer, ext, spot, to_west, to_east,
 ):
-    from_west, from_east = pick(inner, outer)
+    from_west, from_east = pick("lon", inner, outer)
+    from_south, from_north = pick("lat", first, second)
     rows, cells_lat = partial.shape[1] - 16, partial.shape[2] - 256
     tall, wide = ext.shape[1:]
     lat_index = lax.axis_index("lat")
     grid_lat = cells_lat * lat_count
     lane = iota((tall, 128), 1)
-    half = tall // 2
-    below = jnp.concatenate([from_south[3 * FIELDS :, 0:128], from_south[3 * FIELDS :, 128:]], axis=0)
-    above = jnp.concatenate([from_north[3 * FIELDS :, 0:128], from_north[3 * FIELDS :, 128:]], axis=0)
+    below, above = [
+        jnp.concatenate([message[3 * FIELDS :, 0:128], message[3 * FIELDS :, 128:]], axis=0)
+        for message in (from_south, from_north)
+    ]
+    below, above = [jnp.concatenate([v, roll(v, -32, 1), roll(v, -64, 1)], axis=0) for v in (below, above)]
     full = []
     for p in range(PLANES):
         left = jnp.where(lane >= 128 - LOW, roll(below, LOW * p, 1), 0.0)
@@ -365,7 +374,7 @@
             partial[p] = adjoint[c][k]
             to_west[LOW * p : LOW * (p + 1), :] = ext[p, X0 - LOW : X0, :]
             to_east[HIGH * p : HIGH * (p + 1), :] = ext[p, X0 + rows : X0 + rows + HIGH, :]
-    address(to_east, to_west, to_inner, to_outer)
+    address("lon", to_west, to_east, to_inner, to_outer)
     low, part = interpolation(iota((wide, 4 * GROUP), 0) - Y0 - refine // 2, refine)
     column = iota((wide, 4 * GROUP), 1) % GROUP - 1
     onto_lat = jnp.where(column == low, 1.0 - part, 0.0) + jnp.where(column == low + 1, part, 0.0)
@@ -384,8 +393,8 @@
     share[...] = jnp.broadcast_to(jnp.concatenate(parts, axis=0)[None], share.shape)
 
 
-def plane_kernel(lat_count, per, shares, partial, inner, outer, out, own, south, north, rows, total):
-    join(partial, inner, outer, own, south, north)
+def plane_kernel(lat_count, per, shares, partial, outer, inner, out, own, first, second, rows, total):
+    join(partial, inner, outer, own, first, second)
     members = shares.shape[0]
     ring = members // (CORES * lat_count)
     ctrl_lat = per * lat_count
@@ -418,8 +427,8 @@
     out[...] = jnp.broadcast_to(total[...][None], out.shape)
 
 
-def join(partial, inner, outer, own, south, north):
-    from_west, from_east = pick(inner, outer)
+def join(partial, inner, outer, own, first_out, second_out):
+    from_west, from_east = pick("lon", inner, outer)
     rows, cells_lat = own.shape[1:]
     lane = iota((rows, 128), 1)
     first = jnp.zeros((rows, 128), F32)
@@ -433,11 +442,11 @@
         head = jnp.where(lane < HIGH, block[:, Y0 + cells_lat : Y0 + cells_lat + 128], 0.0)
         first = first + roll(tail, -LOW * p, 1)
         last = last + roll(head, HIGH * p, 1)
-    south[...] = first
-    north[...] = last
-
-
-def finish_kernel(normalizer, own, depth, from_south, from_north, shares, grad, out, full):
+    address("lat", first, last, first_out, second_out)
+
+
+def finish_kernel(normalizer, own, depth, first, second, shares, grad, out, full):
+    from_south, from_north = pick("lat", first, second)
     levels, rows, cells_lat = grad.shape[1:]
     periods, _, ctrl_lat, ctrl_lon = out.shape
     table = period_weights(STEPS, periods)
@@ -455,8 +464,8 @@
                 grad[c, k] = jnp.zeros((rows, cells_lat), F32)
                 continue
             p = c * DEPTH + k
-            low = jnp.where(side < HIGH, roll(from_south[...], -HIGH * p, 1), 0.0)
-            high = jnp.where(side >= 128 - LOW, roll(from_north[...], LOW * p, 1), 0.0)
+            low = jnp.where(side < HIGH, roll(from_south, -HIGH * p, 1), 0.0)
+            high = jnp.where(side >= 128 - LOW, roll(from_north, LOW * p, 1), 0.0)
             value = own[p] + jnp.concatenate([low, high], axis=1)
             grad[c, k] = jnp.where(wet_levels > k, value * scale, 0.0)
     for step in range(STEPS):
@@ -477,11 +486,14 @@
             out[period, c] = value[c * ctrl_lat : (c + 1) * ctrl_lat]
 
 
-def swap(inner, outer):
-    count = lax.axis_size("lon")
-    inner = lax.ppermute(inner, "lon", [(i, i ^ 1) for i in range(count)])
-    outer = lax.ppermute(outer, "lon", [((i + 1) % count, ((i ^ 1) + 1) % count) for i in range(count)])
-    return inner, outer
+def swap(axis, first, second, periodic):
+    count = lax.axis_size(axis)
+    across = [(i, i + 1) for i in range(1, count - 1, 2)]
+    if periodic:
+        across.append((count - 1, 0))
+    second = lax.ppermute(second, axis, across + [(b, a) for a, b in across])
+    first = lax.ppermute(first, axis, [(i, i ^ 1) for i in range(count)])
+    return first, second
 
 
 def gather(copies, chips, stride, whole_chips):
@@ -496,11 +508,6 @@
             for few in inside:
                 groups.append([(base + chip * stride) * per_chip + i for chip in range(chips) for i in few])
     return lax.all_to_all(copies, ("lon", "lat"), 0, 0, axis_index_groups=groups, tiled=True)
-
-
-def along(value, distance):
-    count = lax.axis_size("lat")
-    return lax.ppermute(value, "lat", [(i, i + distance) for i in range(max(0, -distance), min(count, count - distance))])
 
 
 def whole(shape):
@@ -555,43 +562,45 @@
         far=True,
         vmem=60,
     )
-    inner, outer = swap(inner, outer)
-    fields, forcing, beside = call(
+    inner, outer = swap("lon", inner, outer, True)
+    fields, forcing = call(
         functools.partial(own_kernel, refine, lat_count),
-        (jnp.swapaxes(controls, 2, 3), drift_move, drift_cell, drift_weight, drift_obs, drift_precision, beside),
-        ((STEPS * FIELDS, count), (2 * STEPS, tall, wide), (2 * FIELDS, 256)),
+        (jnp.swapaxes(controls, 2, 3), drift_move, drift_cell, drift_weight, drift_obs, drift_precision),
+        ((STEPS * FIELDS, count), (2 * STEPS, tall, wide)),
     )
-    message = (3 * FIELDS + tall // 2, 256)
-    padded, south, north = call(
+    message = (3 * FIELDS + tall // 6, 256)
+    (beside,) = call(near_kernel, (beside,), ((2 * FIELDS, 256),))
+    padded, first, second = call(
         merge_kernel,
-        (initial, depth_levels, mixing, beside, inner, outer),
+        (initial, depth_levels, mixing, beside, outer, inner),
         ((PLANES, tall, wide), message, message),
         {0: surface},
+        scratch=(message, message),
     )
-    from_south, from_north = along(north, 1), along(south, -1)
+    first, second = swap("lat", first, second, False)
     edge = (2 * DEPTH * HIGH, wide)
     ring = min(RING, lon_count // CORES)
     members = lon_count // (CORES * ring)
     partial, share, inner, outer = call(
         functools.partial(main_kernel, levels, refine, lat_count),
-        (forcing, fields, drift_precision, inner, outer, from_south, from_north, padded),
+        (forcing, fields, drift_precision, outer, inner, first, second, padded),
         ((2 * DEPTH, tall, wide), (ring * CORES * lat_count, 2 * STEPS, 4 * GROUP), edge, edge),
         scratch=((2 * DEPTH, tall, wide), (2, tall, wide), edge, edge),
     )
     shares = gather(share, ring, 1, True)
-    inner, outer = swap(inner, outer)
+    inner, outer = swap("lon", inner, outer, True)
     height = -(-(4 * ring + 3) // 4) * 4
-    share, own, to_south, to_north = call(
+    share, own, first, second = call(
         functools.partial(plane_kernel, lat_count, ctrl_lat // lat_count),
-        (shares, partial, inner, outer),
+        (shares, partial, outer, inner),
         ((members, STEPS * height, 2 * ctrl_lat), (2 * DEPTH, rows, cells_lat), (rows, 128), (rows, 128)),
         scratch=((4 * ring * CORES * lat_count, 4 * GROUP), (STEPS * height, 2 * ctrl_lat)),
     )
-    from_south, from_north = along(to_north, 1), along(to_south, -1)
+    first, second = swap("lat", first, second, False)
     shares = gather(share, members, ring, False)
     grad_initial, grad_controls = call(
         functools.partial(finish_kernel, float(STEPS * count * lon_count * lat_count)),
-        (own, depth_levels, from_south, from_north, shares),
+        (own, depth_levels, first, second, shares),
         (initial.shape, (periods, 2, ctrl_lat, ctrl_lon)),
         scratch=((STEPS, ctrl_lon, 2 * ctrl_lat),),
     )

time: 73.8 us -> 71.7 us (0.972)
  waiting for transfers between devices: 20.1 us -> 15.8 us
  starting transfers between devices: 40.3 us -> 42.5 us
    ppermute x8, waiting for transfers between devices: 12.6 us -> 4.62 us  [the longest x4 4.22 us: swap(): first = lax.ppermute(first, axis, [(i, i ^ 1) for i in range(count)])]
    all_to_all x2, starting transfers between devices: 19.6 us -> 24.3 us  [gather(): lax.all_to_all(copies, ('lon', 'lat'), 0, 0, axis_index_groups=groups, ti...]
    all_to_all x2, waiting for transfers between devices: 7.49 us -> 11.2 us  [gather(): lax.all_to_all(copies, ('lon', 'lat'), 0, 0, axis_index_groups=groups, ti...]
    ppermute x8, starting transfers between devices: 20.6 us -> 18.2 us  [the longest x4 12.8 us: swap(): first = lax.ppermute(first, axis, [(i, i ^ 1) for i in range(count)])]
    pallas_call x6 -> x7, Pallas kernels: 11.2 us -> 11.2 us  [call(): pl.pallas_call(kernel, grid=(1,), out_shape=[jax.ShapeDtypeStruct(shape,...]
  transfers between devices with their start and end apart: 10 -> 10, of which waited for: 8 -> 7; matrix products, arithmetic and copies ran while one was open for 0% -> 0% of each run, Pallas kernels for 1% -> 1%
where the time goes in v5:
time: 71.7 us; the launch traced here: 71.2 us
  starting transfers between devices  42.5 us (59%)
  waiting for transfers between devices  15.8 us (22%)
  Pallas kernels  11.2 us (16%)
  between operations  0.84 us (1%)
  local copies, waits for them, and re-layouts  0.75 us (1%)
    all_to_all x2, starting transfers between devices, gather(): lax.all_to_all(copies, ('lon', 'lat'), 0, 0, axis_index_groups=groups, ti...  24.3 us
    ppermute x4, starting transfers between devices, swap(): first = lax.ppermute(first, axis, [(i, i ^ 1) for i in range(count)])  12.8 us
    pallas_call x7, Pallas kernels, call(): pl.pallas_call(kernel, grid=(1,), out_shape=[jax.ShapeDtypeStruct(shape,...  11.2 us
    all_to_all x2, waiting for transfers between devices, gather(): lax.all_to_all(copies, ('lon', 'lat'), 0, 0, axis_index_groups=groups, ti...  11.2 us
    ppermute x4, starting transfers between devices, swap(): second = lax.ppermute(second, axis, across + [(b, a) for a, b in across])  5.4 us
    ppermute x4, waiting for transfers between devices, swap(): first = lax.ppermute(first, axis, [(i, i ^ 1) for i in range(count)])  4.22 us
  transfers between devices with their start and end apart: 10, of which 7 were waited for; matrix products, arithmetic and copies ran while one was open for 0% of the time, Pallas kernels for 1%

profile of v5, /device:TPU:8, one launch (start us, length us, event | category | flops | bytes accessed | tf_op | source)
XLA Modules:
  0.0 71.2 jit_solution(10488176491663896625)
XLA Ops:
  0.6 0.0 copy-start
  0.6 0.0 copy-start.4
  0.7 0.0 copy-start.6
  0.7 0.0 copy-start.5
  0.7 2.6 %shard_map.105 = (f32[48,256]{1,0:T(8,128)}, f32[48,256]{1,0:T(8,128)}, f32[16,256]{1,0:T(8,128)}) custom-call(s32[2,4096]{1,0:T(2,128)} %move_far.1, s32[2,4096]{1,0:T(2,128)} %cell_far.1, f32[4,2,4096]{2,1,0:T(2,128)} %weight_far.1, f32[2,2,4096]{2,1,0:T(2,128)} %obs_far.1, f32[2,4096]{1,0:T(2,128)} %precision.1, f32[2,8,32,256]{3,2,1,0:T(8,128)} %init.1, ...), custom_call_target="tpu_custom_call" | custom-call | tf_op jit(solution)/shard_map/pallas_call | solution.py:522
  3.3 0.0 copy-start.2
  3.3 2.1 %collective-permute-start = (f32[48,256]{1,0:T(8,128)}, f32[48,256]{1,0:T(8,128)S(1)}, u32[]{:S(2)}, u32[]{:S(2)}) collective-permute-start(f32[48,256]{1,0:T(8,128)} %get-tuple-element.22), channel_id=1, source_target_pairs={{4,8},{12,16},{20,24},{28,32},{36,40},{44,48},{52,56},{60,64},{68,... | collective-permute-start | bytes 147464 | tf_op jit(solution)/shard_map/ppermute | solution.py:494
  5.3 3.6 %collective-permute-start.1 = (f32[48,256]{1,0:T(8,128)}, f32[48,256]{1,0:T(8,128)S(1)}, u32[]{:S(2)}, u32[]{:S(2)}) collective-permute-start(f32[48,256]{1,0:T(8,128)} %get-tuple-element.23), channel_id=1, source_target_pairs={{0,4},{4,0},{8,12},{12,8},{16,20},{20,16},{24,28},{28,24},{32,36},... | collective-permute-start | bytes 147464 | tf_op jit(solution)/shard_map/ppermute | solution.py:495
  8.9 0.7 copy-done.9
  9.7 0.0 collective-permute-done.outer
  9.7 0.3 collective-permute-done.1.inner
  10.0 0.2 shard_map.107
  10.3 3.4 %collective-permute-start.2 = (f32[32,256]{1,0:T(8,128)S(1)}, f32[32,256]{1,0:T(8,128)S(1)}, u32[]{:S(2)}, u32[]{:S(2)}) collective-permute-start(f32[32,256]{1,0:T(8,128)S(1)} %get-tuple-element.25), channel_id=1, source_target_pairs={{0,1},{1,0},{2,3},{3,2},{4,5},{5,4},{6,7},{7,6},{8,9},{9,8},{10,11... | collective-permute-start | bytes 98312 | tf_op jit(solution)/shard_map/ppermute | solution.py:495
  13.7 0.7 collective-permute-start.3
  14.4 0.7 shard_map.104
  15.1 1.0 %collective-permute-done.2.first = f32[32,256]{1,0:T(8,128)S(1)} collective-permute-done((f32[32,256]{1,0:T(8,128)S(1)}, f32[32,256]{1,0:T(8,128)S(1)}, u32[]{:S(2)}, u32[]{:S(2)}) %collective-permute-start.2) | collective-permute-done | bytes 32800 | tf_op jit(solution)/shard_map/ppermute | solution.py:495
  16.1 0.0 collective-permute-done.3.second
  16.1 5.5 %shard_map.108 = (f32[6,48,512]{2,1,0:T(8,128)S(1)}, f32[64,4,128]{2,1,0:T(4,128)}, f32[18,512]{1,0:T(8,128)S(1)}, f32[18,512]{1,0:T(8,128)S(1)}) custom-call(f32[4,48,512]{2,1,0:T(8,128)S(1)} %get-tuple-element.20.forcing, f32[16,4096]{1,0:T(8,128)S(1)} %get-tuple-element.21.fields, f32[2,4096]{1,0:T(2,128)S(1)} %copy-done.3, ...), custom_call_target="tpu_custom_call" | custom-call | tf_op jit(solution)/shard_map/pallas_call | solution.py:522
  21.6 18.5 %all-to-all-start = ((f32[64,4,128]{2,1,0:T(4,128)}), f32[64,4,128]{2,1,0:T(4,128)S(1)}, u32[]{:S(2)}, u32[]{:S(2)}) async-start(f32[64,4,128]{2,1,0:T(4,128)} %get-tuple-element.28), calls=%async_computation | async-start | bytes 262144 | tf_op jit(solution)/shard_map/all_to_all | solution.py:510
  40.1 2.0 %collective-permute-start.4 = (f32[18,512]{1,0:T(8,128)S(1)}, f32[18,512]{1,0:T(8,128)S(1)}, u32[]{:S(2)}, u32[]{:S(2)}) collective-permute-start(f32[18,512]{1,0:T(8,128)S(1)} %get-tuple-element.30), channel_id=1, source_target_pairs={{4,8},{12,16},{20,24},{28,32},{36,40},{44,48},{52,56},{60,64},{68,... | collective-permute-start | bytes 110600 | tf_op jit(solution)/shard_map/ppermute | solution.py:494
  42.1 3.4 %collective-permute-start.5 = (f32[18,512]{1,0:T(8,128)S(1)}, f32[18,512]{1,0:T(8,128)S(1)}, u32[]{:S(2)}, u32[]{:S(2)}) collective-permute-start(f32[18,512]{1,0:T(8,128)S(1)} %get-tuple-element.31), channel_id=1, source_target_pairs={{0,4},{4,0},{8,12},{12,8},{16,20},{20,16},{24,28},{28,24},{32,36},... | collective-permute-start | bytes 110600 | tf_op jit(solution)/shard_map/ppermute | solution.py:495
  45.5 0.4 collective-permute-done.4.outer
  45.9 0.5 collective-permute-done.5.inner
  46.3 4.3 %all-to-all-done.shares = f32[64,4,128]{2,1,0:T(4,128)S(1)} async-done(((f32[64,4,128]{2,1,0:T(4,128)}), f32[64,4,128]{2,1,0:T(4,128)S(1)}, u32[]{:S(2)}, u32[]{:S(2)}) %all-to-all-start) | async-done | bytes 131104 | tf_op jit(solution)/shard_map/all_to_all | solution.py:510
  50.6 1.0 %shard_map.109 = (f32[8,72,128]{2,1,0:T(8,128)}, f32[6,32,256]{2,1,0:T(8,128)S(1)}, f32[32,128]{1,0:T(8,128)S(1)}, f32[32,128]{1,0:T(8,128)S(1)}) custom-call(f32[64,4,128]{2,1,0:T(4,128)S(1)} %all-to-all-done.shares, f32[6,48,512]{2,1,0:T(8,128)S(1)} %get-tuple-element.29.partial, f32[18,512]{1,0:T(8,128)S(1)} %collective-permute-done.4.outer, ...), custom_call_target="tpu_custom_call" | custom-call | tf_op jit(solution)/shard_map/pallas_call | solution.py:522
  51.6 5.8 %all-to-all-start.1 = ((f32[8,72,128]{2,1,0:T(8,128)}), f32[8,72,128]{2,1,0:T(8,128)S(1)}, u32[]{:S(2)}, u32[]{:S(2)}) async-start(f32[8,72,128]{2,1,0:T(8,128)} %get-tuple-element.35), calls=%async_computation.1 | async-start | bytes 589824 | tf_op jit(solution)/shard_map/all_to_all | solution.py:510
  57.4 2.5 %collective-permute-start.6 = (f32[32,128]{1,0:T(8,128)S(1)}, f32[32,128]{1,0:T(8,128)S(1)}, u32[]{:S(2)}, u32[]{:S(2)}) collective-permute-start(f32[32,128]{1,0:T(8,128)S(1)} %get-tuple-element.33), channel_id=1, source_target_pairs={{0,1},{1,0},{2,3},{3,2},{4,5},{5,4},{6,7},{7,6},{8,9},{9,8},{10,11... | collective-permute-start | bytes 49160 | tf_op jit(solution)/shard_map/ppermute | solution.py:495
  59.9 0.7 collective-permute-start.7
  60.6 2.5 %collective-permute-done.6.first = f32[32,128]{1,0:T(8,128)S(1)} collective-permute-done((f32[32,128]{1,0:T(8,128)S(1)}, f32[32,128]{1,0:T(8,128)S(1)}, u32[]{:S(2)}, u32[]{:S(2)}) %collective-permute-start.6) | collective-permute-done | bytes 16416 | tf_op jit(solution)/shard_map/ppermute | solution.py:495
  63.0 0.0 collective-permute-done.7.second
  63.0 6.9 %all-to-all-done.1.shares = f32[8,72,128]{2,1,0:T(8,128)S(1)} async-done(((f32[8,72,128]{2,1,0:T(8,128)}), f32[8,72,128]{2,1,0:T(8,128)S(1)}, u32[]{:S(2)}, u32[]{:S(2)}) %all-to-all-start.1) | async-done | bytes 294944 | tf_op jit(solution)/shard_map/all_to_all | solution.py:510
  70.0 1.2 %shard_map.110 = (f32[2,8,32,256]{3,2,1,0:T(8,128)}, f32[4,2,64,256]{3,2,1,0:T(8,128)}) custom-call(f32[6,32,256]{2,1,0:T(8,128)S(1)} %get-tuple-element.32.own, s32[32,256]{1,0:T(8,128)S(1)} %copy-done.4, f32[32,128]{1,0:T(8,128)S(1)} %collective-permute-done.6.first, f32[32,128]{1,0:T(8,128)S(1)} %collective-permute-done.7.second, ...), custom_call_target="tpu_custom_call" | custom-call | tf_op jit(solution)/shard_map/pallas_call | solution.py:522
  (15 shorter events, 0.0 us)
Async XLA Ops:
  0.6 9.4 %copy-start = (f32[2,8,32,256]{3,2,1,0:T(8,128)S(1)}, f32[2,8,32,256]{3,2,1,0:T(8,128)}, u32[]{:S(2)}) copy-start(f32[2,8,32,256]{3,2,1,0:T(8,128)} %init.1) | copy-start | bytes 1572868
  0.6 9.4 %copy-start.4 = (s32[32,256]{1,0:T(8,128)S(1)}, s32[32,256]{1,0:T(8,128)}, u32[]{:S(2)}) copy-start(s32[32,256]{1,0:T(8,128)} %depth.3) | copy-start | bytes 98308
  0.7 9.4 %copy-start.6 = (f32[32,256]{1,0:T(8,128)S(1)}, f32[32,256]{1,0:T(8,128)}, u32[]{:S(2)}) copy-start(f32[32,256]{1,0:T(8,128)} %mixing.1) | copy-start | bytes 98308
  0.7 13.7 %copy-start.5 = (f32[2,2,4096]{2,1,0:T(2,128)S(1)}, f32[2,2,4096]{2,1,0:T(2,128)}, u32[]{:S(2)}) copy-start(f32[2,2,4096]{2,1,0:T(2,128)} %obs_far.1) | copy-start | bytes 196612
  0.7 13.7 %copy-start.8 = (s32[2,4096]{1,0:T(2,128)S(1)}, s32[2,4096]{1,0:T(2,128)}, u32[]{:S(2)}) copy-start(s32[2,4096]{1,0:T(2,128)} %cell_far.1) | copy-start | bytes 98308
  3.3 11.1 %copy-start.2 = (f32[4,2,256,64]{2,3,1,0:T(8,128)S(1)}, f32[4,2,256,64]{2,3,1,0:T(8,128)}, u32[]{:S(2)}) copy-start(f32[4,2,256,64]{2,3,1,0:T(8,128)} %param.12) | copy-start | bytes 1572868
  3.3 6.4 %collective-permute-start = (f32[48,256]{1,0:T(8,128)}, f32[48,256]{1,0:T(8,128)S(1)}, u32[]{:S(2)}, u32[]{:S(2)}) collective-permute-start(f32[48,256]{1,0:T(8,128)} %get-tuple-element.22), channel_id=1, source_target_pairs={{4,8},{12,16},{20,24},{28,32},{36,40},{44,48},{52,56},{60,64},{68,... | collective-permute-start | bytes 147464 | tf_op jit(solution)/shard_map/ppermute | solution.py:494
  5.3 4.7 %collective-permute-start.1 = (f32[48,256]{1,0:T(8,128)}, f32[48,256]{1,0:T(8,128)S(1)}, u32[]{:S(2)}, u32[]{:S(2)}) collective-permute-start(f32[48,256]{1,0:T(8,128)} %get-tuple-element.23), channel_id=1, source_target_pairs={{0,4},{4,0},{8,12},{12,8},{16,20},{20,16},{24,28},{28,24},{32,36},... | collective-permute-start | bytes 147464 | tf_op jit(solution)/shard_map/ppermute | solution.py:495
  8.9 0.7 %copy-start.9 = (f32[16,256]{1,0:T(8,128)S(1)}, f32[16,256]{1,0:T(8,128)}, u32[]{:S(2)}) copy-start(f32[16,256]{1,0:T(8,128)} %get-tuple-element.24.beside) | copy-start | bytes 49156
  9.7 4.7 %copy-start.1 = (f32[4,2,4096]{2,1,0:T(2,128)S(1)}, f32[4,2,4096]{2,1,0:T(2,128)}, u32[]{:S(2)}) copy-start(f32[4,2,4096]{2,1,0:T(2,128)} %weight_far.1) | copy-start | bytes 393220
  9.7 4.7 %copy-start.3 = (f32[2,4096]{1,0:T(2,128)S(1)}, f32[2,4096]{1,0:T(2,128)}, u32[]{:S(2)}) copy-start(f32[2,4096]{1,0:T(2,128)} %precision.1) | copy-start | bytes 98308
  9.7 4.7 %copy-start.7 = (s32[2,4096]{1,0:T(2,128)S(1)}, s32[2,4096]{1,0:T(2,128)}, u32[]{:S(2)}) copy-start(s32[2,4096]{1,0:T(2,128)} %move_far.1) | copy-start | bytes 98308
  10.3 5.8 %collective-permute-start.2 = (f32[32,256]{1,0:T(8,128)S(1)}, f32[32,256]{1,0:T(8,128)S(1)}, u32[]{:S(2)}, u32[]{:S(2)}) collective-permute-start(f32[32,256]{1,0:T(8,128)S(1)} %get-tuple-element.25), channel_id=1, source_target_pairs={{0,1},{1,0},{2,3},{3,2},{4,5},{5,4},{6,7},{7,6},{8,9},{9,8},{10,11... | collective-permute-start | bytes 98312 | tf_op jit(solution)/shard_map/ppermute | solution.py:495
  13.7 2.4 %collective-permute-start.3 = (f32[32,256]{1,0:T(8,128)S(1)}, f32[32,256]{1,0:T(8,128)S(1)}, u32[]{:S(2)}, u32[]{:S(2)}) collective-permute-start(f32[32,256]{1,0:T(8,128)S(1)} %get-tuple-element.26), channel_id=1, source_target_pairs={{1,2},{2,1},{5,6},{6,5},{9,10},{10,9},{13,14},{14,13},{17,18},{18,... | collective-permute-start | bytes 98312 | tf_op jit(solution)/shard_map/ppermute | solution.py:494
  21.6 29.0 %all-to-all-start = ((f32[64,4,128]{2,1,0:T(4,128)}), f32[64,4,128]{2,1,0:T(4,128)S(1)}, u32[]{:S(2)}, u32[]{:S(2)}) async-start(f32[64,4,128]{2,1,0:T(4,128)} %get-tuple-element.28), calls=%async_computation | async-start | bytes 262144 | tf_op jit(solution)/shard_map/all_to_all | solution.py:510
  40.1 5.8 %collective-permute-start.4 = (f32[18,512]{1,0:T(8,128)S(1)}, f32[18,512]{1,0:T(8,128)S(1)}, u32[]{:S(2)}, u32[]{:S(2)}) collective-permute-start(f32[18,512]{1,0:T(8,128)S(1)} %get-tuple-element.30), channel_id=1, source_target_pairs={{4,8},{12,16},{20,24},{28,32},{36,40},{44,48},{52,56},{60,64},{68,... | collective-permute-start | bytes 110600 | tf_op jit(solution)/shard_map/ppermute | solution.py:494
  42.1 4.2 %collective-permute-start.5 = (f32[18,512]{1,0:T(8,128)S(1)}, f32[18,512]{1,0:T(8,128)S(1)}, u32[]{:S(2)}, u32[]{:S(2)}) collective-permute-start(f32[18,512]{1,0:T(8,128)S(1)} %get-tuple-element.31), channel_id=1, source_target_pairs={{0,4},{4,0},{8,12},{12,8},{16,20},{20,16},{24,28},{28,24},{32,36},... | collective-permute-start | bytes 110600 | tf_op jit(solution)/shard_map/ppermute | solution.py:495
  51.6 18.3 %all-to-all-start.1 = ((f32[8,72,128]{2,1,0:T(8,128)}), f32[8,72,128]{2,1,0:T(8,128)S(1)}, u32[]{:S(2)}, u32[]{:S(2)}) async-start(f32[8,72,128]{2,1,0:T(8,128)} %get-tuple-element.35), calls=%async_computation.1 | async-start | bytes 589824 | tf_op jit(solution)/shard_map/all_to_all | solution.py:510
  57.4 5.6 %collective-permute-start.6 = (f32[32,128]{1,0:T(8,128)S(1)}, f32[32,128]{1,0:T(8,128)S(1)}, u32[]{:S(2)}, u32[]{:S(2)}) collective-permute-start(f32[32,128]{1,0:T(8,128)S(1)} %get-tuple-element.33), channel_id=1, source_target_pairs={{0,1},{1,0},{2,3},{3,2},{4,5},{5,4},{6,7},{7,6},{8,9},{9,8},{10,11... | collective-permute-start | bytes 49160 | tf_op jit(solution)/shard_map/ppermute | solution.py:495
  59.9 3.1 %collective-permute-start.7 = (f32[32,128]{1,0:T(8,128)S(1)}, f32[32,128]{1,0:T(8,128)S(1)}, u32[]{:S(2)}, u32[]{:S(2)}) collective-permute-start(f32[32,128]{1,0:T(8,128)S(1)} %get-tuple-element.34), channel_id=1, source_target_pairs={{1,2},{2,1},{5,6},{6,5},{9,10},{10,9},{13,14},{14,13},{17,18},{18,... | collective-permute-start | bytes 49160 | tf_op jit(solution)/shard_map/ppermute | solution.py:494

commit v6 on v5

--- a/solution.py
+++ b/solution.py
@@ -252,12 +252,12 @@
 
 def main_kernel(
     levels, refine, lat_count, forcing, fields, precision, outer, inner, first, second,
-    padded, partial, share, to_inner, to_outer, ext, spot, to_west, to_east,
+    padded, partial, share, to_inner, to_outer, spot, to_west, to_east,
 ):
     from_west, from_east = pick("lon", inner, outer)
     from_south, from_north = pick("lat", first, second)
     rows, cells_lat = partial.shape[1] - 16, partial.shape[2] - 256
-    tall, wide = ext.shape[1:]
+    tall, wide = padded.shape[1:]
     lat_index = lax.axis_index("lat")
     grid_lat = cells_lat * lat_count
     lane = iota((tall, 128), 1)
@@ -370,10 +370,9 @@
     for c in range(2):
         for k in range(DEPTH):
             p = c * DEPTH + k
-            ext[p] = adjoint[c][k]
             partial[p] = adjoint[c][k]
-            to_west[LOW * p : LOW * (p + 1), :] = ext[p, X0 - LOW : X0, :]
-            to_east[HIGH * p : HIGH * (p + 1), :] = ext[p, X0 + rows : X0 + rows + HIGH, :]
+            to_west[LOW * p : LOW * (p + 1), :] = partial[p, X0 - LOW : X0, :]
+            to_east[HIGH * p : HIGH * (p + 1), :] = partial[p, X0 + rows : X0 + rows + HIGH, :]
     address("lon", to_west, to_east, to_inner, to_outer)
     low, part = interpolation(iota((wide, 4 * GROUP), 0) - Y0 - refine // 2, refine)
     column = iota((wide, 4 * GROUP), 1) % GROUP - 1
@@ -393,8 +392,8 @@
     share[...] = jnp.broadcast_to(jnp.concatenate(parts, axis=0)[None], share.shape)
 
 
-def plane_kernel(lat_count, per, shares, partial, outer, inner, out, own, first, second, rows, total):
-    join(partial, inner, outer, own, first, second)
+def plane_kernel(lat_count, per, shares, partial, outer, inner, out, own, first, second, rows, total, block):
+    join(partial, inner, outer, own, first, second, block)
     members = shares.shape[0]
     ring = members // (CORES * lat_count)
     ctrl_lat = per * lat_count
@@ -402,7 +401,7 @@
         rows[4 * m : 4 * m + 4, :] = shares[m]
     total[...] = jnp.zeros_like(total)
     lane = iota((ring, 4 * GROUP), 1)
-    height = total.shape[0] // STEPS
+    height = out.shape[1] // STEPS
     weight = jnp.zeros((ring, 4 * GROUP), F32)
     for core in range(CORES):
         for step in range(STEPS):
@@ -424,22 +423,22 @@
     weight = jnp.sum(jnp.where(lane == 4 * GROUP - 1, weight, 0.0), axis=0, keepdims=True)
     weight = jnp.sum(weight, axis=1, keepdims=True)
     total[4 * ring + 2 : 4 * ring + 3, :] = jnp.broadcast_to(weight, (1, 4 * GROUP))
-    out[...] = jnp.broadcast_to(total[...][None], out.shape)
-
-
-def join(partial, inner, outer, own, first_out, second_out):
+    out[...] = jnp.broadcast_to(total[: out.shape[1], :][None], out.shape)
+
+
+def join(partial, inner, outer, own, first_out, second_out, block):
     from_west, from_east = pick("lon", inner, outer)
     rows, cells_lat = own.shape[1:]
     lane = iota((rows, 128), 1)
     first = jnp.zeros((rows, 128), F32)
     last = jnp.zeros((rows, 128), F32)
     for p in range(2 * DEPTH):
-        partial[p, X0 : X0 + HIGH, :] += from_west[HIGH * p : HIGH * (p + 1), :]
-        partial[p, X0 + rows - LOW : X0 + rows, :] += from_east[LOW * p : LOW * (p + 1), :]
-        block = partial[p, X0 : X0 + rows, :]
-        own[p] = block[:, Y0 : Y0 + cells_lat]
-        tail = jnp.where(lane >= 128 - LOW, block[:, Y0 - 128 : Y0], 0.0)
-        head = jnp.where(lane < HIGH, block[:, Y0 + cells_lat : Y0 + cells_lat + 128], 0.0)
+        block[p] = partial[p, X0 : X0 + rows, :]
+        block[p, :HIGH, :] += from_west[HIGH * p : HIGH * (p + 1), :]
+        block[p, rows - LOW :, :] += from_east[LOW * p : LOW * (p + 1), :]
+        own[p] = block[p, :, Y0 : Y0 + cells_lat]
+        tail = jnp.where(lane >= 128 - LOW, block[p, :, Y0 - 128 : Y0], 0.0)
+        head = jnp.where(lane < HIGH, block[p, :, Y0 + cells_lat : Y0 + cells_lat + 128], 0.0)
         first = first + roll(tail, -LOW * p, 1)
         last = last + roll(head, HIGH * p, 1)
     address("lat", first, last, first_out, second_out)
@@ -476,12 +475,11 @@
             before, after = (m * span + ctrl_lon - 1) % ctrl_lon, (m + 1) * span % ctrl_lon
             full[step, before : before + 1, :] += shares[m, at : at + 1, :]
             full[step, after : after + 1, :] += shares[m, at + span + 1 : at + span + 2, :]
-    scaled = [scale * full[step] for step in range(STEPS)]
+    scaled = [(scale * full[step]).T for step in range(STEPS)]
     for period in range(periods):
         value = table[0][period] * scaled[0]
         for step in range(1, STEPS):
             value = value + table[step][period] * scaled[step]
-        value = value.T
         for c in range(2):
             out[period, c] = value[c * ctrl_lat : (c + 1) * ctrl_lat]
 
@@ -585,7 +583,7 @@
         functools.partial(main_kernel, levels, refine, lat_count),
         (forcing, fields, drift_precision, outer, inner, first, second, padded),
         ((2 * DEPTH, tall, wide), (ring * CORES * lat_count, 2 * STEPS, 4 * GROUP), edge, edge),
-        scratch=((2 * DEPTH, tall, wide), (2, tall, wide), edge, edge),
+        scratch=((2, tall, wide), edge, edge),
     )
     shares = gather(share, ring, 1, True)
     inner, outer = swap("lon", inner, outer, True)
@@ -594,7 +592,11 @@
         functools.partial(plane_kernel, lat_count, ctrl_lat // lat_count),
         (shares, partial, outer, inner),
         ((members, STEPS * height, 2 * ctrl_lat), (2 * DEPTH, rows, cells_lat), (rows, 128), (rows, 128)),
-        scratch=((4 * ring * CORES * lat_count, 4 * GROUP), (STEPS * height, 2 * ctrl_lat)),
+        scratch=(
+            (4 * (ring + 1) * CORES * lat_count, 4 * GROUP),
+            (STEPS * height + 8, 2 * ctrl_lat),
+            (2 * DEPTH, rows, wide),
+        ),
     )
     first, second = swap("lat", first, second, False)
     shares = gather(share, members, ring, False)

time: 71.7 us -> 71.6 us (level)
  no operation moved by 1% of the time
where the time goes in v6:
time: 71.6 us; the launch traced here: 71.1 us
  starting transfers between devices  42.5 us (59%)
  waiting for transfers between devices  15.8 us (22%)
  Pallas kernels  11.2 us (16%)
  between operations  0.84 us (1%)
  local copies, waits for them, and re-layouts  0.75 us (1%)
    all_to_all x2, starting transfers between devices, gather(): lax.all_to_all(copies, ('lon', 'lat'), 0, 0, axis_index_groups=groups, ti...  24.3 us
    ppermute x4, starting transfers between devices, swap(): first = lax.ppermute(first, axis, [(i, i ^ 1) for i in range(count)])  12.8 us
    all_to_all x2, waiting for transfers between devices, gather(): lax.all_to_all(copies, ('lon', 'lat'), 0, 0, axis_index_groups=groups, ti...  11.2 us
    pallas_call x7, Pallas kernels, call(): pl.pallas_call(kernel, grid=(1,), out_shape=[jax.ShapeDtypeStruct(shape,...  11.2 us
    ppermute x4, starting transfers between devices, swap(): second = lax.ppermute(second, axis, across + [(b, a) for a, b in across])  5.4 us
    ppermute x4, waiting for transfers between devices, swap(): first = lax.ppermute(first, axis, [(i, i ^ 1) for i in range(count)])  4.22 us
  transfers between devices with their start and end apart: 10, of which 7 were waited for; matrix products, arithmetic and copies ran while one was open for 0% of the time, Pallas kernels for 1%

profile of v6, /device:TPU:8, one launch (start us, length us, event | category | flops | bytes accessed | tf_op | source)
XLA Modules:
  0.0 71.1 jit_solution(17460696365298776318)
XLA Ops:
  0.6 0.0 copy-start
  0.6 0.0 copy-start.4
  0.7 0.0 copy-start.6
  0.7 0.0 copy-start.5
  0.7 2.6 %shard_map.105 = (f32[48,256]{1,0:T(8,128)}, f32[48,256]{1,0:T(8,128)}, f32[16,256]{1,0:T(8,128)}) custom-call(s32[2,4096]{1,0:T(2,128)} %move_far.1, s32[2,4096]{1,0:T(2,128)} %cell_far.1, f32[4,2,4096]{2,1,0:T(2,128)} %weight_far.1, f32[2,2,4096]{2,1,0:T(2,128)} %obs_far.1, f32[2,4096]{1,0:T(2,128)} %precision.1, f32[2,8,32,256]{3,2,1,0:T(8,128)} %init.1, ...), custom_call_target="tpu_custom_call" | custom-call | tf_op jit(solution)/shard_map/pallas_call | solution.py:520
  3.3 0.0 copy-start.2
  3.3 2.1 %collective-permute-start = (f32[48,256]{1,0:T(8,128)}, f32[48,256]{1,0:T(8,128)S(1)}, u32[]{:S(2)}, u32[]{:S(2)}) collective-permute-start(f32[48,256]{1,0:T(8,128)} %get-tuple-element.22), channel_id=1, source_target_pairs={{4,8},{12,16},{20,24},{28,32},{36,40},{44,48},{52,56},{60,64},{68,... | collective-permute-start | bytes 147464 | tf_op jit(solution)/shard_map/ppermute | solution.py:492
  5.3 3.6 %collective-permute-start.1 = (f32[48,256]{1,0:T(8,128)}, f32[48,256]{1,0:T(8,128)S(1)}, u32[]{:S(2)}, u32[]{:S(2)}) collective-permute-start(f32[48,256]{1,0:T(8,128)} %get-tuple-element.23), channel_id=1, source_target_pairs={{0,4},{4,0},{8,12},{12,8},{16,20},{20,16},{24,28},{28,24},{32,36},... | collective-permute-start | bytes 147464 | tf_op jit(solution)/shard_map/ppermute | solution.py:493
  8.9 0.7 copy-done.9
  9.7 0.0 collective-permute-done.outer
  9.7 0.3 collective-permute-done.1.inner
  10.0 0.2 shard_map.107
  10.3 3.4 %collective-permute-start.2 = (f32[32,256]{1,0:T(8,128)S(1)}, f32[32,256]{1,0:T(8,128)S(1)}, u32[]{:S(2)}, u32[]{:S(2)}) collective-permute-start(f32[32,256]{1,0:T(8,128)S(1)} %get-tuple-element.25), channel_id=1, source_target_pairs={{0,1},{1,0},{2,3},{3,2},{4,5},{5,4},{6,7},{7,6},{8,9},{9,8},{10,11... | collective-permute-start | bytes 98312 | tf_op jit(solution)/shard_map/ppermute | solution.py:493
  13.7 0.7 collective-permute-start.3
  14.4 0.7 shard_map.104
  15.1 1.0 %collective-permute-done.2.first = f32[32,256]{1,0:T(8,128)S(1)} collective-permute-done((f32[32,256]{1,0:T(8,128)S(1)}, f32[32,256]{1,0:T(8,128)S(1)}, u32[]{:S(2)}, u32[]{:S(2)}) %collective-permute-start.2) | collective-permute-done | bytes 32800 | tf_op jit(solution)/shard_map/ppermute | solution.py:493
  16.1 0.0 collective-permute-done.3.second
  16.1 5.5 %shard_map.108 = (f32[6,48,512]{2,1,0:T(8,128)S(1)}, f32[64,4,128]{2,1,0:T(4,128)}, f32[18,512]{1,0:T(8,128)S(1)}, f32[18,512]{1,0:T(8,128)S(1)}) custom-call(f32[4,48,512]{2,1,0:T(8,128)S(1)} %get-tuple-element.20.forcing, f32[16,4096]{1,0:T(8,128)S(1)} %get-tuple-element.21.fields, f32[2,4096]{1,0:T(2,128)S(1)} %copy-done.3, ...), custom_call_target="tpu_custom_call" | custom-call | tf_op jit(solution)/shard_map/pallas_call | solution.py:520
  21.6 18.5 %all-to-all-start = ((f32[64,4,128]{2,1,0:T(4,128)}), f32[64,4,128]{2,1,0:T(4,128)S(1)}, u32[]{:S(2)}, u32[]{:S(2)}) async-start(f32[64,4,128]{2,1,0:T(4,128)} %get-tuple-element.28), calls=%async_computation | async-start | bytes 262144 | tf_op jit(solution)/shard_map/all_to_all | solution.py:508
  40.1 2.0 %collective-permute-start.4 = (f32[18,512]{1,0:T(8,128)S(1)}, f32[18,512]{1,0:T(8,128)S(1)}, u32[]{:S(2)}, u32[]{:S(2)}) collective-permute-start(f32[18,512]{1,0:T(8,128)S(1)} %get-tuple-element.30), channel_id=1, source_target_pairs={{4,8},{12,16},{20,24},{28,32},{36,40},{44,48},{52,56},{60,64},{68,... | collective-permute-start | bytes 110600 | tf_op jit(solution)/shard_map/ppermute | solution.py:492
  42.1 3.4 %collective-permute-start.5 = (f32[18,512]{1,0:T(8,128)S(1)}, f32[18,512]{1,0:T(8,128)S(1)}, u32[]{:S(2)}, u32[]{:S(2)}) collective-permute-start(f32[18,512]{1,0:T(8,128)S(1)} %get-tuple-element.31), channel_id=1, source_target_pairs={{0,4},{4,0},{8,12},{12,8},{16,20},{20,16},{24,28},{28,24},{32,36},... | collective-permute-start | bytes 110600 | tf_op jit(solution)/shard_map/ppermute | solution.py:493
  45.5 0.4 collective-permute-done.4.outer
  45.9 0.5 collective-permute-done.5.inner
  46.3 4.3 %all-to-all-done.shares = f32[64,4,128]{2,1,0:T(4,128)S(1)} async-done(((f32[64,4,128]{2,1,0:T(4,128)}), f32[64,4,128]{2,1,0:T(4,128)S(1)}, u32[]{:S(2)}, u32[]{:S(2)}) %all-to-all-start) | async-done | bytes 131104 | tf_op jit(solution)/shard_map/all_to_all | solution.py:508
  50.6 1.0 %shard_map.109 = (f32[8,72,128]{2,1,0:T(8,128)}, f32[6,32,256]{2,1,0:T(8,128)S(1)}, f32[32,128]{1,0:T(8,128)S(1)}, f32[32,128]{1,0:T(8,128)S(1)}) custom-call(f32[64,4,128]{2,1,0:T(4,128)S(1)} %all-to-all-done.shares, f32[6,48,512]{2,1,0:T(8,128)S(1)} %get-tuple-element.29.partial, f32[18,512]{1,0:T(8,128)S(1)} %collective-permute-done.4.outer, ...), custom_call_target="tpu_custom_call" | custom-call | tf_op jit(solution)/shard_map/pallas_call | solution.py:520
  51.6 5.8 %all-to-all-start.1 = ((f32[8,72,128]{2,1,0:T(8,128)}), f32[8,72,128]{2,1,0:T(8,128)S(1)}, u32[]{:S(2)}, u32[]{:S(2)}) async-start(f32[8,72,128]{2,1,0:T(8,128)} %get-tuple-element.35), calls=%async_computation.1 | async-start | bytes 589824 | tf_op jit(solution)/shard_map/all_to_all | solution.py:508
  57.4 2.5 %collective-permute-start.6 = (f32[32,128]{1,0:T(8,128)S(1)}, f32[32,128]{1,0:T(8,128)S(1)}, u32[]{:S(2)}, u32[]{:S(2)}) collective-permute-start(f32[32,128]{1,0:T(8,128)S(1)} %get-tuple-element.33), channel_id=1, source_target_pairs={{0,1},{1,0},{2,3},{3,2},{4,5},{5,4},{6,7},{7,6},{8,9},{9,8},{10,11... | collective-permute-start | bytes 49160 | tf_op jit(solution)/shard_map/ppermute | solution.py:493
  59.9 0.7 collective-permute-start.7
  60.6 2.5 %collective-permute-done.6.first = f32[32,128]{1,0:T(8,128)S(1)} collective-permute-done((f32[32,128]{1,0:T(8,128)S(1)}, f32[32,128]{1,0:T(8,128)S(1)}, u32[]{:S(2)}, u32[]{:S(2)}) %collective-permute-start.6) | collective-permute-done | bytes 16416 | tf_op jit(solution)/shard_map/ppermute | solution.py:493
  63.0 0.0 collective-permute-done.7.second
  63.0 6.9 %all-to-all-done.1.shares = f32[8,72,128]{2,1,0:T(8,128)S(1)} async-done(((f32[8,72,128]{2,1,0:T(8,128)}), f32[8,72,128]{2,1,0:T(8,128)S(1)}, u32[]{:S(2)}, u32[]{:S(2)}) %all-to-all-start.1) | async-done | bytes 294944 | tf_op jit(solution)/shard_map/all_to_all | solution.py:508
  70.0 1.1 %shard_map.110 = (f32[2,8,32,256]{3,2,1,0:T(8,128)}, f32[4,2,64,256]{3,2,1,0:T(8,128)}) custom-call(f32[6,32,256]{2,1,0:T(8,128)S(1)} %get-tuple-element.32.own, s32[32,256]{1,0:T(8,128)S(1)} %copy-done.4, f32[32,128]{1,0:T(8,128)S(1)} %collective-permute-done.6.first, f32[32,128]{1,0:T(8,128)S(1)} %collective-permute-done.7.second, ...), custom_call_target="tpu_custom_call" | custom-call | tf_op jit(solution)/shard_map/pallas_call | solution.py:520
  (15 shorter events, 0.0 us)
Async XLA Ops:
  0.6 9.4 %copy-start = (f32[2,8,32,256]{3,2,1,0:T(8,128)S(1)}, f32[2,8,32,256]{3,2,1,0:T(8,128)}, u32[]{:S(2)}) copy-start(f32[2,8,32,256]{3,2,1,0:T(8,128)} %init.1) | copy-start | bytes 1572868
  0.6 9.4 %copy-start.4 = (s32[32,256]{1,0:T(8,128)S(1)}, s32[32,256]{1,0:T(8,128)}, u32[]{:S(2)}) copy-start(s32[32,256]{1,0:T(8,128)} %depth.3) | copy-start | bytes 98308
  0.7 9.4 %copy-start.6 = (f32[32,256]{1,0:T(8,128)S(1)}, f32[32,256]{1,0:T(8,128)}, u32[]{:S(2)}) copy-start(f32[32,256]{1,0:T(8,128)} %mixing.1) | copy-start | bytes 98308
  0.7 13.7 %copy-start.5 = (f32[2,2,4096]{2,1,0:T(2,128)S(1)}, f32[2,2,4096]{2,1,0:T(2,128)}, u32[]{:S(2)}) copy-start(f32[2,2,4096]{2,1,0:T(2,128)} %obs_far.1) | copy-start | bytes 196612
  0.7 13.7 %copy-start.8 = (s32[2,4096]{1,0:T(2,128)S(1)}, s32[2,4096]{1,0:T(2,128)}, u32[]{:S(2)}) copy-start(s32[2,4096]{1,0:T(2,128)} %cell_far.1) | copy-start | bytes 98308
  3.3 11.1 %copy-start.2 = (f32[4,2,256,64]{2,3,1,0:T(8,128)S(1)}, f32[4,2,256,64]{2,3,1,0:T(8,128)}, u32[]{:S(2)}) copy-start(f32[4,2,256,64]{2,3,1,0:T(8,128)} %param.12) | copy-start | bytes 1572868
  3.3 6.4 %collective-permute-start = (f32[48,256]{1,0:T(8,128)}, f32[48,256]{1,0:T(8,128)S(1)}, u32[]{:S(2)}, u32[]{:S(2)}) collective-permute-start(f32[48,256]{1,0:T(8,128)} %get-tuple-element.22), channel_id=1, source_target_pairs={{4,8},{12,16},{20,24},{28,32},{36,40},{44,48},{52,56},{60,64},{68,... | collective-permute-start | bytes 147464 | tf_op jit(solution)/shard_map/ppermute | solution.py:492
  5.3 4.7 %collective-permute-start.1 = (f32[48,256]{1,0:T(8,128)}, f32[48,256]{1,0:T(8,128)S(1)}, u32[]{:S(2)}, u32[]{:S(2)}) collective-permute-start(f32[48,256]{1,0:T(8,128)} %get-tuple-element.23), channel_id=1, source_target_pairs={{0,4},{4,0},{8,12},{12,8},{16,20},{20,16},{24,28},{28,24},{32,36},... | collective-permute-start | bytes 147464 | tf_op jit(solution)/shard_map/ppermute | solution.py:493
  8.9 0.7 %copy-start.9 = (f32[16,256]{1,0:T(8,128)S(1)}, f32[16,256]{1,0:T(8,128)}, u32[]{:S(2)}) copy-start(f32[16,256]{1,0:T(8,128)} %get-tuple-element.24.beside) | copy-start | bytes 49156
  9.7 4.7 %copy-start.1 = (f32[4,2,4096]{2,1,0:T(2,128)S(1)}, f32[4,2,4096]{2,1,0:T(2,128)}, u32[]{:S(2)}) copy-start(f32[4,2,4096]{2,1,0:T(2,128)} %weight_far.1) | copy-start | bytes 393220
  9.7 4.7 %copy-start.3 = (f32[2,4096]{1,0:T(2,128)S(1)}, f32[2,4096]{1,0:T(2,128)}, u32[]{:S(2)}) copy-start(f32[2,4096]{1,0:T(2,128)} %precision.1) | copy-start | bytes 98308
  9.7 4.7 %copy-start.7 = (s32[2,4096]{1,0:T(2,128)S(1)}, s32[2,4096]{1,0:T(2,128)}, u32[]{:S(2)}) copy-start(s32[2,4096]{1,0:T(2,128)} %move_far.1) | copy-start | bytes 98308
  10.3 5.8 %collective-permute-start.2 = (f32[32,256]{1,0:T(8,128)S(1)}, f32[32,256]{1,0:T(8,128)S(1)}, u32[]{:S(2)}, u32[]{:S(2)}) collective-permute-start(f32[32,256]{1,0:T(8,128)S(1)} %get-tuple-element.25), channel_id=1, source_target_pairs={{0,1},{1,0},{2,3},{3,2},{4,5},{5,4},{6,7},{7,6},{8,9},{9,8},{10,11... | collective-permute-start | bytes 98312 | tf_op jit(solution)/shard_map/ppermute | solution.py:493
  13.7 2.4 %collective-permute-start.3 = (f32[32,256]{1,0:T(8,128)S(1)}, f32[32,256]{1,0:T(8,128)S(1)}, u32[]{:S(2)}, u32[]{:S(2)}) collective-permute-start(f32[32,256]{1,0:T(8,128)S(1)} %get-tuple-element.26), channel_id=1, source_target_pairs={{1,2},{2,1},{5,6},{6,5},{9,10},{10,9},{13,14},{14,13},{17,18},{18,... | collective-permute-start | bytes 98312 | tf_op jit(solution)/shard_map/ppermute | solution.py:492
  21.6 29.0 %all-to-all-start = ((f32[64,4,128]{2,1,0:T(4,128)}), f32[64,4,128]{2,1,0:T(4,128)S(1)}, u32[]{:S(2)}, u32[]{:S(2)}) async-start(f32[64,4,128]{2,1,0:T(4,128)} %get-tuple-element.28), calls=%async_computation | async-start | bytes 262144 | tf_op jit(solution)/shard_map/all_to_all | solution.py:508
  40.1 5.8 %collective-permute-start.4 = (f32[18,512]{1,0:T(8,128)S(1)}, f32[18,512]{1,0:T(8,128)S(1)}, u32[]{:S(2)}, u32[]{:S(2)}) collective-permute-start(f32[18,512]{1,0:T(8,128)S(1)} %get-tuple-element.30), channel_id=1, source_target_pairs={{4,8},{12,16},{20,24},{28,32},{36,40},{44,48},{52,56},{60,64},{68,... | collective-permute-start | bytes 110600 | tf_op jit(solution)/shard_map/ppermute | solution.py:492
  42.1 4.2 %collective-permute-start.5 = (f32[18,512]{1,0:T(8,128)S(1)}, f32[18,512]{1,0:T(8,128)S(1)}, u32[]{:S(2)}, u32[]{:S(2)}) collective-permute-start(f32[18,512]{1,0:T(8,128)S(1)} %get-tuple-element.31), channel_id=1, source_target_pairs={{0,4},{4,0},{8,12},{12,8},{16,20},{20,16},{24,28},{28,24},{32,36},... | collective-permute-start | bytes 110600 | tf_op jit(solution)/shard_map/ppermute | solution.py:493
  51.6 18.3 %all-to-all-start.1 = ((f32[8,72,128]{2,1,0:T(8,128)}), f32[8,72,128]{2,1,0:T(8,128)S(1)}, u32[]{:S(2)}, u32[]{:S(2)}) async-start(f32[8,72,128]{2,1,0:T(8,128)} %get-tuple-element.35), calls=%async_computation.1 | async-start | bytes 589824 | tf_op jit(solution)/shard_map/all_to_all | solution.py:508
  57.4 5.6 %collective-permute-start.6 = (f32[32,128]{1,0:T(8,128)S(1)}, f32[32,128]{1,0:T(8,128)S(1)}, u32[]{:S(2)}, u32[]{:S(2)}) collective-permute-start(f32[32,128]{1,0:T(8,128)S(1)} %get-tuple-element.33), channel_id=1, source_target_pairs={{0,1},{1,0},{2,3},{3,2},{4,5},{5,4},{6,7},{7,6},{8,9},{9,8},{10,11... | collective-permute-start | bytes 49160 | tf_op jit(solution)/shard_map/ppermute | solution.py:493
  59.9 3.1 %collective-permute-start.7 = (f32[32,128]{1,0:T(8,128)S(1)}, f32[32,128]{1,0:T(8,128)S(1)}, u32[]{:S(2)}, u32[]{:S(2)}) collective-permute-start(f32[32,128]{1,0:T(8,128)S(1)} %get-tuple-element.34), channel_id=1, source_target_pairs={{1,2},{2,1},{5,6},{6,5},{9,10},{10,9},{13,14},{14,13},{17,18},{18,... | collective-permute-start | bytes 49160 | tf_op jit(solution)/shard_map/ppermute | solution.py:492

commit v7 on v6

--- a/solution.py
+++ b/solution.py
@@ -251,7 +251,7 @@
 
 
 def main_kernel(
-    levels, refine, lat_count, forcing, fields, precision, outer, inner, first, second,
+    levels, refine, lat_count, forcing, fields, precision, outer, inner, second, first,
     padded, partial, share, to_inner, to_outer, spot, to_west, to_east,
 ):
     from_west, from_east = pick("lon", inner, outer)
@@ -444,7 +444,7 @@
     address("lat", first, last, first_out, second_out)
 
 
-def finish_kernel(normalizer, own, depth, first, second, shares, grad, out, full):
+def finish_kernel(normalizer, own, depth, second, first, shares, grad, out, full):
     from_south, from_north = pick("lat", first, second)
     levels, rows, cells_lat = grad.shape[1:]
     periods, _, ctrl_lat, ctrl_lon = out.shape
@@ -581,7 +581,7 @@
     members = lon_count // (CORES * ring)
     partial, share, inner, outer = call(
         functools.partial(main_kernel, levels, refine, lat_count),
-        (forcing, fields, drift_precision, outer, inner, first, second, padded),
+        (forcing, fields, drift_precision, outer, inner, second, first, padded),
         ((2 * DEPTH, tall, wide), (ring * CORES * lat_count, 2 * STEPS, 4 * GROUP), edge, edge),
         scratch=((2, tall, wide), edge, edge),
     )
@@ -602,7 +602,7 @@
     shares = gather(share, members, ring, False)
     grad_initial, grad_controls = call(
         functools.partial(finish_kernel, float(STEPS * count * lon_count * lat_count)),
-        (own, depth_levels, first, second, shares),
+        (own, depth_levels, second, first, shares),
         (initial.shape, (periods, 2, ctrl_lat, ctrl_lon)),
         scratch=((STEPS, ctrl_lon, 2 * ctrl_lat),),
     )

time: 71.6 us -> 70.9 us (level)
  waiting for transfers between devices: 15.8 us -> 14.1 us
  starting transfers between devices: 42.5 us -> 43.6 us
    ppermute x4, starting transfers between devices: 12.8 us -> 17.5 us  [swap(): first = lax.ppermute(first, axis, [(i, i ^ 1) for i in range(count)])]
    all_to_all x2, starting transfers between devices: 24.3 us -> 20.7 us  [gather(): lax.all_to_all(copies, ('lon', 'lat'), 0, 0, axis_index_groups=groups, ti...]
    all_to_all x2, waiting for transfers between devices: 11.2 us -> 10.1 us  [gather(): lax.all_to_all(copies, ('lon', 'lat'), 0, 0, axis_index_groups=groups, ti...]
where the time goes in v7:
time: 70.9 us; the launch traced here: 70.4 us
  starting transfers between devices  43.6 us (61%)
  waiting for transfers between devices  14.1 us (20%)
  Pallas kernels  11.2 us (16%)
  between operations  0.86 us (1%)
  local copies, waits for them, and re-layouts  0.75 us (1%)
    all_to_all x2, starting transfers between devices, gather(): lax.all_to_all(copies, ('lon', 'lat'), 0, 0, axis_index_groups=groups, ti...  20.7 us
    ppermute x4, starting transfers between devices, swap(): first = lax.ppermute(first, axis, [(i, i ^ 1) for i in range(count)])  17.5 us
    pallas_call x7, Pallas kernels, call(): pl.pallas_call(kernel, grid=(1,), out_shape=[jax.ShapeDtypeStruct(shape,...  11.2 us
    all_to_all x2, waiting for transfers between devices, gather(): lax.all_to_all(copies, ('lon', 'lat'), 0, 0, axis_index_groups=groups, ti...  10.1 us
    ppermute x4, starting transfers between devices, swap(): second = lax.ppermute(second, axis, across + [(b, a) for a, b in across])  5.38 us
    ppermute x4, waiting for transfers between devices, swap(): first = lax.ppermute(first, axis, [(i, i ^ 1) for i in range(count)])  3.6 us
  transfers between devices with their start and end apart: 10, of which 7 were waited for; matrix products, arithmetic and copies ran while one was open for 0% of the time, Pallas kernels for 1%

profile of v7, /device:TPU:8, one launch (start us, length us, event | category | flops | bytes accessed | tf_op | source)
XLA Modules:
  0.0 70.4 jit_solution(12943799960256661576)
XLA Ops:
  0.6 0.0 copy-start
  0.6 0.0 copy-start.4
  0.7 0.0 copy-start.6
  0.7 0.0 copy-start.5
  0.7 2.6 %shard_map.105 = (f32[48,256]{1,0:T(8,128)}, f32[48,256]{1,0:T(8,128)}, f32[16,256]{1,0:T(8,128)}) custom-call(s32[2,4096]{1,0:T(2,128)} %move_far.1, s32[2,4096]{1,0:T(2,128)} %cell_far.1, f32[4,2,4096]{2,1,0:T(2,128)} %weight_far.1, f32[2,2,4096]{2,1,0:T(2,128)} %obs_far.1, f32[2,4096]{1,0:T(2,128)} %precision.1, f32[2,8,32,256]{3,2,1,0:T(8,128)} %init.1, ...), custom_call_target="tpu_custom_call" | custom-call | tf_op jit(solution)/shard_map/pallas_call | solution.py:520
  3.3 0.0 copy-start.2
  3.3 2.1 %collective-permute-start = (f32[48,256]{1,0:T(8,128)}, f32[48,256]{1,0:T(8,128)S(1)}, u32[]{:S(2)}, u32[]{:S(2)}) collective-permute-start(f32[48,256]{1,0:T(8,128)} %get-tuple-element.22), channel_id=1, source_target_pairs={{4,8},{12,16},{20,24},{28,32},{36,40},{44,48},{52,56},{60,64},{68,... | collective-permute-start | bytes 147464 | tf_op jit(solution)/shard_map/ppermute | solution.py:492
  5.3 3.6 %collective-permute-start.1 = (f32[48,256]{1,0:T(8,128)}, f32[48,256]{1,0:T(8,128)S(1)}, u32[]{:S(2)}, u32[]{:S(2)}) collective-permute-start(f32[48,256]{1,0:T(8,128)} %get-tuple-element.23), channel_id=1, source_target_pairs={{0,4},{4,0},{8,12},{12,8},{16,20},{20,16},{24,28},{28,24},{32,36},... | collective-permute-start | bytes 147464 | tf_op jit(solution)/shard_map/ppermute | solution.py:493
  8.9 0.7 %copy-done.9 = f32[16,256]{1,0:T(8,128)S(1)} copy-done((f32[16,256]{1,0:T(8,128)S(1)}, f32[16,256]{1,0:T(8,128)}, u32[]{:S(2)}) %copy-start.9) | copy-done | bytes 16408
  9.7 0.0 collective-permute-done.outer
  9.7 0.3 collective-permute-done.1.inner
  10.0 0.2 shard_map.107
  10.3 0.7 collective-permute-start.2
  10.9 6.1 %collective-permute-start.3 = (f32[32,256]{1,0:T(8,128)S(1)}, f32[32,256]{1,0:T(8,128)S(1)}, u32[]{:S(2)}, u32[]{:S(2)}) collective-permute-start(f32[32,256]{1,0:T(8,128)S(1)} %get-tuple-element.26), channel_id=1, source_target_pairs={{0,1},{1,0},{2,3},{3,2},{4,5},{5,4},{6,7},{7,6},{8,9},{9,8},{10,11... | collective-permute-start | bytes 98312 | tf_op jit(solution)/shard_map/ppermute | solution.py:493
  17.1 0.7 shard_map.104
  17.8 0.0 collective-permute-done.2.second
  17.8 1.1 %collective-permute-done.3.first = f32[32,256]{1,0:T(8,128)S(1)} collective-permute-done((f32[32,256]{1,0:T(8,128)S(1)}, f32[32,256]{1,0:T(8,128)S(1)}, u32[]{:S(2)}, u32[]{:S(2)}) %collective-permute-start.3) | collective-permute-done | bytes 32800 | tf_op jit(solution)/shard_map/ppermute | solution.py:493
  19.0 5.5 %shard_map.108 = (f32[6,48,512]{2,1,0:T(8,128)S(1)}, f32[64,4,128]{2,1,0:T(4,128)}, f32[18,512]{1,0:T(8,128)S(1)}, f32[18,512]{1,0:T(8,128)S(1)}) custom-call(f32[4,48,512]{2,1,0:T(8,128)S(1)} %get-tuple-element.20.forcing, f32[16,4096]{1,0:T(8,128)S(1)} %get-tuple-element.21.fields, f32[2,4096]{1,0:T(2,128)S(1)} %copy-done.3, ...), custom_call_target="tpu_custom_call" | custom-call | tf_op jit(solution)/shard_map/pallas_call | solution.py:520
  24.5 14.9 %all-to-all-start = ((f32[64,4,128]{2,1,0:T(4,128)}), f32[64,4,128]{2,1,0:T(4,128)S(1)}, u32[]{:S(2)}, u32[]{:S(2)}) async-start(f32[64,4,128]{2,1,0:T(4,128)} %get-tuple-element.28), calls=%async_computation | async-start | bytes 262144 | tf_op jit(solution)/shard_map/all_to_all | solution.py:508
  39.4 2.0 %collective-permute-start.4 = (f32[18,512]{1,0:T(8,128)S(1)}, f32[18,512]{1,0:T(8,128)S(1)}, u32[]{:S(2)}, u32[]{:S(2)}) collective-permute-start(f32[18,512]{1,0:T(8,128)S(1)} %get-tuple-element.30), channel_id=1, source_target_pairs={{4,8},{12,16},{20,24},{28,32},{36,40},{44,48},{52,56},{60,64},{68,... | collective-permute-start | bytes 110600 | tf_op jit(solution)/shard_map/ppermute | solution.py:492
  41.4 3.4 %collective-permute-start.5 = (f32[18,512]{1,0:T(8,128)S(1)}, f32[18,512]{1,0:T(8,128)S(1)}, u32[]{:S(2)}, u32[]{:S(2)}) collective-permute-start(f32[18,512]{1,0:T(8,128)S(1)} %get-tuple-element.31), channel_id=1, source_target_pairs={{0,4},{4,0},{8,12},{12,8},{16,20},{20,16},{24,28},{28,24},{32,36},... | collective-permute-start | bytes 110600 | tf_op jit(solution)/shard_map/ppermute | solution.py:493
  44.8 0.4 collective-permute-done.4.outer
  45.2 0.5 collective-permute-done.5.inner
  45.7 4.3 %all-to-all-done.shares = f32[64,4,128]{2,1,0:T(4,128)S(1)} async-done(((f32[64,4,128]{2,1,0:T(4,128)}), f32[64,4,128]{2,1,0:T(4,128)S(1)}, u32[]{:S(2)}, u32[]{:S(2)}) %all-to-all-start) | async-done | bytes 131104 | tf_op jit(solution)/shard_map/all_to_all | solution.py:508
  50.0 1.0 %shard_map.109 = (f32[8,72,128]{2,1,0:T(8,128)}, f32[6,32,256]{2,1,0:T(8,128)S(1)}, f32[32,128]{1,0:T(8,128)S(1)}, f32[32,128]{1,0:T(8,128)S(1)}) custom-call(f32[64,4,128]{2,1,0:T(4,128)S(1)} %all-to-all-done.shares, f32[6,48,512]{2,1,0:T(8,128)S(1)} %get-tuple-element.29.partial, f32[18,512]{1,0:T(8,128)S(1)} %collective-permute-done.4.outer, ...), custom_call_target="tpu_custom_call" | custom-call | tf_op jit(solution)/shard_map/pallas_call | solution.py:520
  51.0 5.8 %all-to-all-start.1 = ((f32[8,72,128]{2,1,0:T(8,128)}), f32[8,72,128]{2,1,0:T(8,128)S(1)}, u32[]{:S(2)}, u32[]{:S(2)}) async-start(f32[8,72,128]{2,1,0:T(8,128)} %get-tuple-element.35), calls=%async_computation.1 | async-start | bytes 589824 | tf_op jit(solution)/shard_map/all_to_all | solution.py:508
  56.7 0.7 collective-permute-start.6
  57.4 4.4 %collective-permute-start.7 = (f32[32,128]{1,0:T(8,128)S(1)}, f32[32,128]{1,0:T(8,128)S(1)}, u32[]{:S(2)}, u32[]{:S(2)}) collective-permute-start(f32[32,128]{1,0:T(8,128)S(1)} %get-tuple-element.34), channel_id=1, source_target_pairs={{0,1},{1,0},{2,3},{3,2},{4,5},{5,4},{6,7},{7,6},{8,9},{9,8},{10,11... | collective-permute-start | bytes 49160 | tf_op jit(solution)/shard_map/ppermute | solution.py:493
  61.8 0.0 collective-permute-done.6.second
  61.8 1.7 %collective-permute-done.7.first = f32[32,128]{1,0:T(8,128)S(1)} collective-permute-done((f32[32,128]{1,0:T(8,128)S(1)}, f32[32,128]{1,0:T(8,128)S(1)}, u32[]{:S(2)}, u32[]{:S(2)}) %collective-permute-start.7) | collective-permute-done | bytes 16416 | tf_op jit(solution)/shard_map/ppermute | solution.py:493
  63.5 5.8 %all-to-all-done.1.shares = f32[8,72,128]{2,1,0:T(8,128)S(1)} async-done(((f32[8,72,128]{2,1,0:T(8,128)}), f32[8,72,128]{2,1,0:T(8,128)S(1)}, u32[]{:S(2)}, u32[]{:S(2)}) %all-to-all-start.1) | async-done | bytes 294944 | tf_op jit(solution)/shard_map/all_to_all | solution.py:508
  69.3 1.1 %shard_map.110 = (f32[2,8,32,256]{3,2,1,0:T(8,128)}, f32[4,2,64,256]{3,2,1,0:T(8,128)}) custom-call(f32[6,32,256]{2,1,0:T(8,128)S(1)} %get-tuple-element.32.own, s32[32,256]{1,0:T(8,128)S(1)} %copy-done.4, f32[32,128]{1,0:T(8,128)S(1)} %collective-permute-done.6.second, f32[32,128]{1,0:T(8,128)S(1)} %collective-permute-done.7.first, ...), custom_call_target="tpu_custom_call" | custom-call | tf_op jit(solution)/shard_map/pallas_call | solution.py:520
  (15 shorter events, 0.0 us)
Async XLA Ops:
  0.6 9.4 %copy-start = (f32[2,8,32,256]{3,2,1,0:T(8,128)S(1)}, f32[2,8,32,256]{3,2,1,0:T(8,128)}, u32[]{:S(2)}) copy-start(f32[2,8,32,256]{3,2,1,0:T(8,128)} %init.1) | copy-start | bytes 1572868
  0.6 9.4 %copy-start.4 = (s32[32,256]{1,0:T(8,128)S(1)}, s32[32,256]{1,0:T(8,128)}, u32[]{:S(2)}) copy-start(s32[32,256]{1,0:T(8,128)} %depth.3) | copy-start | bytes 98308
  0.7 9.4 %copy-start.6 = (f32[32,256]{1,0:T(8,128)S(1)}, f32[32,256]{1,0:T(8,128)}, u32[]{:S(2)}) copy-start(f32[32,256]{1,0:T(8,128)} %mixing.1) | copy-start | bytes 98308
  0.7 16.4 %copy-start.5 = (f32[2,2,4096]{2,1,0:T(2,128)S(1)}, f32[2,2,4096]{2,1,0:T(2,128)}, u32[]{:S(2)}) copy-start(f32[2,2,4096]{2,1,0:T(2,128)} %obs_far.1) | copy-start | bytes 196612
  0.7 16.4 %copy-start.8 = (s32[2,4096]{1,0:T(2,128)S(1)}, s32[2,4096]{1,0:T(2,128)}, u32[]{:S(2)}) copy-start(s32[2,4096]{1,0:T(2,128)} %cell_far.1) | copy-start | bytes 98308
  3.3 13.8 %copy-start.2 = (f32[4,2,256,64]{2,3,1,0:T(8,128)S(1)}, f32[4,2,256,64]{2,3,1,0:T(8,128)}, u32[]{:S(2)}) copy-start(f32[4,2,256,64]{2,3,1,0:T(8,128)} %param.12) | copy-start | bytes 1572868
  3.3 6.4 %collective-permute-start = (f32[48,256]{1,0:T(8,128)}, f32[48,256]{1,0:T(8,128)S(1)}, u32[]{:S(2)}, u32[]{:S(2)}) collective-permute-start(f32[48,256]{1,0:T(8,128)} %get-tuple-element.22), channel_id=1, source_target_pairs={{4,8},{12,16},{20,24},{28,32},{36,40},{44,48},{52,56},{60,64},{68,... | collective-permute-start | bytes 147464 | tf_op jit(solution)/shard_map/ppermute | solution.py:492
  5.3 4.7 %collective-permute-start.1 = (f32[48,256]{1,0:T(8,128)}, f32[48,256]{1,0:T(8,128)S(1)}, u32[]{:S(2)}, u32[]{:S(2)}) collective-permute-start(f32[48,256]{1,0:T(8,128)} %get-tuple-element.23), channel_id=1, source_target_pairs={{0,4},{4,0},{8,12},{12,8},{16,20},{20,16},{24,28},{28,24},{32,36},... | collective-permute-start | bytes 147464 | tf_op jit(solution)/shard_map/ppermute | solution.py:493
  8.9 0.7 %copy-start.9 = (f32[16,256]{1,0:T(8,128)S(1)}, f32[16,256]{1,0:T(8,128)}, u32[]{:S(2)}) copy-start(f32[16,256]{1,0:T(8,128)} %get-tuple-element.24.beside) | copy-start | bytes 49156
  9.7 7.5 %copy-start.1 = (f32[4,2,4096]{2,1,0:T(2,128)S(1)}, f32[4,2,4096]{2,1,0:T(2,128)}, u32[]{:S(2)}) copy-start(f32[4,2,4096]{2,1,0:T(2,128)} %weight_far.1) | copy-start | bytes 393220
  9.7 7.5 %copy-start.3 = (f32[2,4096]{1,0:T(2,128)S(1)}, f32[2,4096]{1,0:T(2,128)}, u32[]{:S(2)}) copy-start(f32[2,4096]{1,0:T(2,128)} %precision.1) | copy-start | bytes 98308
  9.7 7.5 %copy-start.7 = (s32[2,4096]{1,0:T(2,128)S(1)}, s32[2,4096]{1,0:T(2,128)}, u32[]{:S(2)}) copy-start(s32[2,4096]{1,0:T(2,128)} %move_far.1) | copy-start | bytes 98308
  10.3 7.6 %collective-permute-start.2 = (f32[32,256]{1,0:T(8,128)S(1)}, f32[32,256]{1,0:T(8,128)S(1)}, u32[]{:S(2)}, u32[]{:S(2)}) collective-permute-start(f32[32,256]{1,0:T(8,128)S(1)} %get-tuple-element.25), channel_id=1, source_target_pairs={{1,2},{2,1},{5,6},{6,5},{9,10},{10,9},{13,14},{14,13},{17,18},{18,... | collective-permute-start | bytes 98312 | tf_op jit(solution)/shard_map/ppermute | solution.py:492
  10.9 8.0 %collective-permute-start.3 = (f32[32,256]{1,0:T(8,128)S(1)}, f32[32,256]{1,0:T(8,128)S(1)}, u32[]{:S(2)}, u32[]{:S(2)}) collective-permute-start(f32[32,256]{1,0:T(8,128)S(1)} %get-tuple-element.26), channel_id=1, source_target_pairs={{0,1},{1,0},{2,3},{3,2},{4,5},{5,4},{6,7},{7,6},{8,9},{9,8},{10,11... | collective-permute-start | bytes 98312 | tf_op jit(solution)/shard_map/ppermute | solution.py:493
  24.5 25.5 %all-to-all-start = ((f32[64,4,128]{2,1,0:T(4,128)}), f32[64,4,128]{2,1,0:T(4,128)S(1)}, u32[]{:S(2)}, u32[]{:S(2)}) async-start(f32[64,4,128]{2,1,0:T(4,128)} %get-tuple-element.28), calls=%async_computation | async-start | bytes 262144 | tf_op jit(solution)/shard_map/all_to_all | solution.py:508
  39.4 5.8 %collective-permute-start.4 = (f32[18,512]{1,0:T(8,128)S(1)}, f32[18,512]{1,0:T(8,128)S(1)}, u32[]{:S(2)}, u32[]{:S(2)}) collective-permute-start(f32[18,512]{1,0:T(8,128)S(1)} %get-tuple-element.30), channel_id=1, source_target_pairs={{4,8},{12,16},{20,24},{28,32},{36,40},{44,48},{52,56},{60,64},{68,... | collective-permute-start | bytes 110600 | tf_op jit(solution)/shard_map/ppermute | solution.py:492
  41.4 4.2 %collective-permute-start.5 = (f32[18,512]{1,0:T(8,128)S(1)}, f32[18,512]{1,0:T(8,128)S(1)}, u32[]{:S(2)}, u32[]{:S(2)}) collective-permute-start(f32[18,512]{1,0:T(8,128)S(1)} %get-tuple-element.31), channel_id=1, source_target_pairs={{0,4},{4,0},{8,12},{12,8},{16,20},{20,16},{24,28},{28,24},{32,36},... | collective-permute-start | bytes 110600 | tf_op jit(solution)/shard_map/ppermute | solution.py:493
  51.0 18.3 %all-to-all-start.1 = ((f32[8,72,128]{2,1,0:T(8,128)}), f32[8,72,128]{2,1,0:T(8,128)S(1)}, u32[]{:S(2)}, u32[]{:S(2)}) async-start(f32[8,72,128]{2,1,0:T(8,128)} %get-tuple-element.35), calls=%async_computation.1 | async-start | bytes 589824 | tf_op jit(solution)/shard_map/all_to_all | solution.py:508
  56.7 5.0 %collective-permute-start.6 = (f32[32,128]{1,0:T(8,128)S(1)}, f32[32,128]{1,0:T(8,128)S(1)}, u32[]{:S(2)}, u32[]{:S(2)}) collective-permute-start(f32[32,128]{1,0:T(8,128)S(1)} %get-tuple-element.33), channel_id=1, source_target_pairs={{1,2},{2,1},{5,6},{6,5},{9,10},{10,9},{13,14},{14,13},{17,18},{18,... | collective-permute-start | bytes 49160 | tf_op jit(solution)/shard_map/ppermute | solution.py:492
  57.4 6.1 %collective-permute-start.7 = (f32[32,128]{1,0:T(8,128)S(1)}, f32[32,128]{1,0:T(8,128)S(1)}, u32[]{:S(2)}, u32[]{:S(2)}) collective-permute-start(f32[32,128]{1,0:T(8,128)S(1)} %get-tuple-element.34), channel_id=1, source_target_pairs={{0,1},{1,0},{2,3},{3,2},{4,5},{5,4},{6,7},{7,6},{8,9},{9,8},{10,11... | collective-permute-start | bytes 49160 | tf_op jit(solution)/shard_map/ppermute | solution.py:493
